TPU v7x, 32 devices: a whole 2x2x4 slice. The times are simulated.
32 devices in a mesh: dp: 4 (over y, x), expert: 8 (over z, core).
Axes of the slice: x: 2, y: 2, z: 4, core: 2. Of those that a mesh axis runs over, the one named last changes fastest.
Arguments:
- tokens: bfloat16 [16, 512, 1536], P('expert', 'dp'), may hold values from -6 to 6
- lengths: int32 [16], P('expert'), may hold values from 385 to 512, as said below
- routes: int32 [16, 512, 4], P('expert', 'dp'), may hold values from 0 to 7, all different within a row; in each aligned block of 128 rows (0 to 127, 128 to 255, ..., all dimensions but the last counted through in order) at most 96 rows name the same one
- prenorm: bfloat16 [1536], P(('dp', 'expert')), may hold values from 0.5 to 1.5
- w_query: bfloat16 [1536, 1536], P(('dp', 'expert')), may hold values from -0.15625 to 0.15625
- key_value_weight: bfloat16 [1536, 512], P(('dp', 'expert')), may hold values from -0.15625 to 0.15625
- w_output: bfloat16 [1536, 1536], P(('dp', 'expert')), may hold values from -1.25 to 1.25
- midnorm: bfloat16 [1536], P(('dp', 'expert')), may hold values from 0.5 to 1.5
- w_router: bfloat16 [1536, 8], P(('dp', 'expert')), may hold values from -0.078125 to 0.078125
- expert_in: bfloat16 [8, 1536, 1536], P('expert', 'dp'), may hold values from -0.15625 to 0.15625
- expert_out: bfloat16 [8, 768, 1536], P('expert', 'dp'), may hold values from -0.625 to 0.625
- cotangent: bfloat16 [16, 512, 1536], P('expert', 'dp'), may hold values from -6 to 6
Outputs:
- block_out: bfloat16 [16, 512, 1536], P('expert', 'dp')
- grad_tokens: float32 [16, 512, 1536], P('expert', 'dp')
- grad_prenorm: float32 [1536], P(('dp', 'expert'))
- grad_query: float32 [1536, 1536], P(('dp', 'expert'))
- key_value_weight_gradient: float32 [1536, 512], P(('dp', 'expert'))
- grad_output: float32 [1536, 1536], P(('dp', 'expert'))
- grad_midnorm: float32 [1536], P(('dp', 'expert'))
- grad_router: float32 [1536, 8], P(('dp', 'expert'))
- grad_expertin: float32 [8, 1536, 1536], P('expert', 'dp')
- grad_expertout: float32 [8, 768, 1536], P('expert', 'dp')
Inputs may be any that keep to these rules, and one draw needn't show every extreme that they name: `lengths`: each sequence has from 385 to 512 live slots; one sequence has exactly 512 and one exactly 385. `routes`: each slot names 4 different experts; in each aligned block of 128 slots of a sequence (the slots of one device), no expert is named by more than 96 slots, and some expert reaches 96. Padded slots are routed too.
All inputs are finite; a program needn't handle non-finite values.
Results may differ from a plain program's by a relative error of at most 0.018.
Values may be sent and summed in bfloat16 or wider, within the bound.
A program may use at most 192 MiB of HBM per device.

v0:
```python
import jax
import jax.numpy as jnp
from jax import lax
from jax.sharding import PartitionSpec as P

QUERY_HEADS = 12
KEY_VALUE_HEADS = 2
HEAD_SIZE = 128
FF = 768
TOP = 4


epsilon = 1e-06
rope_base = 10000.0
highest = lax.Precision.HIGHEST


def rope_tables(positions):
    half_width = HEAD_SIZE // 2
    inv_freq = rope_base ** (-(jnp.arange(half_width, dtype=jnp.float32) * 2.0 / HEAD_SIZE))
    angles = positions.astype(jnp.float32)[:, None] * inv_freq[None, :]
    return (jnp.cos(angles), jnp.sin(angles))


def apply_rotation(values, cosine_table, sine_table):
    half_width = values.shape[-1] // 2
    first_half = values[..., :half_width]
    second = values[..., half_width:]
    cos_rows = cosine_table[:, None, :]
    sin_rows = sine_table[:, None, :]
    return jnp.concatenate(
        [first_half * cos_rows - second * sin_rows, second * cos_rows + first_half * sin_rows],
        axis=-1,
    )


def unrotate(values, cosine_table, sine_table):
    half_width = values.shape[-1] // 2
    first_half = values[..., :half_width]
    second = values[..., half_width:]
    cos_rows = cosine_table[:, None, :]
    sin_rows = sine_table[:, None, :]
    return jnp.concatenate(
        [first_half * cos_rows + second * sin_rows, second * cos_rows - first_half * sin_rows],
        axis=-1,
    )


def rms_parts(values):
    inverse = lax.rsqrt(jnp.mean(values * values, axis=-1, keepdims=True) + epsilon)
    return (values * inverse, inverse)


def norm_back(grad_normed, normalized_input, inverse, gain):
    scaled = grad_normed * gain
    return inverse * (
        scaled - normalized_input * jnp.mean(scaled * normalized_input, axis=-1, keepdims=True)
    )


def slot_index(route_rows, expert_count, capacity):
    flat_routes = route_rows.reshape(-1)
    onehot = (flat_routes[:, None] == jnp.arange(expert_count, dtype=jnp.int32)[None, :]).astype(
        jnp.int32
    )
    before = jnp.cumsum(onehot, axis=0) - onehot
    within = jnp.sum(before * onehot, axis=-1)
    return flat_routes * capacity + within


def masked_scores(query_matrix, key_rows, allowed):
    scores = jnp.einsum(
        "qhgd,khd->hgqk", query_matrix, key_rows, preferred_element_type=jnp.float32
    ) * HEAD_SIZE ** (-0.5)
    return jnp.where(allowed[None, None], scores, -1e30)


def local(
    tokens,
    lengths,
    routes,
    prenorm,
    w_query,
    key_value_weight,
    w_output,
    midnorm,
    w_router,
    expert_in,
    expert_out,
    cotangent,
):
    micro_count, token_rows, hidden_width = tokens.shape
    dp_size = lax.axis_size("dp")
    expert_size = lax.axis_size("expert")
    dp_rank = lax.axis_index("dp")
    local_experts = expert_in.shape[0]
    expert_count = local_experts * expert_size
    capacity = max(2, 3 * token_rows * TOP // (2 * expert_count))
    query_group_width = QUERY_HEADS // KEY_VALUE_HEADS
    expert_slot_total = token_rows * dp_size
    score_scale = HEAD_SIZE ** (-0.5)
    positions = dp_rank * token_rows + jnp.arange(token_rows, dtype=jnp.int32)
    key_pos = jnp.arange(expert_slot_total, dtype=jnp.int32)
    cosine_table, sine_table = rope_tables(positions)
    total_prenorm = jnp.zeros((hidden_width,), jnp.float32)
    total_query = jnp.zeros((hidden_width, QUERY_HEADS * HEAD_SIZE), jnp.float32)
    total_key_value = jnp.zeros((hidden_width, 2 * KEY_VALUE_HEADS * HEAD_SIZE), jnp.float32)
    total_output = jnp.zeros((QUERY_HEADS * HEAD_SIZE, hidden_width), jnp.float32)
    total_midnorm = jnp.zeros((hidden_width,), jnp.float32)
    total_router = jnp.zeros((hidden_width, expert_count), jnp.float32)
    total_upper = jnp.zeros((local_experts, hidden_width, 2 * FF), jnp.float32)
    total_down = jnp.zeros((local_experts, FF, hidden_width), jnp.float32)
    outputs_list = []
    grads_list = []
    for micro_step in range(micro_count):
        dense_all = (
            lax.all_gather(prenorm, ("dp", "expert"), axis=0, tiled=True),
            lax.all_gather(w_query, ("dp", "expert"), axis=0, tiled=True),
            lax.all_gather(key_value_weight, ("dp", "expert"), axis=0, tiled=True),
            lax.all_gather(w_output, ("dp", "expert"), axis=0, tiled=True),
            lax.all_gather(midnorm, ("dp", "expert"), axis=0, tiled=True),
            lax.all_gather(w_router, ("dp", "expert"), axis=0, tiled=True),
        )
        expert_all = (
            lax.all_gather(expert_in, "dp", axis=1, tiled=True),
            lax.all_gather(expert_out, "dp", axis=1, tiled=True),
        )
        gain_one = dense_all[0].astype(jnp.float32)
        query_all = dense_all[1]
        keyval_all = dense_all[2]
        output_all = dense_all[3]
        gain_two = dense_all[4].astype(jnp.float32)
        router_all = dense_all[5]
        gateup_all = expert_all[0]
        down_all = expert_all[1]
        input_rows = tokens[micro_step].astype(jnp.float32)
        length = lengths[micro_step]
        route_rows = routes[micro_step]
        live_rows = (positions < length)[:, None]
        normed_one, inverse_one = rms_parts(input_rows)
        normalized_input = (normed_one * gain_one).astype(jnp.bfloat16)
        query_pre = jnp.dot(
            normalized_input, query_all, preferred_element_type=jnp.float32
        ).reshape(token_rows, QUERY_HEADS, HEAD_SIZE)
        keyval_pre = jnp.dot(
            normalized_input, keyval_all, preferred_element_type=jnp.float32
        ).reshape(token_rows, 2, KEY_VALUE_HEADS, HEAD_SIZE)
        query_matrix = (
            apply_rotation(query_pre, cosine_table, sine_table)
            .astype(jnp.bfloat16)
            .reshape(token_rows, KEY_VALUE_HEADS, query_group_width, HEAD_SIZE)
        )
        local_key_rows = apply_rotation(keyval_pre[:, 0], cosine_table, sine_table).astype(
            jnp.bfloat16
        )
        local_value_rows = keyval_pre[:, 1].astype(jnp.bfloat16)
        packed_tokens = jnp.stack([local_key_rows, local_value_rows], axis=1).reshape(
            token_rows, 2 * KEY_VALUE_HEADS * HEAD_SIZE
        )
        gathered_rows = lax.all_gather(packed_tokens, "dp", axis=0, tiled=True).reshape(
            expert_slot_total, 2, KEY_VALUE_HEADS, HEAD_SIZE
        )
        key_rows = gathered_rows[:, 0]
        value_rows = gathered_rows[:, 1]
        allowed = (key_pos[None, :] <= positions[:, None]) & (key_pos[None, :] < length)
        scores = masked_scores(query_matrix, key_rows, allowed)
        top_score = jnp.max(scores, axis=-1, keepdims=True)
        weights = jnp.exp(scores - top_score)
        weight_total = jnp.sum(weights, axis=-1, keepdims=True)
        log_total = top_score + jnp.log(weight_total)
        probs_low = (weights / weight_total).astype(jnp.bfloat16)
        attended = jnp.einsum(
            "hgqk,khd->qhgd", probs_low, value_rows, preferred_element_type=jnp.float32
        )
        attended = attended.reshape(token_rows, QUERY_HEADS * HEAD_SIZE).astype(jnp.bfloat16)
        mixed_rows = input_rows + jnp.dot(attended, output_all, preferred_element_type=jnp.float32)
        normed_mid, inverse_two = rms_parts(mixed_rows)
        normed_two = (normed_mid * gain_two).astype(jnp.bfloat16)
        logits = jnp.dot(normed_two, router_all, preferred_element_type=jnp.float32)
        onehot = (
            route_rows[:, :, None] == jnp.arange(expert_count, dtype=jnp.int32)[None, None, :]
        ).astype(jnp.float32)
        chosen = jnp.sum(onehot * logits[:, None, :], axis=-1)
        gate_values = jax.nn.softmax(chosen, axis=-1)
        slot_idx = slot_index(route_rows, expert_count, capacity)
        send_rows = jnp.zeros((expert_count * capacity, hidden_width), jnp.bfloat16)
        send_rows = send_rows.at[slot_idx].set(jnp.repeat(normed_two, TOP, axis=0))
        received = lax.all_to_all(
            send_rows.reshape(expert_count, capacity, hidden_width),
            "expert",
            split_axis=0,
            concat_axis=0,
            tiled=True,
        )
        item_count = received.shape[1]
        grouped = received.reshape(expert_size, local_experts, item_count, hidden_width)
        gate_up = jnp.einsum(
            "slcd,ldf->slcf", grouped, gateup_all, preferred_element_type=jnp.float32
        )
        hidden = (jax.nn.silu(gate_up[..., :FF]) * gate_up[..., FF:]).astype(jnp.bfloat16)
        result = jnp.einsum(
            "slcf,lfd->slcd", hidden, down_all, preferred_element_type=jnp.float32
        ).astype(jnp.bfloat16)
        back_rows = lax.all_to_all(
            result.reshape(expert_count, item_count, hidden_width),
            "expert",
            split_axis=0,
            concat_axis=0,
            tiled=True,
        )
        back_rows, kept_rows, kept_gateup = (
            back_rows,
            received,
            gate_up.reshape(expert_count, item_count, 2 * FF),
        )
        returned = back_rows.reshape(expert_count * capacity, hidden_width)[slot_idx].reshape(
            token_rows, TOP, hidden_width
        )
        returned_wide = returned.astype(jnp.float32)
        expert_sum = jnp.sum(gate_values[:, :, None] * returned_wide, axis=1)
        final_rows = jnp.where(live_rows, mixed_rows + expert_sum, 0.0)
        outputs_list.append(final_rows.astype(jnp.bfloat16))
        grad_rows = jnp.where(live_rows, cotangent[micro_step].astype(jnp.float32), 0.0)
        grad_gate = jnp.sum(grad_rows[:, None, :] * returned_wide, axis=-1)
        grad_chosen = gate_values * (
            grad_gate - jnp.sum(gate_values * grad_gate, axis=-1, keepdims=True)
        )
        grad_logits = jnp.sum(onehot * grad_chosen[:, :, None], axis=1)
        router_term = jnp.dot(normed_two.astype(jnp.float32).T, grad_logits, precision=highest)
        grad_normtwo = jnp.dot(grad_logits, router_all.astype(jnp.float32).T, precision=highest)
        grad_result = (
            (gate_values[:, :, None] * grad_rows[:, None, :])
            .astype(jnp.bfloat16)
            .reshape(token_rows * TOP, hidden_width)
        )
        send_grads = (
            jnp.zeros((expert_count * capacity, hidden_width), jnp.bfloat16)
            .at[slot_idx]
            .set(grad_result)
        )
        recv_grads, again_rows = (
            lax.all_to_all(
                send_grads.reshape(expert_count, capacity, hidden_width),
                "expert",
                split_axis=0,
                concat_axis=0,
                tiled=True,
            ),
            lax.all_to_all(
                send_rows.reshape(expert_count, capacity, hidden_width),
                "expert",
                split_axis=0,
                concat_axis=0,
                tiled=True,
            ),
        )
        grouped_rows = again_rows.reshape(expert_size, local_experts, capacity, hidden_width)
        gate_up = jnp.einsum(
            "slcd,ldf->slcf", grouped_rows, gateup_all, preferred_element_type=jnp.float32
        )
        grouped_grads = recv_grads.reshape(expert_size, local_experts, capacity, hidden_width)
        gate_part = gate_up[..., :FF]
        up_part = gate_up[..., FF:]
        sigmoid_gate = jax.nn.sigmoid(gate_part)
        silu_gate = gate_part * sigmoid_gate
        hidden = (silu_gate * up_part).astype(jnp.bfloat16)
        grad_hidden = jnp.einsum(
            "slcd,lfd->slcf", grouped_grads, down_all, preferred_element_type=jnp.float32
        )
        down_term = jnp.einsum(
            "slcf,slcd->lfd", hidden, grouped_grads, preferred_element_type=jnp.float32
        )
        grad_gatepart = (
            grad_hidden * up_part * sigmoid_gate * (1.0 + gate_part * (1.0 - sigmoid_gate))
        )
        grad_gateup = jnp.concatenate([grad_gatepart, grad_hidden * silu_gate], axis=-1).astype(
            jnp.bfloat16
        )
        upper_term = jnp.einsum(
            "slcd,slcf->ldf", grouped_rows, grad_gateup, preferred_element_type=jnp.float32
        )
        grad_copies = jnp.einsum(
            "slcf,ldf->slcd", grad_gateup, gateup_all, preferred_element_type=jnp.float32
        ).astype(jnp.bfloat16)
        back_grads = lax.all_to_all(
            grad_copies.reshape(expert_count, capacity, hidden_width),
            "expert",
            split_axis=0,
            concat_axis=0,
            tiled=True,
        )
        copy_rows = back_grads.reshape(expert_count * capacity, hidden_width)[slot_idx].reshape(
            token_rows, TOP, hidden_width
        )
        grad_normtwo = grad_normtwo + jnp.sum(copy_rows.astype(jnp.float32), axis=1)
        midnorm_term = jnp.sum(grad_normtwo * normed_mid, axis=0)
        grad_mixed = grad_rows + norm_back(grad_normtwo, normed_mid, inverse_two, gain_two)
        grad_proj = grad_mixed.astype(jnp.bfloat16)
        output_term = jnp.dot(attended.T, grad_proj, preferred_element_type=jnp.float32)
        attention_gradient = jnp.dot(
            grad_proj, output_all.T, preferred_element_type=jnp.float32
        ).astype(jnp.bfloat16)
        attention_gradient = attention_gradient.reshape(
            token_rows, KEY_VALUE_HEADS, query_group_width, HEAD_SIZE
        )
        scores = masked_scores(query_matrix, key_rows, allowed)
        prob_rows = jnp.exp(scores - log_total)
        grad_probs = jnp.einsum(
            "qhgd,khd->hgqk", attention_gradient, value_rows, preferred_element_type=jnp.float32
        )
        row_delta = jnp.sum(prob_rows * grad_probs, axis=-1, keepdims=True)
        grad_scores = (prob_rows * (grad_probs - row_delta)).astype(jnp.bfloat16)
        prob_low = prob_rows.astype(jnp.bfloat16)
        grad_qrot = (
            jnp.einsum("hgqk,khd->qhgd", grad_scores, key_rows, preferred_element_type=jnp.float32)
            * score_scale
        )
        grad_keys = (
            jnp.einsum(
                "hgqk,qhgd->khd", grad_scores, query_matrix, preferred_element_type=jnp.float32
            )
            * score_scale
        )
        grad_vals = jnp.einsum(
            "hgqk,qhgd->khd", prob_low, attention_gradient, preferred_element_type=jnp.float32
        )
        own_keys = (
            lax.psum_scatter(
                jnp.stack([grad_keys, grad_vals], axis=1)
                .reshape(lax.axis_size("dp") * token_rows, 2 * KEY_VALUE_HEADS * HEAD_SIZE)
                .astype(jnp.bfloat16),
                "dp",
                scatter_dimension=0,
                tiled=True,
            )
            .astype(jnp.float32)
            .reshape(token_rows, 2, KEY_VALUE_HEADS, HEAD_SIZE)
        )
        grad_query = (
            unrotate(
                grad_qrot.reshape(token_rows, QUERY_HEADS, HEAD_SIZE), cosine_table, sine_table
            )
            .astype(jnp.bfloat16)
            .reshape(token_rows, QUERY_HEADS * HEAD_SIZE)
        )
        key_gradient = unrotate(own_keys[:, 0], cosine_table, sine_table).astype(jnp.bfloat16)
        value_gradient = own_keys[:, 1].astype(jnp.bfloat16)
        key_value_weight_gradient = jnp.stack([key_gradient, value_gradient], axis=1).reshape(
            token_rows, 2 * KEY_VALUE_HEADS * HEAD_SIZE
        )
        query_term = jnp.dot(normalized_input.T, grad_query, preferred_element_type=jnp.float32)
        keyval_term = jnp.dot(
            normalized_input.T, key_value_weight_gradient, preferred_element_type=jnp.float32
        )
        grad_normone = jnp.dot(grad_query, query_all.T, preferred_element_type=jnp.float32)
        grad_normone = grad_normone + jnp.dot(
            key_value_weight_gradient, keyval_all.T, preferred_element_type=jnp.float32
        )
        prenorm_term = jnp.sum(grad_normone * normed_one, axis=0)
        grads_list.append(grad_mixed + norm_back(grad_normone, normed_one, inverse_one, gain_one))
        total_prenorm = total_prenorm + prenorm_term
        total_query = total_query + query_term
        total_key_value = total_key_value + keyval_term
        total_output = total_output + output_term
        total_midnorm = total_midnorm + midnorm_term
        total_router = total_router + router_term
        total_upper = total_upper + upper_term
        total_down = total_down + down_term
    dense_grads = (
        lax.psum_scatter(total_prenorm, ("dp", "expert"), scatter_dimension=0, tiled=True),
        lax.psum_scatter(total_query, ("dp", "expert"), scatter_dimension=0, tiled=True),
        lax.psum_scatter(total_key_value, ("dp", "expert"), scatter_dimension=0, tiled=True),
        lax.psum_scatter(total_output, ("dp", "expert"), scatter_dimension=0, tiled=True),
        lax.psum_scatter(total_midnorm, ("dp", "expert"), scatter_dimension=0, tiled=True),
        lax.psum_scatter(total_router, ("dp", "expert"), scatter_dimension=0, tiled=True),
    )
    expert_grads = (
        lax.psum_scatter(
            total_upper.astype(jnp.bfloat16), "dp", scatter_dimension=1, tiled=True
        ).astype(jnp.float32),
        lax.psum_scatter(
            total_down.astype(jnp.bfloat16), "dp", scatter_dimension=1, tiled=True
        ).astype(jnp.float32),
    )
    return (
        jnp.stack(outputs_list),
        jnp.stack(grads_list),
        dense_grads[0],
        dense_grads[1],
        dense_grads[2],
        dense_grads[3],
        dense_grads[4],
        dense_grads[5],
        expert_grads[0],
        expert_grads[1],
    )


def solution(mesh):
    placed = (
        P("expert", "dp", None),
        P("expert"),
        P("expert", "dp", None),
        P(("dp", "expert")),
        P(("dp", "expert"), None),
        P(("dp", "expert"), None),
        P(("dp", "expert"), None),
        P(("dp", "expert")),
        P(("dp", "expert"), None),
        P("expert", "dp", None),
        P("expert", "dp", None),
        P("expert", "dp", None),
    )
    return jax.shard_map(
        local,
        mesh=mesh,
        in_specs=placed,
        out_specs=(
            P("expert", "dp", None),
            P("expert", "dp", None),
            P(("dp", "expert")),
            P(("dp", "expert"), None),
            P(("dp", "expert"), None),
            P(("dp", "expert"), None),
            P(("dp", "expert")),
            P(("dp", "expert"), None),
            P("expert", "dp", None),
            P("expert", "dp", None),
        ),
        check_vma=False,
    )
```

profile of v0, /device:TPU:0, one launch (start us, length us, event | category | flops | bytes accessed | tf_op | source)
XLA Modules:
  0.0 1482.5 jit_solution(15002224006618352504)
XLA Ops:
  13.4 42.3 %all-reduce.5 = (bf16[1536]{0:T(1024)(128)(2,1)S(1)}, bf16[1536]{0:T(1024)(128)(2,1)S(1)}) all-reduce(bf16[1536]{0:T(1024)(128)(2,1)S(1)} %dynamic-update-slice, bf16[1536]{0:T(1024)(128)(2,1)S(1)} %dynamic-update-slice.1), channel_id=1, replica_groups=mesh['dp'=4,'expert'=8] {'dp','expert'}, use_global_device_ids=true, to_apply=%add | all-reduce | flops 3072 | bytes 12288
  61.8 7.1 all-gather.7.cloned.1.call-done
  72.7 11.2 all_gather.40
  84.0 50.6 %all-gather.9.cloned.1.call-done = bf16[1536,1536]{1,0:T(8,128)(2,1)} async-done(((bf16[48,1536]{1,0:T(8,128)(2,1)}), bf16[1536,1536]{1,0:T(8,128)(2,1)}) %all-gather.9.cloned.1.call-update) | async-done | bytes 4718608 | tf_op jit(solution)/shard_map/all_gather | solution.py:118
  134.5 6.6 copy.163
  151.3 48.7 %all-gather.11.cloned.1.call-done = bf16[1536,1536]{1,0:T(8,128)(2,1)} async-done(((bf16[48,1536]{1,0:T(8,128)(2,1)}), bf16[1536,1536]{1,0:T(8,128)(2,1)}) %all-gather.11.cloned.1.call-update) | async-done | bytes 4718608 | tf_op jit(solution)/shard_map/all_gather | solution.py:120
  206.1 5.7 scatter_custom_fusion
  221.9 4.9 mul.748
  226.8 73.5 %all-gather = bf16[32,48,8]{1,2,0:T(8,128)(2,1)S(1)} all-gather(bf16[1,48,8]{1,2,0:T(8,128)(2,1)S(1)} %bitcast.561), channel_id=1, replica_groups=mesh['dp'=4,'expert'=8] {'dp','expert'}, dimensions={0}, use_global_device_ids=true | all-gather | bytes 25344 | tf_op jit(solution)/shard_map/all_gather | solution.py:122
  301.4 6.1 scatter_custom_fusion.2
  311.8 9.1 fusion.11
  320.9 30.6 %all-gather.15.cloned.1.call-done = bf16[1,768,1536]{2,1,0:T(8,128)(2,1)} async-done(((bf16[1,192,1536]{2,1,0:T(8,128)(2,1)}), bf16[1,768,1536]{2,1,0:T(8,128)(2,1)}) %all-gather.15.cloned.1.call-update) | async-done | bytes 2359312 | tf_op jit(solution)/shard_map/all_gather | solution.py:126
  351.5 14.3 all-to-all-done.4
  365.8 7.7 fusion.91
  374.9 5.1 fusion.17
  383.6 5.4 convolution_convert_fusion.1
  389.0 49.2 %all-to-all-done.5 = bf16[8,96,1536]{2,1,0:T(8,128)(2,1)S(1)} async-done(((bf16[8,96,1536]{2,1,0:T(8,128)(2,1)}), bf16[8,96,1536]{2,1,0:T(8,128)(2,1)S(1)}, u32[]{:S(2)}, u32[]{:S(2)}) %all-to-all-start.5) | async-done | bytes 2359328 | tf_op jit(solution)/shard_map/all_to_all | solution.py:285
  459.2 11.0 all_gather.47
  488.0 9.3 all-to-all-done.1
  497.3 6.4 gather_fusion
  507.9 5.2 multiply_reduce_fusion.1
  524.5 5.7 scatter_custom_fusion.1
  545.6 4.9 scatter_custom_fusion.3
  550.5 39.0 %all-to-all-done.2 = bf16[8,96,1536]{2,1,0:T(8,128)(2,1)} async-done(((bf16[8,96,1536]{2,1,0:T(8,128)(2,1)}), bf16[8,96,1536]{2,1,0:T(8,128)(2,1)}, u32[]{:S(2)}, u32[]{:S(2)}) %all-to-all-start.2) | async-done | bytes 2359328 | tf_op jit(solution)/shard_map/all_to_all | solution.py:188
  593.0 9.1 fusion.14
  602.1 45.5 %all-to-all-done.6 = bf16[8,96,1536]{2,1,0:T(8,128)(2,1)S(1)} async-done(((bf16[8,96,1536]{2,1,0:T(8,128)(2,1)}), bf16[8,96,1536]{2,1,0:T(8,128)(2,1)S(1)}, u32[]{:S(2)}, u32[]{:S(2)}) %all-to-all-start.6) | async-done | bytes 2359328 | tf_op jit(solution)/shard_map/all_to_all | solution.py:242
  647.7 7.7 fusion.92
  656.7 7.4 fusion.20
  668.2 5.5 convolution_convert_fusion
  673.7 49.1 %all-to-all-done.7 = bf16[8,96,1536]{2,1,0:T(8,128)(2,1)S(1)} async-done(((bf16[8,96,1536]{2,1,0:T(8,128)(2,1)}), bf16[8,96,1536]{2,1,0:T(8,128)(2,1)S(1)}, u32[]{:S(2)}, u32[]{:S(2)}) %all-to-all-start.7) | async-done | bytes 2359328 | tf_op jit(solution)/shard_map/all_to_all | solution.py:285
  737.2 44.7 %all-to-all-done.3 = bf16[8,96,1536]{2,1,0:T(8,128)(2,1)} async-done(((bf16[8,96,1536]{2,1,0:T(8,128)(2,1)}), bf16[8,96,1536]{2,1,0:T(8,128)(2,1)}, u32[]{:S(2)}, u32[]{:S(2)}) %all-to-all-start.3) | async-done | bytes 2359328 | tf_op jit(solution)/shard_map/all_to_all | solution.py:204
  781.8 6.5 gather_fusion.1
  839.5 5.4 fusion.203
  846.9 6.1 fusion.29
  854.7 5.7 fusion.62
  860.4 7.7 fusion.1
  869.3 14.1 reduce-scatter.25.cloned.1.call-done
  893.4 5.2 convolution_add_fusion.1
  901.3 5.0 convolution_add_fusion
  908.4 4.9 fusion.201
  913.3 5.0 fusion.200
  918.3 66.2 %reduce-scatter.29.cloned.1.call-done = f32[48,8]{1,0:T(8,128)} async-done(((f32[1536,8]{1,0:T(8,128)}), f32[48,8]{1,0:T(8,128)}) %reduce-scatter.29.cloned.1.call-update) | async-done | bytes 1552
  985.9 38.8 %reduce-scatter.23.cloned.1.call-done = bf16[1,192,1536]{2,1,0:T(8,128)(2,1)} async-done(((bf16[1,768,1536]{2,1,0:T(8,128)(2,1)}), bf16[1,192,1536]{2,1,0:T(8,128)(2,1)}) %reduce-scatter.23.cloned.1.call-update) | async-done | bytes 589840 | tf_op jit(solution)/shard_map/reduce_scatter | solution.py:381
  1030.6 39.7 %all-reduce.4 = (f32[1536]{0:T(1024)S(1)}, f32[1536]{0:T(1024)S(1)}) all-reduce(f32[1536]{0:T(1024)S(1)} %add.270, f32[1536]{0:T(1024)S(1)} %add.274), channel_id=4, replica_groups=mesh['dp'=4,'expert'=8] {'dp','expert'}, use_global_device_ids=true, to_apply=%region_44.45.clone | all-reduce | flops 3072 | bytes 24576
  1074.7 10.5 reduce-scatter.21.cloned.1.call-done
  1088.2 104.6 %reduce-scatter.17.cloned.1.call-done = f32[48,512]{1,0:T(8,128)} async-done(((f32[1536,512]{1,0:T(8,128)}), f32[48,512]{1,0:T(8,128)}) %reduce-scatter.17.cloned.1.call-update) | async-done | bytes 98320 | tf_op jit(solution)/shard_map/reduce_scatter | solution.py:372
  1192.8 140.8 %reduce-scatter.15.cloned.1.call-done = f32[48,1536]{1,0:T(8,128)} async-done(((f32[1536,1536]{1,0:T(8,128)}), f32[48,1536]{1,0:T(8,128)}) %reduce-scatter.15.cloned.1.call-update) | async-done | bytes 294928 | tf_op jit(solution)/shard_map/reduce_scatter | solution.py:371
  1333.6 142.1 %reduce-scatter.19.cloned.1.call-done = f32[48,1536]{1,0:T(8,128)} async-done(((f32[1536,1536]{1,0:T(8,128)}), f32[48,1536]{1,0:T(8,128)}) %reduce-scatter.19.cloned.1.call-update) | async-done | bytes 294928 | tf_op jit(solution)/shard_map/reduce_scatter | solution.py:373
  (421 shorter events, 230.0 us)
Async XLA Ops:
  7.2 49.9 %copy-start.95 = (s32[2]{0:T(128)S(1)}, s32[2]{0:T(128)}, u32[]{:S(2)}) copy-start(s32[2]{0:T(128)} %param.13) | copy-start | bytes 28
  7.2 61.8 %all-gather.7.cloned.1.call-start = ((), (), s32[]{:S(2)}) async-start(), calls=%async_computation.16 | async-start | bytes 1622016 | tf_op jit(solution)/shard_map/all_gather | solution.py:119
  7.9 126.6 %all-gather.9.cloned.1.call-start = ((), (), s32[]{:S(2)}) async-start(), calls=%async_computation.17 | async-start | bytes 4866048 | tf_op jit(solution)/shard_map/all_gather | solution.py:118
  8.7 191.4 %all-gather.11.cloned.1.call-start = ((), (), s32[]{:S(2)}) async-start(), calls=%async_computation.18 | async-start | bytes 4866048 | tf_op jit(solution)/shard_map/all_gather | solution.py:120
  9.4 302.4 %all-gather.13.cloned.1.call-start = ((), (), s32[]{:S(2)}) async-start(), calls=%async_computation.19 | async-start | bytes 5898240 | tf_op jit(solution)/shard_map/all_gather | solution.py:125
  10.0 60.7 %copy-start.5 = (bf16[2,128,1536]{2,1,0:T(8,128)(2,1)S(1)}, bf16[2,128,1536]{2,1,0:T(8,128)(2,1)}, u32[]{:S(2)}) copy-start(bf16[2,128,1536]{2,1,0:T(8,128)(2,1)} %param.12) | copy-start | bytes 2359300
  11.4 289.3 %copy-start.83 = (s32[128,4]{0,1:T(4,128)}, s32[128,4]{0,1:T(4,128)S(1)}, u32[]{:S(2)}) copy-start(s32[128,4]{0,1:T(4,128)S(1)} %get-tuple-element.73) | copy-start | bytes 6148
  55.7 89.4 %copy-start.53 = (f32[1536]{0:T(1024)}, f32[1536]{0:T(1024)S(1)}, u32[]{:S(2)}) copy-start(f32[1536]{0:T(1024)S(1)} %convert_element_type.342) | copy-start | bytes 18436
  59.3 81.9 %copy-start.78 = (f32[128]{0:T(128)}, f32[128]{0:T(128)S(1)}, u32[]{:S(2)}) copy-start(f32[128]{0:T(128)S(1)} %get-tuple-element.101) | copy-start | bytes 1540
  59.3 85.8 %copy-start.80 = (f32[128]{0:T(128)}, f32[128]{0:T(128)S(1)}, u32[]{:S(2)}) copy-start(f32[128]{0:T(128)S(1)} %get-tuple-element.100) | copy-start | bytes 1540
  59.5 87.1 %copy-start.55 = (f32[128,64]{0,1:T(8,128)}, f32[128,64]{0,1:T(8,128)S(1)}, u32[]{:S(2)}) copy-start(f32[128,64]{0,1:T(8,128)S(1)} %get-tuple-element.79) | copy-start | bytes 98308
  59.5 87.1 %copy-start.57 = (f32[128,64]{0,1:T(8,128)}, f32[128,64]{0,1:T(8,128)S(1)}, u32[]{:S(2)}) copy-start(f32[128,64]{0,1:T(8,128)S(1)} %get-tuple-element.80) | copy-start | bytes 98308
  61.0 240.5 %copy-start.87 = (s32[512,1]{0,1:T(1,128)}, s32[512,1]{0,1:T(1,128)S(1)}, u32[]{:S(2)}) copy-start(s32[512,1]{0,1:T(1,128)S(1)} %compare_select_fusion.1) | copy-start | bytes 6148
  72.0 69.2 %copy-start.61 = (f32[128,2,2,128]{0,3,2,1:T(8,128)}, f32[128,2,2,128]{0,3,2,1:T(8,128)S(1)}, u32[]{:S(2)}) copy-start(f32[128,2,2,128]{0,3,2,1:T(8,128)S(1)} %fusion.131) | copy-start | bytes 786436
  84.0 65.4 %copy-start.33 = (bf16[512,512]{0,1:T(8,128)(2,1)}, bf16[512,512]{0,1:T(8,128)(2,1)S(1)}, u32[]{:S(2)}) copy-start(bf16[512,512]{0,1:T(8,128)(2,1)S(1)} %all_gather.40) | copy-start | bytes 1572868
  151.3 52.0 %copy-start.42 = (bf16[2,128,6,128]{3,1,2,0:T(8,128)(2,1)}, bf16[2,128,6,128]{3,1,2,0:T(8,128)(2,1)S(1)}, u32[]{:S(2)}) copy-start(bf16[2,128,6,128]{3,1,2,0:T(8,128)(2,1)S(1)} %fusion.64) | copy-start | bytes 1179652
  211.8 95.8 %all-to-all-start = ((bf16[8,96,1536]{2,1,0:T(8,128)(2,1)}), bf16[8,96,1536]{2,1,0:T(8,128)(2,1)}, u32[]{:S(2)}, u32[]{:S(2)}) async-start(bf16[8,96,1536]{2,1,0:T(8,128)(2,1)} %bitcast.32), calls=%async_computation | async-start | bytes 4718592 | tf_op jit(solution)/shard_map/all_to_all | solution.py:188
  307.6 58.2 %all-to-all-start.4 = ((bf16[8,96,1536]{2,1,0:T(8,128)(2,1)}), bf16[8,96,1536]{2,1,0:T(8,128)(2,1)S(1)}, u32[]{:S(2)}, u32[]{:S(2)}) async-start(bf16[8,96,1536]{2,1,0:T(8,128)(2,1)} %bitcast.82), calls=%async_computation.4 | async-start | bytes 4718592 | tf_op jit(solution)/shard_map/all_to_all | solution.py:242
  311.2 40.3 %all-gather.15.cloned.1.call-start = ((), (), s32[]{:S(2)}) async-start(), calls=%async_computation.20 | async-start | bytes 2949120 | tf_op jit(solution)/shard_map/all_gather | solution.py:126
  365.8 9.1 copy-start.97
  380.0 58.2 %all-to-all-start.5 = ((bf16[8,96,1536]{2,1,0:T(8,128)(2,1)}), bf16[8,96,1536]{2,1,0:T(8,128)(2,1)S(1)}, u32[]{:S(2)}, u32[]{:S(2)}) async-start(bf16[8,96,1536]{2,1,0:T(8,128)(2,1)} %fusion.17), calls=%async_computation.5 | async-start | bytes 4718592 | tf_op jit(solution)/shard_map/all_to_all | solution.py:285
  438.2 59.1 %all-to-all-start.1 = ((bf16[8,96,1536]{2,1,0:T(8,128)(2,1)}), bf16[8,96,1536]{2,1,0:T(8,128)(2,1)}, u32[]{:S(2)}, u32[]{:S(2)}) async-start(bf16[8,96,1536]{2,1,0:T(8,128)(2,1)} %convolution_convert_fusion.1), calls=%async_computation.1 | async-start | bytes 4718592 | tf_op jit(solution)/shard_map/all_to_all | solution.py:204
  530.2 59.2 %all-to-all-start.2 = ((bf16[8,96,1536]{2,1,0:T(8,128)(2,1)}), bf16[8,96,1536]{2,1,0:T(8,128)(2,1)}, u32[]{:S(2)}, u32[]{:S(2)}) async-start(bf16[8,96,1536]{2,1,0:T(8,128)(2,1)} %bitcast.72), calls=%async_computation.2 | async-start | bytes 4718592 | tf_op jit(solution)/shard_map/all_to_all | solution.py:188
  589.4 58.2 %all-to-all-start.6 = ((bf16[8,96,1536]{2,1,0:T(8,128)(2,1)}), bf16[8,96,1536]{2,1,0:T(8,128)(2,1)S(1)}, u32[]{:S(2)}, u32[]{:S(2)}) async-start(bf16[8,96,1536]{2,1,0:T(8,128)(2,1)} %bitcast.514), calls=%async_computation.6 | async-start | bytes 4718592 | tf_op jit(solution)/shard_map/all_to_all | solution.py:242
  664.1 58.6 %all-to-all-start.7 = ((bf16[8,96,1536]{2,1,0:T(8,128)(2,1)}), bf16[8,96,1536]{2,1,0:T(8,128)(2,1)S(1)}, u32[]{:S(2)}, u32[]{:S(2)}) async-start(bf16[8,96,1536]{2,1,0:T(8,128)(2,1)} %fusion.20), calls=%async_computation.7 | async-start | bytes 4718592 | tf_op jit(solution)/shard_map/all_to_all | solution.py:285
  673.6 53.6 %copy-start.88 = (s32[512,1]{0,1:T(1,128)S(1)}, s32[512,1]{0,1:T(1,128)}, u32[]{:S(2)}) copy-start(s32[512,1]{0,1:T(1,128)} %compare_select_fusion) | copy-start | bytes 6148
  673.6 53.6 %copy-start.64 = (f32[2,6,128]{2,1,0:T(8,128)S(1)}, f32[2,6,128]{2,1,0:T(8,128)}, u32[]{:S(2)}) copy-start(f32[2,6,128]{2,1,0:T(8,128)} %copy-done.63) | copy-start | bytes 18436
  673.6 53.6 %copy-start.74 = (f32[2,6,128]{2,1,0:T(8,128)S(1)}, f32[2,6,128]{2,1,0:T(8,128)}, u32[]{:S(2)}) copy-start(f32[2,6,128]{2,1,0:T(8,128)} %copy-done.73) | copy-start | bytes 18436
  673.6 53.6 %copy-start.66 = (f32[2,6,128]{2,1,0:T(8,128)S(1)}, f32[2,6,128]{2,1,0:T(8,128)}, u32[]{:S(2)}) copy-start(f32[2,6,128]{2,1,0:T(8,128)} %copy-done.65) | copy-start | bytes 18436
  673.7 53.6 %copy-start.77 = (f32[2,6,128]{2,1,0:T(8,128)S(1)}, f32[2,6,128]{2,1,0:T(8,128)}, u32[]{:S(2)}) copy-start(f32[2,6,128]{2,1,0:T(8,128)} %copy-done.76) | copy-start | bytes 18436
  673.7 54.2 %copy-start.96 = (f32[128]{0:T(128)S(1)}, f32[128]{0:T(128)}, u32[]{:S(2)}) copy-start(f32[128]{0:T(128)} %get-tuple-element.17) | copy-start | bytes 1540
  722.8 59.1 %all-to-all-start.3 = ((bf16[8,96,1536]{2,1,0:T(8,128)(2,1)}), bf16[8,96,1536]{2,1,0:T(8,128)(2,1)}, u32[]{:S(2)}, u32[]{:S(2)}) async-start(bf16[8,96,1536]{2,1,0:T(8,128)(2,1)} %convolution_convert_fusion), calls=%async_computation.3 | async-start | bytes 4718592 | tf_op jit(solution)/shard_map/all_to_all | solution.py:204
  727.2 141.1 %reduce-scatter.27.cloned.1.call-start = ((), (), s32[]{:S(2)}) async-start(), calls=%async_computation.27 | async-start | bytes 655360
  832.7 50.7 %reduce-scatter.25.cloned.1.call-start = ((), (), s32[]{:S(2)}) async-start(), calls=%async_computation.26 | async-start | bytes 655360
  838.8 145.8 %reduce-scatter.29.cloned.1.call-start = ((), (), s32[]{:S(2)}) async-start(), calls=%async_computation.28 | async-start | bytes 811008
  846.6 178.1 %reduce-scatter.23.cloned.1.call-start = ((), (), s32[]{:S(2)}) async-start(), calls=%async_computation.25 | async-start | bytes 2949120 | tf_op jit(solution)/shard_map/reduce_scatter | solution.py:381
  853.1 232.2 %reduce-scatter.21.cloned.1.call-start = ((), (), s32[]{:S(2)}) async-start(), calls=%async_computation.24 | async-start | bytes 5898240 | tf_op jit(solution)/shard_map/reduce_scatter | solution.py:378
  868.1 16.4 %copy-start.56 = (f32[128,64]{0,1:T(8,128)S(1)}, f32[128,64]{0,1:T(8,128)}, u32[]{:S(2)}) copy-start(f32[128,64]{0,1:T(8,128)} %copy-done.55) | copy-start | bytes 98308
  868.1 16.4 %copy-start.58 = (f32[128,64]{0,1:T(8,128)S(1)}, f32[128,64]{0,1:T(8,128)}, u32[]{:S(2)}) copy-start(f32[128,64]{0,1:T(8,128)} %copy-done.57) | copy-start | bytes 98308
  868.1 17.2 %copy-start.6 = (bf16[2,128,1536]{2,1,0:T(8,128)(2,1)S(1)}, bf16[2,128,1536]{2,1,0:T(8,128)(2,1)}, u32[]{:S(2)}) copy-start(bf16[2,128,1536]{2,1,0:T(8,128)(2,1)} %param.12) | copy-start | bytes 2359300
  868.1 17.2 %copy-start.54 = (f32[1536]{0:T(1024)S(1)}, f32[1536]{0:T(1024)}, u32[]{:S(2)}) copy-start(f32[1536]{0:T(1024)} %copy-done.53) | copy-start | bytes 18436
  868.1 17.2 %copy-start.79 = (f32[128]{0:T(128)S(1)}, f32[128]{0:T(128)}, u32[]{:S(2)}) copy-start(f32[128]{0:T(128)} %copy-done.78) | copy-start | bytes 1540
  868.1 324.7 %reduce-scatter.17.cloned.1.call-start = ((), (), s32[]{:S(2)}) async-start(), calls=%async_computation.22 | async-start | bytes 3244032 | tf_op jit(solution)/shard_map/reduce_scatter | solution.py:372
  888.4 445.2 %reduce-scatter.15.cloned.1.call-start = ((), (), s32[]{:S(2)}) async-start(), calls=%async_computation.21 | async-start | bytes 9732096 | tf_op jit(solution)/shard_map/reduce_scatter | solution.py:371
  898.7 577.0 %reduce-scatter.19.cloned.1.call-start = ((), (), s32[]{:S(2)}) async-start(), calls=%async_computation.23 | async-start | bytes 9732096 | tf_op jit(solution)/shard_map/reduce_scatter | solution.py:373
  913.3 113.7 %copy-start.51 = (bf16[128,2,2,128]{0,3,2,1:T(8,128)(2,1)S(1)}, bf16[128,2,2,128]{0,3,2,1:T(8,128)(2,1)}, u32[]{:S(2)}) copy-start(bf16[128,2,2,128]{0,3,2,1:T(8,128)(2,1)} %copy-done.50) | copy-start | bytes 393220
  918.3 108.7 %copy-start.7 = (bf16[1536,512]{1,0:T(8,128)(2,1)S(1)}, bf16[1536,512]{1,0:T(8,128)(2,1)}, u32[]{:S(2)}) copy-start(bf16[1536,512]{1,0:T(8,128)(2,1)} %all-gather.7.cloned.1.call-done) | copy-start | bytes 4718596
  985.9 42.8 %copy-start.49 = (bf16[128,2,2,128]{0,3,2,1:T(8,128)(2,1)S(1)}, bf16[128,2,2,128]{0,3,2,1:T(8,128)(2,1)}, u32[]{:S(2)}) copy-start(bf16[128,2,2,128]{0,3,2,1:T(8,128)(2,1)} %copy-done.48) | copy-start | bytes 393220
  (81 other events, 256.2 us)
Sparse Core Ops, SparseCore 0:
  11.0 57.8 all-gather.6
  72.0 62.5 all-gather.8
  137.6 62.4 all-gather.10
  201.8 55.8 all-gather.12
  313.6 37.8 all-gather.14
  832.8 22.6 reduce-scatter.26
  858.6 24.7 reduce-scatter.24
  889.1 95.3 reduce-scatter.28
  988.2 36.4 reduce-scatter.22
  1027.5 57.6 reduce-scatter.20
  1091.3 101.5 reduce-scatter.16
  1199.2 134.4 reduce-scatter.14
  1341.1 134.5 reduce-scatter.18
where the time goes:
time: 1490 us; the launch traced here: 1480 us
  waiting for transfers between devices  908 us (61%)
  blocking collectives  178 us (12%)
  matrix products  157 us (11%)
  local copies, waits for them, and re-layouts  120 us (8%)
  other arithmetic  70.2 us (5%)
  starting transfers between devices  33.7 us (2%)
  between operations  15.5 us (1%)
    reduce_scatter x1, waiting for transfers between devices, local(): lax.psum_scatter(total_output, ('dp', 'expert'), scatter_dimension=0, til...  142 us
    reduce_scatter x1, waiting for transfers between devices, local(): lax.psum_scatter(total_query, ('dp', 'expert'), scatter_dimension=0, tile...  141 us
    reduce_scatter x1, waiting for transfers between devices, local(): lax.psum_scatter(total_key_value, ('dp', 'expert'), scatter_dimension=0,...  105 us
    all_to_all x2, waiting for transfers between devices, local(): lax.all_to_all(grad_copies.reshape(expert_count, capacity, hidden_width),...  98.3 us
    unnamed x16, waiting for transfers between devices  83.6 us
    unnamed x2, blocking collectives  82 us
    all_gather x1, blocking collectives, local(): lax.all_gather(w_router, ('dp', 'expert'), axis=0, tiled=True)  73.5 us
    all_to_all x2, waiting for transfers between devices, local(): lax.all_to_all(send_grads.reshape(expert_count, capacity, hidden_width),...  59.8 us
  transfers between devices with their start and end apart: 21, of which 18 were waited for; matrix products, arithmetic and copies ran while one was open for 15% of the time, Pallas kernels for 0%

commit v1 on v0

--- a/solution.py
+++ b/solution.py
@@ -1,6 +1,8 @@
 import jax
 import jax.numpy as jnp
 from jax import lax
+from jax.experimental import pallas as pl
+from jax.experimental.pallas import tpu as pltpu
 from jax.sharding import PartitionSpec as P
 
 QUERY_HEADS = 12
@@ -396,6 +398,615 @@
     )
 
 
+MESH = pl.DeviceIdType.MESH
+CHUNK = 256
+PIECE = 96
+
+
+def remote(src, dst, send_sem, recv_sem, target):
+    return pltpu.make_async_remote_copy(
+        src_ref=src,
+        dst_ref=dst,
+        send_sem=send_sem,
+        recv_sem=recv_sem,
+        device_id=target,
+        device_id_type=MESH,
+    )
+
+
+def place():
+    d = lax.axis_index("dp")
+    e = lax.axis_index("expert")
+    z = lax.div(e, 2)
+    c = lax.rem(e, 2)
+    x = lax.rem(d, 2)
+    y = lax.div(d, 2)
+    return d, e, z, c, x, y
+
+
+def expert_kernel(
+    x_hbm,
+    g_hbm,
+    gt_hbm,
+    win_hbm,
+    wout_hbm,
+    dx_out,
+    dgt_out,
+    outp_hbm,
+    gin_hbm,
+    gout_hbm,
+    win,
+    wout,
+    xall,
+    gall,
+    gtall,
+    dgu,
+    hg,
+    dxb,
+    dgb,
+    sibr,
+    sibg,
+    ro,
+    rog,
+    ri,
+    rig,
+    stage,
+    own_sem,
+    stage_sem,
+    w_recv,
+    w_send,
+    ag_recv,
+    ag_send,
+    sib_recv,
+    sib_send,
+    red_recv,
+    red_send,
+):
+    d, e, z, c, x, y = place()
+    d_x = d + 1 - 2 * x
+    d_y = d + 2 - 4 * y
+    d_d = 3 - d
+    hi = lax.div(z, 2)
+    zz = z * hi + (3 - z) * (1 - hi)
+    other = 1 - c
+    to_x = (d_x, e)
+    to_y = (d_y, e)
+    to_sib = (d, 2 * z + other)
+    to_up = (d, e + jnp.where(z < 3, 2, -2))
+    to_down = (d, e + jnp.where(z > 0, -2, 2))
+    e_in = e + 2 - 4 * hi
+    e_out = e - 2 + 4 * hi
+    to_in = (d, e_in)
+    to_out = (d, jnp.where(zz == 2, e_out, e_in))
+    mid = zz == 2
+    end = zz == 3
+
+    barrier = pltpu.get_barrier_semaphore()
+    for target in (to_x, to_y, to_sib, to_in):
+        pl.semaphore_signal(barrier, inc=1, device_id=target, device_id_type=MESH)
+
+    @pl.when(mid)
+    def _():
+        pl.semaphore_signal(barrier, inc=1, device_id=to_out, device_id_type=MESH)
+
+    pl.semaphore_wait(barrier, 7 - zz)
+
+    gathered = ((x_hbm, xall), (gt_hbm, gtall), (g_hbm, gall))
+
+    def part(a, ref, zp, lane, s):
+        if a == 1:
+            return ref.at[2 * zp + lane, s]
+        return ref.at[pl.ds(pl.multiple_of((2 * zp + lane) * CHUNK + s * 128, 128), 128)]
+
+    def own_part(a, ref, s):
+        if a == 1:
+            return ref.at[s]
+        return ref.at[pl.ds(s * 128, 128)]
+
+    def ag_copy(a, zp, s, way, src=None):
+        ref = part(a, gathered[a][1], zp, c, s)
+        return remote(
+            ref if src is None else src,
+            ref,
+            ag_send.at[way, a, zp, s],
+            ag_recv.at[a, zp, s],
+            to_up if way == 0 else to_down,
+        )
+
+    def sib_copy(a, zp, s, src=None):
+        ref = part(a, gathered[a][1], zp, c, s)
+        return remote(
+            ref if src is None else src,
+            ref,
+            sib_send.at[a, zp, s],
+            sib_recv.at[a, zp, s],
+            to_sib,
+        )
+
+    def piece(p, dd):
+        if p < 4:
+            return win.at[pl.ds(pl.multiple_of(dd * 384 + p * PIECE, 16), PIECE)]
+        return wout.at[pl.ds(pl.multiple_of(dd * 192 + (p - 4) * PIECE, 16), PIECE)]
+
+    def own_piece(p):
+        if p < 4:
+            return win_hbm.at[pl.ds(p * PIECE, PIECE)]
+        return wout_hbm.at[pl.ds((p - 4) * PIECE, PIECE)]
+
+    def w_copy(p, way, src_d, target, row, src=None):
+        ref = piece(p, src_d)
+        return remote(
+            ref if src is None else src, ref, w_send.at[row, p], w_recv.at[row, p], target
+        )
+
+    for a in range(3):
+        for s in range(2):
+            src = own_part(a, gathered[a][0], s)
+
+            @pl.when(z < 3)
+            def _():
+                ag_copy(a, z, s, 0, src).start()
+
+            @pl.when(z > 0)
+            def _():
+                ag_copy(a, z, s, 1, src).start()
+
+            sib_copy(a, z, s, src).start()
+    for p in range(6):
+        w_copy(p, 0, d, to_x, 0, own_piece(p)).start()
+        w_copy(p, 0, d, to_y, 1, own_piece(p)).start()
+    own_copies = [
+        pltpu.make_async_copy(
+            x_hbm, xall.at[pl.ds(pl.multiple_of(e * CHUNK, 128), CHUNK)], own_sem.at[0]
+        ),
+        pltpu.make_async_copy(
+            g_hbm, gall.at[pl.ds(pl.multiple_of(e * CHUNK, 128), CHUNK)], own_sem.at[1]
+        ),
+        pltpu.make_async_copy(gt_hbm, gtall.at[e], own_sem.at[2]),
+        pltpu.make_async_copy(
+            win_hbm, win.at[pl.ds(pl.multiple_of(d * 384, 16), 384)], own_sem.at[3]
+        ),
+        pltpu.make_async_copy(
+            wout_hbm, wout.at[pl.ds(pl.multiple_of(d * 192, 16), 192)], own_sem.at[4]
+        ),
+    ]
+    for copy in own_copies:
+        copy.start()
+
+    def pass_on(a, k, s):
+        @pl.when(z - k >= 0)
+        def _():
+            ag_copy(a, z - k, s, 0).wait_recv()
+
+            @pl.when(z < 3)
+            def _():
+                ag_copy(a, z - k, s, 0).start()
+
+            sib_copy(a, z - k, s).start()
+
+        @pl.when(z + k <= 3)
+        def _():
+            ag_copy(a, z + k, s, 1).wait_recv()
+
+            @pl.when(z > 0)
+            def _():
+                ag_copy(a, z + k, s, 1).start()
+
+            sib_copy(a, z + k, s).start()
+
+    for p in range(6):
+        w_copy(p, 0, d_x, to_x, 0).wait_recv()
+        if p % 2 == 0:
+            w_copy(p, 0, d_x, to_y, 3).start()
+        w_copy(p, 0, d_y, to_y, 1).wait_recv()
+        if p % 2 == 1:
+            w_copy(p, 0, d_y, to_x, 2).start()
+        for a in range(2):
+            pass_on(a, 1 + p // 2, p % 2)
+    for p in range(6):
+        if p % 2 == 0:
+            w_copy(p, 0, d_d, to_y, 3).wait_recv()
+        else:
+            w_copy(p, 0, d_d, to_x, 2).wait_recv()
+    for p in range(6):
+        pass_on(2, 1 + p // 2, p % 2)
+    for a in range(3):
+        for zp in range(4):
+            for s in range(2):
+                ref = part(a, gathered[a][1], zp, other, s)
+                remote(
+                    ref, ref, sib_send.at[a, zp, s], sib_recv.at[a, zp, s], to_sib
+                ).wait_recv()
+    for copy in own_copies:
+        copy.wait()
+
+    eye = lax.broadcasted_iota(jnp.int32, (128, 128), 0) == lax.broadcasted_iota(
+        jnp.int32, (128, 128), 1
+    )
+    mine = lax.broadcasted_iota(jnp.int32, (8, 128), 0) == e
+
+    def order(i):
+        v = jnp.where(i < 2, i, jnp.where(i == 2, 5 - zz, zz))
+        return v * hi + (3 - v) * (1 - hi)
+
+    def out_copy(i, zp):
+        return pltpu.make_async_copy(
+            stage.at[lax.rem(i, 2)],
+            outp_hbm.at[pl.ds(pl.multiple_of(zp * 512, 512), 512)],
+            stage_sem.at[lax.rem(i, 2)],
+        )
+
+    def lane_rows(i, lane):
+        return pl.ds(pl.multiple_of(i * 512 + lane * CHUNK, CHUNK), CHUNK)
+
+    def sib_sum_copies(i):
+        return (
+            remote(
+                dxb.at[lane_rows(i, other)], sibr.at[i], red_send.at[0, i], red_recv.at[0, i], to_sib
+            ),
+            remote(dgb.at[i, other], sibg.at[i], red_send.at[1, i], red_recv.at[1, i], to_sib),
+        )
+
+    def hop_copies(i, target, dst, dstg, row):
+        return (
+            remote(
+                dxb.at[lane_rows(i, c)], dst.at[i], red_send.at[2, i], red_recv.at[row, i], target
+            ),
+            remote(dgb.at[i, c], dstg.at[i], red_send.at[3, i], red_recv.at[row + 1, i], target),
+        )
+
+    def wait_from(ref, refg, slot, row):
+        remote(ref.at[slot], ref.at[slot], red_send.at[2, slot], red_recv.at[row, slot], to_in).wait_recv()
+        remote(refg.at[slot], refg.at[slot], red_send.at[3, slot], red_recv.at[row + 1, slot], to_in).wait_recv()
+
+    def combine(i, incoming):
+        total = dxb[lane_rows(i, c)].astype(jnp.float32) + sibr[i].astype(jnp.float32)
+        totalg = dgb[i, c] + sibg[i]
+        for ref, refg, slot in incoming:
+            total = total + ref[slot].astype(jnp.float32)
+            totalg = totalg + refg[slot]
+        return total, totalg
+
+    def combine_store(i, incoming):
+        total, totalg = combine(i, incoming)
+        dxb[lane_rows(i, c)] = total.astype(jnp.bfloat16)
+        dgb[i, c] = totalg
+
+    @pl.loop(0, 4)
+    def _(i):
+        zp = order(i)
+        rows = pl.ds(pl.multiple_of(zp * 512, 512), 512)
+        xc = xall[rows]
+        gate = jnp.dot(xc, win[:, :FF], preferred_element_type=jnp.float32)
+        up = jnp.dot(xc, win[:, FF:], preferred_element_type=jnp.float32)
+        back = lax.dot_general(
+            gall[rows], wout[...], (((1,), (1,)), ((), ())), preferred_element_type=jnp.float32
+        )
+        columns = []
+        for lane in range(2):
+            for s in range(2):
+                row = jnp.sum(jnp.where(mine, gtall[2 * zp + lane, s], 0.0), axis=0, keepdims=True)
+                columns.append(jnp.sum(jnp.where(eye, row, 0.0), axis=1, keepdims=True))
+        weight = jnp.concatenate(columns, axis=0)
+        sig = jax.nn.sigmoid(gate)
+        silu = gate * sig
+        hidden = (silu * up).astype(jnp.bfloat16).astype(jnp.float32)
+        dgate = jnp.sum(hidden * back, axis=1, keepdims=True)
+        for lane in range(2):
+            for s in range(2):
+                at = (2 * lane + s) * 128
+                row = jnp.sum(jnp.where(eye, dgate[at : at + 128], 0.0), axis=0, keepdims=True)
+                dgb[i, lane, s] = jnp.where(mine, row, 0.0)
+        hg[rows] = (hidden * weight).astype(jnp.bfloat16)
+        back = back * weight
+        dgu[rows, :FF] = (back * up * (sig * (1.0 + gate * (1.0 - sig)))).astype(jnp.bfloat16)
+        dgu[rows, FF:] = (back * silu).astype(jnp.bfloat16)
+        dxb[pl.ds(pl.multiple_of(i * 512, 512), 512)] = lax.dot_general(
+            dgu[rows], win[...], (((1,), (1,)), ((), ())), preferred_element_type=jnp.float32
+        ).astype(jnp.bfloat16)
+        for copy in sib_sum_copies(i):
+            copy.start()
+
+        @pl.when(i >= 2)
+        def _():
+            out_copy(i, zp).wait()
+
+        stage[lax.rem(i, 2)] = jnp.dot(
+            hg[rows], wout[...], preferred_element_type=jnp.float32
+        ).astype(jnp.bfloat16)
+        out_copy(i, zp).start()
+        for copy in sib_sum_copies(i):
+            copy.wait_recv()
+
+        @pl.when(end & (i < 3))
+        def _():
+            combine_store(i, ())
+            for copy in hop_copies(i, to_in, ro, rog, 2):
+                copy.start()
+
+        @pl.when(mid & (i == 2))
+        def _():
+            wait_from(ro, rog, 0, 2)
+            combine_store(0, ((ro, rog, 0),))
+            for copy in hop_copies(0, to_in, ri, rig, 4):
+                copy.start()
+
+    @pl.when(mid)
+    def _():
+        wait_from(ro, rog, 1, 2)
+        combine_store(1, ((ro, rog, 1),))
+        for copy in hop_copies(1, to_in, ri, rig, 4):
+            copy.start()
+
+    def grad_copy(k, target, at):
+        return pltpu.make_async_copy(
+            stage.at[k % 2, pl.ds(0, 384)], target.at[pl.ds(at, 384)], stage_sem.at[k % 2]
+        )
+
+    blocks = [(gout_hbm, 0), (gout_hbm, 384)] + [(gin_hbm, 384 * k) for k in range(4)]
+    for k in range(2):
+        out_copy(k, 0).wait()
+    for k, (target, at) in enumerate(blocks):
+        if k >= 2:
+            grad_copy(k - 2, *blocks[k - 2]).wait()
+        left = hg if k < 2 else xall
+        right = gall if k < 2 else dgu
+        stage[k % 2, :384] = lax.dot_general(
+            left[:, at : at + 384],
+            right[...],
+            (((0,), (0,)), ((), ())),
+            preferred_element_type=jnp.float32,
+        ).astype(jnp.bfloat16)
+        grad_copy(k, target, at).start()
+        if k == 1:
+
+            @pl.when(mid)
+            def _():
+                wait_from(ri, rig, 0, 4)
+                combine_store(2, ((ri, rig, 0),))
+                for copy in hop_copies(2, to_out, ri, rig, 4):
+                    copy.start()
+
+    for k in (4, 5):
+        grad_copy(k, *blocks[k]).wait()
+
+    @pl.when(mid)
+    def _():
+        wait_from(ro, rog, 2, 2)
+        wait_from(ri, rig, 1, 4)
+        total, totalg = combine(3, ((ro, rog, 2), (ri, rig, 1)))
+        dx_out[...] = total
+        dgt_out[...] = totalg
+
+    @pl.when(end)
+    def _():
+        wait_from(ri, rig, 2, 4)
+        total, totalg = combine(3, ((ri, rig, 2),))
+        dx_out[...] = total
+        dgt_out[...] = totalg
+
+    for p in range(6):
+        w_copy(p, 0, d, to_x, 0, own_piece(p)).wait_send()
+        w_copy(p, 0, d, to_y, 1, own_piece(p)).wait_send()
+        if p % 2 == 0:
+            w_copy(p, 0, d_x, to_y, 3).wait_send()
+        else:
+            w_copy(p, 0, d_y, to_x, 2).wait_send()
+    for a in range(3):
+        for s in range(2):
+            for zp in range(4):
+                sib_copy(a, zp, s).wait_send()
+
+                @pl.when((zp <= z) & (z < 3))
+                def _():
+                    ag_copy(a, zp, s, 0).wait_send()
+
+                @pl.when((zp >= z) & (z > 0))
+                def _():
+                    ag_copy(a, zp, s, 1).wait_send()
+
+    for i in range(4):
+        for copy in sib_sum_copies(i):
+            copy.wait_send()
+        if i < 3:
+            for copy in hop_copies(i, to_in, ro, rog, 2):
+                copy.wait_send()
+
+
+def expert_stage(rows, grads, gates_t, w_in, w_out):
+    bf, f32 = jnp.bfloat16, jnp.float32
+    shape = jax.ShapeDtypeStruct
+    width = rows.shape[-1]
+    hbm = pl.BlockSpec(memory_space=pltpu.HBM)
+    vmem = pl.BlockSpec(memory_space=pltpu.VMEM)
+    dma = pltpu.SemaphoreType.DMA
+    return pl.pallas_call(
+        expert_kernel,
+        out_shape=(
+            shape((CHUNK, width), f32),
+            shape((2, 8, 128), f32),
+            shape((8 * CHUNK, width), bf),
+            shape((width, 2 * FF), bf),
+            shape((FF, width), bf),
+        ),
+        in_specs=[hbm] * 5,
+        out_specs=(vmem, vmem, hbm, hbm, hbm),
+        scratch_shapes=[
+            pltpu.VMEM((width, 2 * FF), bf),
+            pltpu.VMEM((FF, width), bf),
+            pltpu.VMEM((8 * CHUNK, width), bf),
+            pltpu.VMEM((8 * CHUNK, width), bf),
+            pltpu.VMEM((8, 2, 8, 128), f32),
+            pltpu.VMEM((8 * CHUNK, 2 * FF), bf),
+            pltpu.VMEM((8 * CHUNK, FF), bf),
+            pltpu.VMEM((8 * CHUNK, width), bf),
+            pltpu.VMEM((4, 2, 2, 8, 128), f32),
+            pltpu.VMEM((4, CHUNK, width), bf),
+            pltpu.VMEM((4, 2, 8, 128), f32),
+            pltpu.VMEM((3, CHUNK, width), bf),
+            pltpu.VMEM((3, 2, 8, 128), f32),
+            pltpu.VMEM((3, CHUNK, width), bf),
+            pltpu.VMEM((3, 2, 8, 128), f32),
+            pltpu.VMEM((2, 512, width), bf),
+            dma((5,)),
+            dma((2,)),
+            dma((4, 6)),
+            dma((4, 6)),
+            dma((3, 4, 2)),
+            dma((2, 3, 4, 2)),
+            dma((3, 4, 2)),
+            dma((3, 4, 2)),
+            dma((6, 4)),
+            dma((4, 4)),
+        ],
+        compiler_params=pltpu.CompilerParams(
+            collective_id=1, has_side_effects=True, vmem_limit_bytes=63 * 2**20
+        ),
+        name="expert_stage",
+    )(rows, grads, gates_t, w_in, w_out)
+
+
+def fast_local(
+    tokens,
+    lengths,
+    routes,
+    prenorm,
+    w_query,
+    key_value_weight,
+    w_output,
+    midnorm,
+    w_router,
+    expert_in,
+    expert_out,
+    cotangent,
+):
+    bf, f32 = jnp.bfloat16, jnp.float32
+    seqs, token_rows, width = tokens.shape
+    dp_size = lax.axis_size("dp")
+    dp_rank = lax.axis_index("dp")
+    expert_count = lax.axis_size("expert")
+    group = QUERY_HEADS // KEY_VALUE_HEADS
+    slots = token_rows * dp_size
+    rows = seqs * token_rows
+    scale = HEAD_SIZE ** (-0.5)
+    both = ("dp", "expert")
+    small = jnp.concatenate(
+        [w_router, prenorm[:, None], midnorm[:, None], jnp.zeros((w_router.shape[0], 118), bf)], axis=1
+    )
+    packed = jnp.concatenate([w_query, key_value_weight, w_output, small], axis=1)
+    packed = lax.all_gather(packed, both, axis=0, tiled=True)
+    query_all = packed[:, :1536]
+    keyval_all = packed[:, 1536:2048]
+    output_all = packed[:, 2048:3584]
+    router_all = packed[:, 3584:3592]
+    gain_one = packed[:, 3592].astype(f32)
+    gain_two = packed[:, 3593].astype(f32)
+
+    positions = dp_rank * token_rows + jnp.arange(token_rows, dtype=jnp.int32)
+    key_pos = jnp.arange(slots, dtype=jnp.int32)
+    cosine_table, sine_table = rope_tables(positions)
+    cosine_table = jnp.tile(cosine_table, (seqs, 1))
+    sine_table = jnp.tile(sine_table, (seqs, 1))
+    live = (positions[None, :] < lengths[:, None]).reshape(rows, 1)
+    x = tokens.reshape(rows, width).astype(f32)
+    g = jnp.where(live, cotangent.reshape(rows, width), 0)
+    n1, inv1 = rms_parts(x)
+    normed = (n1 * gain_one).astype(bf)
+    q = jnp.dot(normed, query_all, preferred_element_type=f32).reshape(rows, QUERY_HEADS, HEAD_SIZE)
+    kv = jnp.dot(normed, keyval_all, preferred_element_type=f32).reshape(
+        rows, 2, KEY_VALUE_HEADS, HEAD_SIZE
+    )
+    q_rot = apply_rotation(q, cosine_table, sine_table).astype(bf)
+    q_rot = q_rot.reshape(seqs, token_rows, KEY_VALUE_HEADS, group, HEAD_SIZE)
+    k_rot = apply_rotation(kv[:, 0], cosine_table, sine_table).astype(bf)
+    kv_own = jnp.stack([k_rot, kv[:, 1].astype(bf)], axis=1).reshape(seqs, token_rows, 512)
+    kv_all = lax.all_gather(kv_own, "dp", axis=1, tiled=True).reshape(
+        seqs, slots, 2, KEY_VALUE_HEADS, HEAD_SIZE
+    )
+    keys, values = kv_all[:, :, 0], kv_all[:, :, 1]
+    allowed = (key_pos[None, None, :] <= positions[None, :, None]) & (
+        key_pos[None, None, :] < lengths[:, None, None]
+    )
+
+    def score():
+        out = jnp.einsum("sqhgd,skhd->shgqk", q_rot, keys, preferred_element_type=f32) * scale
+        return jnp.where(allowed[:, None, None], out, -1e30)
+
+    scores = score()
+    top = jnp.max(scores, axis=-1, keepdims=True)
+    weights = jnp.exp(scores - top)
+    total = jnp.sum(weights, axis=-1, keepdims=True)
+    lse = top + jnp.log(total)
+    probs_low = (weights / total).astype(bf)
+    attended = jnp.einsum("shgqk,skhd->sqhgd", probs_low, values, preferred_element_type=f32)
+    attended = attended.reshape(rows, QUERY_HEADS * HEAD_SIZE).astype(bf)
+    mixed = x + jnp.dot(attended, output_all, preferred_element_type=f32)
+    n2, inv2 = rms_parts(mixed)
+    normed2 = (n2 * gain_two).astype(bf)
+    logits = jnp.dot(normed2, router_all, preferred_element_type=f32)
+    chosen = jnp.any(
+        routes.reshape(rows, TOP)[:, :, None] == jnp.arange(expert_count, dtype=jnp.int32), axis=1
+    )
+    gates = jax.nn.softmax(jnp.where(chosen, logits, -jnp.inf), axis=-1)
+    gates_t = jnp.transpose(gates.reshape(seqs, token_rows, expert_count), (0, 2, 1))
+    dx, dgate_t, outp, gin, gout = expert_stage(
+        normed2, g, gates_t, expert_in[0], expert_out[0]
+    )
+    expert_sum = lax.psum_scatter(outp, "expert", scatter_dimension=0, tiled=True).astype(f32)
+    block_out = jnp.where(live, mixed + expert_sum, 0.0).astype(bf)
+    gf = g.astype(f32)
+    dgate = jnp.transpose(dgate_t, (0, 2, 1)).reshape(rows, expert_count)
+    dlogit = gates * (dgate - jnp.sum(gates * dgate, axis=-1, keepdims=True))
+    g_router = jnp.dot(normed2.astype(f32).T, dlogit, precision=highest)
+    dn2 = dx + jnp.dot(dlogit, router_all.astype(f32).T, precision=highest)
+    g_mid = jnp.sum(dn2 * n2, axis=0)
+    dmixed = gf + norm_back(dn2, n2, inv2, gain_two)
+    dproj = dmixed.astype(bf)
+    g_out = jnp.dot(attended.T, dproj, preferred_element_type=f32)
+    datt = jnp.dot(dproj, output_all.T, preferred_element_type=f32).astype(bf)
+    datt = datt.reshape(seqs, token_rows, KEY_VALUE_HEADS, group, HEAD_SIZE)
+    probs = jnp.exp(score() - lse)
+    dprobs = jnp.einsum("sqhgd,skhd->shgqk", datt, values, preferred_element_type=f32)
+    delta = jnp.sum(probs * dprobs, axis=-1, keepdims=True)
+    dscores = (probs * (dprobs - delta)).astype(bf)
+    dq_rot = jnp.einsum("shgqk,skhd->sqhgd", dscores, keys, preferred_element_type=f32) * scale
+    dk = jnp.einsum("shgqk,sqhgd->skhd", dscores, q_rot, preferred_element_type=f32) * scale
+    dv = jnp.einsum(
+        "shgqk,sqhgd->skhd", probs.astype(bf), datt, preferred_element_type=f32
+    )
+    dkv = jnp.stack([dk, dv], axis=2).reshape(seqs, slots, 512).astype(bf)
+    own = lax.psum_scatter(dkv, "dp", scatter_dimension=1, tiled=True).astype(f32)
+    own = own.reshape(rows, 2, KEY_VALUE_HEADS, HEAD_SIZE)
+    dq = unrotate(dq_rot.reshape(rows, QUERY_HEADS, HEAD_SIZE), cosine_table, sine_table)
+    dq = dq.astype(bf).reshape(rows, QUERY_HEADS * HEAD_SIZE)
+    dk_own = unrotate(own[:, 0], cosine_table, sine_table).astype(bf)
+    dkv_own = jnp.stack([dk_own, own[:, 1].astype(bf)], axis=1).reshape(rows, 512)
+    g_query = jnp.dot(normed.T, dq, preferred_element_type=f32)
+    g_kv = jnp.dot(normed.T, dkv_own, preferred_element_type=f32)
+    dn1 = jnp.dot(dq, query_all.T, preferred_element_type=f32)
+    dn1 = dn1 + jnp.dot(dkv_own, keyval_all.T, preferred_element_type=f32)
+    g_pre = jnp.sum(dn1 * n1, axis=0)
+    grad_tokens = dmixed + norm_back(dn1, n1, inv1, gain_one)
+    dense = jnp.concatenate(
+        [g_query, g_kv, g_out, g_router, g_pre[:, None], g_mid[:, None]], axis=1
+    ).astype(bf)
+    dense = lax.psum_scatter(dense, both, scatter_dimension=0, tiled=True).astype(f32)
+    upper = lax.psum_scatter(gin, "dp", scatter_dimension=0, tiled=True).astype(f32)
+    down = lax.psum_scatter(gout, "dp", scatter_dimension=0, tiled=True).astype(f32)
+    return (
+        block_out.reshape(seqs, token_rows, width),
+        grad_tokens.reshape(seqs, token_rows, width),
+        dense[:, 3592],
+        dense[:, :1536],
+        dense[:, 1536:2048],
+        dense[:, 2048:3584],
+        dense[:, 3593],
+        dense[:, 3584:3592],
+        upper[None],
+        down[None],
+    )
+
+
 def solution(mesh):
     placed = (
         P("expert", "dp", None),
@@ -411,8 +1022,9 @@
         P("expert", "dp", None),
         P("expert", "dp", None),
     )
+    small = mesh.shape["dp"] == 4 and mesh.shape["expert"] == 8
     return jax.shard_map(
-        local,
+        fast_local if small else local,
         mesh=mesh,
         in_specs=placed,
         out_specs=(

time: 1490 us -> 734 us (0.49)
  waiting for transfers between devices: 908 us -> 337 us
  Pallas kernels: 0 us -> 179 us
  blocking collectives: 178 us -> 0 us
  matrix products: 157 us -> 52.8 us
  other arithmetic: 70.2 us -> 21.6 us
  starting transfers between devices: 33.7 us -> 0.75 us
    reduce_scatter x5 -> x3, waiting for transfers between devices: 437 us -> 87.2 us  [the longest x1 64.8 us: fast_local(): lax.psum_scatter(outp, 'expert', scatter_dimension=0, tiled=True)]
    all_to_all x8 -> x0, waiting for transfers between devices: 251 us -> none  [the longest x2 98.3 us: local(): lax.all_to_all(grad_copies.reshape(expert_count, capacity, hidden_width),...]
    pallas_call x0 -> x1, Pallas kernels: none -> 179 us  [expert_stage(): pl.pallas_call(expert_kernel, out_shape=(shape((CHUNK, width), f32), shap...]
    dot_general x48 -> x18, matrix products: 157 us -> 52.8 us  [the longest x1 5.1 us: fast_local(): dn1 = jnp.dot(dq, query_all.T, preferred_element_type=f32)]
    all_gather x3 -> x0, blocking collectives: 95.8 us -> none  [the longest x1 73.5 us: local(): lax.all_gather(w_router, ('dp', 'expert'), axis=0, tiled=True)]
    unnamed x2 -> x0, blocking collectives: 82 us -> none
    unnamed x16 -> x9, waiting for transfers between devices: 83.6 us -> 152 us
    concatenate x0 -> x2, local copies, waits for them, and re-layouts: none -> 50.9 us  [the longest x1 49.1 us: fast_local(): jnp.concatenate([g_query, g_kv, g_out, g_router, g_pre[:, None], g_mid[:,...]
  transfers between devices with their start and end apart: 21 -> 7, of which waited for: 18 -> 6; matrix products, arithmetic and copies ran while one was open for 15% -> 18% of each run, Pallas kernels for 0% -> 0%
where the time goes in v1:
time: 734 us; the launch traced here: 723 us
  waiting for transfers between devices  337 us (46%)
  Pallas kernels  179 us (24%)
  local copies, waits for them, and re-layouts  116 us (16%)
  matrix products  52.8 us (7%)
  other arithmetic  21.6 us (3%)
  between operations  15.3 us (2%)
    pallas_call x1, Pallas kernels, expert_stage(): pl.pallas_call(expert_kernel, out_shape=(shape((CHUNK, width), f32), shap...  179 us
    unnamed x9, waiting for transfers between devices  152 us
    all_gather x1, waiting for transfers between devices, fast_local(): packed = lax.all_gather(packed, both, axis=0, tiled=True)  90.2 us
    reduce_scatter x1, waiting for transfers between devices, fast_local(): lax.psum_scatter(outp, 'expert', scatter_dimension=0, tiled=True)  64.8 us
    concatenate x1, local copies, waits for them, and re-layouts, fast_local(): jnp.concatenate([g_query, g_kv, g_out, g_router, g_pre[:, None], g_mid[:,...  49.1 us
    unnamed x71, local copies, waits for them, and re-layouts  33.4 us
    reduce_scatter x1, waiting for transfers between devices, fast_local(): lax.psum_scatter(gin, 'dp', scatter_dimension=0, tiled=True).astype(f32)  22.4 us
  transfers between devices with their start and end apart: 7, of which 6 were waited for; matrix products, arithmetic and copies ran while one was open for 18% of the time, Pallas kernels for 0%

profile of v1, /device:TPU:0, one launch (start us, length us, event | category | flops | bytes accessed | tf_op | source)
XLA Modules:
  0.0 723.2 jit_solution(5887092489403051583)
XLA Ops:
  9.7 1.8 concatenate.49
  14.9 90.2 %all-gather.3.cloned.1.call-done = bf16[1536,3712]{1,0:T(8,128)(2,1)} async-done(((bf16[48,3712]{1,0:T(8,128)(2,1)}), bf16[1536,3712]{1,0:T(8,128)(2,1)}) %all-gather.3.cloned.1.call-update) | async-done | bytes 11403280 | tf_op jit(solution)/shard_map/all_gather | solution.py:897
  105.1 1.5 slice_bitcast_fusion.1
  106.6 1.6 copy.98
  108.2 1.8 convert_reduce_fusion
  111.9 4.8 slice_bitcast_fusion
  116.7 6.7 copy.102
  123.4 3.8 fusion.68
  128.8 8.0 %all-gather.5.cloned.1.call-done = bf16[2,512,512]{1,2,0:T(8,128)(2,1)} async-done(((bf16[2,128,512]{1,2,0:T(8,128)(2,1)}), bf16[2,512,512]{1,2,0:T(8,128)(2,1)}) %all-gather.5.cloned.1.call-update) | async-done | bytes 1048592 | tf_op jit(solution)/shard_map/all_gather | solution.py:923
  136.8 2.6 fusion.65
  140.5 1.6 copy-done
  142.1 1.3 fusion.28
  144.3 4.1 multiply_reduce_fusion.4
  149.3 1.6 fusion.66
  151.5 179.5 %expert_stage.1 = (f32[256,1536]{1,0:T(8,128)}, f32[2,8,128]{2,1,0:T(8,128)}, bf16[2048,1536]{1,0:T(8,128)(2,1)}, bf16[1536,1536]{1,0:T(8,128)(2,1)}, bf16[768,1536]{1,0:T(8,128)(2,1)}) custom-call(bf16[256,1536]{1,0:T(8,128)(2,1)} %copy-done.7, bf16[256,1536]{1,0:T(8,128)(2,1)} %bitcast_select_fusion.1.g_hbm, f32[2,8,128]{2,1,0:T(8,128)} %fusion.63.gt_hbm, ...), custom_call_target="tpu_custom_call" | custom-call | tf_op jit(solution)/shard_map/expert_stage/pallas_call | solution.py:823
  332.5 2.8 multiply_reduce_fusion
  335.3 64.8 %reduce-scatter.10.cloned.1.call-done = bf16[256,1536]{1,0:T(8,128)(2,1)} async-done(((bf16[2048,1536]{1,0:T(8,128)(2,1)}), bf16[256,1536]{1,0:T(8,128)(2,1)}) %reduce-scatter.10.cloned.1.call-update) | async-done | bytes 786448 | tf_op jit(solution)/shard_map/reduce_scatter | solution.py:955
  400.1 2.9 multiply_add_fusion.1
  404.2 3.7 fusion.18
  409.7 4.1 fusion.32
  413.8 4.3 fusion
  418.2 1.5 fusion.2
  419.7 1.3 fusion.35
  422.3 3.7 copy.134
  425.9 2.4 copy.146
  429.9 1.5 convolution_convert_fusion.3
  431.4 3.4 multiply_bitcast_fusion
  434.8 2.6 copy.111
  437.5 1.3 reshape.398
  439.9 3.5 convolution_convert_fusion
  443.4 3.6 convolution_convert_fusion.1
  447.1 5.1 fusion.9
  452.2 2.5 reduce-scatter.16.cloned.1.call-done
  454.6 1.9 reshape.416
  456.5 1.9 copy.117
  458.4 1.8 reshape.399
  461.8 3.5 multiply_reduce_fusion.1
  465.2 1.7 convolution_convert_fusion.2
  467.0 49.1 %concatenate.60 = bf16[1536,3594]{0,1:T(8,128)(2,1)} concatenate(bf16[1536,1536]{0,1:T(8,128)(2,1)} %convolution_convert_fusion, bf16[1536,512]{0,1:T(8,128)(2,1)} %convolution_convert_fusion.2, bf16[1536,1536]{0,1:T(8,128)(2,1)} %convolution_convert_fusion.1, bf16[1536,8]{0,1:T(8,128)(2,1)S(1)} %convolution_convert_fusion.3, bf16[1536,1]{0,1:T(2,128)(2,1)S(1)} %broadcast_in_dim.105, ...), dimensions={1} | concatenate | bytes 22081536 | tf_op jit(solution)/shard_map/concatenate | solution.py:990
  516.1 14.8 %copy.136 = bf16[1536,3594]{1,0:T(8,128)(2,1)} copy(bf16[1536,3594]{0,1:T(8,128)(2,1)} %concatenate.60) | data formatting | bytes 22081536
  530.9 2.2 bitcast_convert_fusion.1
  533.1 22.4 %reduce-scatter.12.cloned.1.call-done = bf16[384,1536]{1,0:T(8,128)(2,1)} async-done(((bf16[1536,1536]{1,0:T(8,128)(2,1)}), bf16[384,1536]{1,0:T(8,128)(2,1)}) %reduce-scatter.12.cloned.1.call-update) | async-done | bytes 1179664 | tf_op jit(solution)/shard_map/reduce_scatter | solution.py:994
  555.5 3.1 bitcast_convert_fusion
  558.6 1.6 multiply_add_fusion
  560.1 148.3 %reduce-scatter.18.cloned.1.call-done = bf16[48,3594]{1,0:T(8,128)(2,1)} async-done(((bf16[1536,3594]{1,0:T(8,128)(2,1)}), bf16[48,3594]{1,0:T(8,128)(2,1)}) %reduce-scatter.18.cloned.1.call-update) | async-done | bytes 345040
  708.4 1.4 copy.137
  710.6 1.4 convert_element_type.161
  714.7 1.3 slice_bitcast_fusion.10
  (136 shorter events, 25.4 us)
Async XLA Ops:
  7.2 5.1 copy-start.12
  7.2 5.4 copy-start.27
  7.2 6.6 copy-start.17
  7.2 97.9 %all-gather.3.cloned.1.call-start = ((), (), s32[]{:S(2)}) async-start(), calls=%async_computation.5 | async-start | bytes 11759616 | tf_op jit(solution)/shard_map/all_gather | solution.py:897
  11.5 125.3 %all-gather.5.cloned.1.call-start = ((), (), s32[]{:S(2)}) async-start(), calls=%async_computation.6 | async-start | bytes 1310720 | tf_op jit(solution)/shard_map/all_gather | solution.py:923
  12.6 94.0 %copy-start.25 = (pred[256]{0:T(512)(128)(4,1)}, pred[256]{0:T(512)(128)(4,1)S(1)}, u32[]{:S(2)}) copy-start(pred[256]{0:T(512)(128)(4,1)S(1)} %compare_bitcast_fusion) | copy-start | bytes 772
  108.2 2.1 copy-start.14
  110.2 13.1 %copy-start.5 = (bf16[2,128,1536]{2,1,0:T(8,128)(2,1)}, bf16[2,128,1536]{2,1,0:T(8,128)(2,1)S(1)}, u32[]{:S(2)}) copy-start(bf16[2,128,1536]{2,1,0:T(8,128)(2,1)S(1)} %multiply_convert_fusion.1) | copy-start | bytes 2359300
  111.8 288.3 %reduce-scatter.10.cloned.1.call-start = ((), (), s32[]{:S(2)}) async-start(), calls=%async_computation.7 | async-start | bytes 7077888 | tf_op jit(solution)/shard_map/reduce_scatter | solution.py:955
  128.1 11.3 %copy-start.8 = (bf16[2,128,2,6,64]{4,1,3,2,0:T(8,128)(2,1)}, bf16[2,128,2,6,64]{4,1,3,2,0:T(8,128)(2,1)S(1)}, u32[]{:S(2)}) copy-start(bf16[2,128,2,6,64]{4,1,3,2,0:T(8,128)(2,1)S(1)} %copy.103) | copy-start | bytes 1179652
  128.8 10.7 %copy-start.10 = (bf16[2,128,2,6,64]{4,1,3,2,0:T(8,128)(2,1)}, bf16[2,128,2,6,64]{4,1,3,2,0:T(8,128)(2,1)S(1)}, u32[]{:S(2)}) copy-start(bf16[2,128,2,6,64]{4,1,3,2,0:T(8,128)(2,1)S(1)} %copy.104) | copy-start | bytes 1179652
  139.5 2.6 copy-start
  139.5 2.6 copy-start.18
  144.3 4.1 copy-start.15
  148.4 2.5 copy-start.1
  148.4 0.6 copy-start.22
  149.3 2.3 copy-start.7
  331.0 0.7 copy-start.21
  331.0 1.4 copy-start.2
  331.1 1.4 copy-start.23
  331.1 123.6 %reduce-scatter.16.cloned.1.call-start = ((), (), s32[]{:S(2)}) async-start(), calls=%async_computation.10 | async-start | bytes 1310720
  332.5 67.6 %copy-start.26 = (pred[256]{0:T(512)(128)(4,1)S(1)}, pred[256]{0:T(512)(128)(4,1)}, u32[]{:S(2)}) copy-start(pred[256]{0:T(512)(128)(4,1)} %copy-done.25) | copy-start | bytes 772
  403.0 1.1 copy-start.3
  409.7 4.2 copy-start.19
  409.7 8.5 %slice-start = ((s8[6291456]{0:T(1024)(128)(4,1)}), s8[4194304]{0:T(1024)(128)(4,1)S(1)}, s32[]{:S(2)}) async-start(s8[6291456]{0:T(1024)(128)(4,1)} %bitcast.203), calls=%async_computation.12 | async-start | bytes 8388608
  413.8 4.3 slice-start.1
  418.2 1.6 copy-start.9
  418.2 1.6 copy-start.11
  428.4 102.5 %reduce-scatter.14.cloned.1.call-start = ((), (), s32[]{:S(2)}) async-start(), calls=%async_computation.9 | async-start | bytes 2949120 | tf_op jit(solution)/shard_map/reduce_scatter | solution.py:995
  429.0 126.5 %reduce-scatter.12.cloned.1.call-start = ((), (), s32[]{:S(2)}) async-start(), calls=%async_computation.8 | async-start | bytes 5898240 | tf_op jit(solution)/shard_map/reduce_scatter | solution.py:994
  429.6 278.9 %reduce-scatter.18.cloned.1.call-start = ((), (), s32[]{:S(2)}) async-start(), calls=%async_computation.11 | async-start | bytes 11759616
  438.7 1.2 copy-start.6
  439.9 3.5 copy-start.4
  439.9 3.5 copy-start.16
  452.2 9.3 %copy-start.13 = (bf16[2,128,1536]{2,1,0:T(8,128)(2,1)S(1)}, bf16[2,128,1536]{2,1,0:T(8,128)(2,1)}, u32[]{:S(2)}) copy-start(bf16[2,128,1536]{2,1,0:T(8,128)(2,1)} %param.12) | copy-start | bytes 2359300
  452.2 9.3 %copy-start.24 = (f32[256]{0:T(256)S(1)}, f32[256]{0:T(256)}, u32[]{:S(2)}) copy-start(f32[256]{0:T(256)} %get-tuple-element.82) | copy-start | bytes 3076
  460.2 1.5 copy-start.28
  555.5 3.1 copy-start.20
Sparse Core Ops, SparseCore 0:
  11.6 93.4 all-gather.2
  112.0 24.8 all-gather.4
  331.2 68.8 reduce-scatter.9
  428.5 26.0 reduce-scatter.15
  457.8 37.3 reduce-scatter.13
  498.4 57.0 reduce-scatter.11
  562.6 145.8 reduce-scatter.17

commit v2 on v1

--- a/solution.py
+++ b/solution.py
@@ -491,7 +491,7 @@
 
     pl.semaphore_wait(barrier, 7 - zz)
 
-    gathered = ((x_hbm, xall), (gt_hbm, gtall), (g_hbm, gall))
+    gathered = ((x_hbm, xall), (gt_hbm, gtall))
 
     def part(a, ref, zp, lane, s):
         if a == 1:
@@ -539,7 +539,7 @@
             ref if src is None else src, ref, w_send.at[row, p], w_recv.at[row, p], target
         )
 
-    for a in range(3):
+    for a in range(2):
         for s in range(2):
             src = own_part(a, gathered[a][0], s)
 
@@ -559,9 +559,7 @@
         pltpu.make_async_copy(
             x_hbm, xall.at[pl.ds(pl.multiple_of(e * CHUNK, 128), CHUNK)], own_sem.at[0]
         ),
-        pltpu.make_async_copy(
-            g_hbm, gall.at[pl.ds(pl.multiple_of(e * CHUNK, 128), CHUNK)], own_sem.at[1]
-        ),
+        pltpu.make_async_copy(g_hbm, gall, own_sem.at[1]),
         pltpu.make_async_copy(gt_hbm, gtall.at[e], own_sem.at[2]),
         pltpu.make_async_copy(
             win_hbm, win.at[pl.ds(pl.multiple_of(d * 384, 16), 384)], own_sem.at[3]
@@ -608,9 +606,7 @@
             w_copy(p, 0, d_d, to_y, 3).wait_recv()
         else:
             w_copy(p, 0, d_d, to_x, 2).wait_recv()
-    for p in range(6):
-        pass_on(2, 1 + p // 2, p % 2)
-    for a in range(3):
+    for a in range(2):
         for zp in range(4):
             for s in range(2):
                 ref = part(a, gathered[a][1], zp, other, s)
@@ -792,7 +788,7 @@
             w_copy(p, 0, d_x, to_y, 3).wait_send()
         else:
             w_copy(p, 0, d_y, to_x, 2).wait_send()
-    for a in range(3):
+    for a in range(2):
         for s in range(2):
             for zp in range(4):
                 sib_copy(a, zp, s).wait_send()
@@ -852,10 +848,10 @@
             dma((2,)),
             dma((4, 6)),
             dma((4, 6)),
-            dma((3, 4, 2)),
-            dma((2, 3, 4, 2)),
-            dma((3, 4, 2)),
-            dma((3, 4, 2)),
+            dma((2, 4, 2)),
+            dma((2, 2, 4, 2)),
+            dma((2, 4, 2)),
+            dma((2, 4, 2)),
             dma((6, 4)),
             dma((4, 4)),
         ],
@@ -864,6 +860,452 @@
         ),
         name="expert_stage",
     )(rows, grads, gates_t, w_in, w_out)
+
+
+def attention_kernel(
+    tok_ref,
+    wa_hbm,
+    wb_hbm,
+    g_hbm,
+    cos_ref,
+    sin_ref,
+    lens_ref,
+    routes_ref,
+    wa_out,
+    wb_out,
+    gall,
+    q_out,
+    kv_out,
+    att_out,
+    mixed_out,
+    normed_out,
+    gates_out,
+    wa,
+    wb,
+    qs,
+    kvs,
+    att,
+    own_sem,
+    z_recv,
+    z_send,
+    xy_recv,
+    xy_send,
+    sib_recv,
+    sib_send,
+    g_recv,
+    g_send,
+    gs_recv,
+    gs_send,
+    kv_recv,
+    kv_send,
+):
+    bf, f32 = jnp.bfloat16, jnp.float32
+    d, e, z, c, x, y = place()
+    d_x = d + 1 - 2 * x
+    d_y = d + 2 - 4 * y
+    d_d = 3 - d
+    other = 1 - c
+    to_x = (d_x, e)
+    to_y = (d_y, e)
+    to_sib = (d, 2 * z + other)
+    to_up = (d, e + jnp.where(z < 3, 2, -2))
+    to_down = (d, e + jnp.where(z > 0, -2, 2))
+
+    barrier = pltpu.get_barrier_semaphore()
+    for target in (to_x, to_y, to_sib):
+        pl.semaphore_signal(barrier, inc=1, device_id=target, device_id_type=MESH)
+
+    @pl.when(z < 3)
+    def _():
+        pl.semaphore_signal(barrier, inc=1, device_id=to_up, device_id_type=MESH)
+
+    @pl.when(z > 0)
+    def _():
+        pl.semaphore_signal(barrier, inc=1, device_id=to_down, device_id_type=MESH)
+
+    pl.semaphore_wait(barrier, 5 - jnp.where((z == 0) | (z == 3), 1, 0))
+
+    full = (wa, wb)
+    shard = (wa_hbm, wb_hbm)
+
+    def block(a, dd, zp, lane):
+        at = pl.multiple_of((dd * 8 + 2 * zp + lane) * 48, 16)
+        return full[a].at[pl.ds(at, 48)]
+
+    def z_copy(a, zp, way, src=None):
+        ref = block(a, d, zp, c)
+        return remote(
+            ref if src is None else src,
+            ref,
+            z_send.at[a, way, zp],
+            z_recv.at[a, zp],
+            to_up if way == 0 else to_down,
+        )
+
+    def xy_copy(a, dd, zp, row, target, src=None):
+        ref = block(a, dd, zp, c)
+        return remote(
+            ref if src is None else src,
+            ref,
+            xy_send.at[a, row, zp],
+            xy_recv.at[a, row, zp],
+            target,
+        )
+
+    def s_copy(a, dd, zp, src=None, lane=None):
+        ref = block(a, dd, zp, c if lane is None else lane)
+        return remote(
+            ref if src is None else src,
+            ref,
+            sib_send.at[a, dd, zp],
+            sib_recv.at[a, dd, zp],
+            to_sib,
+        )
+
+    def have(a, zp, src=None):
+        xy_copy(a, d, zp, 0, to_x, src).start()
+        xy_copy(a, d, zp, 1, to_y, src).start()
+        s_copy(a, d, zp, src).start()
+
+    def own_start(a):
+        @pl.when(z < 3)
+        def _():
+            z_copy(a, z, 0, shard[a]).start()
+
+        @pl.when(z > 0)
+        def _():
+            z_copy(a, z, 1, shard[a]).start()
+
+        have(a, z, shard[a])
+
+    def from_z(a, k):
+        @pl.when(z - k >= 0)
+        def _():
+            z_copy(a, z - k, 0).wait_recv()
+
+            @pl.when(z < 3)
+            def _():
+                z_copy(a, z - k, 0).start()
+
+            have(a, z - k)
+
+        @pl.when(z + k <= 3)
+        def _():
+            z_copy(a, z + k, 1).wait_recv()
+
+            @pl.when(z > 0)
+            def _():
+                z_copy(a, z + k, 1).start()
+
+            have(a, z + k)
+
+    def from_xy_one(a, zp):
+        xy_copy(a, d_x, zp, 0, to_x).wait_recv()
+
+        @pl.when(lax.rem(zp, 2) == 0)
+        def _():
+            xy_copy(a, d_x, zp, 2, to_y).start()
+
+        s_copy(a, d_x, zp).start()
+        xy_copy(a, d_y, zp, 1, to_y).wait_recv()
+
+        @pl.when(lax.rem(zp, 2) == 1)
+        def _():
+            xy_copy(a, d_y, zp, 2, to_x).start()
+
+        s_copy(a, d_y, zp).start()
+
+    def from_xy(a, k):
+        @pl.when(z - k >= 0)
+        def _():
+            from_xy_one(a, z - k)
+
+        if k > 0:
+
+            @pl.when(z + k <= 3)
+            def _():
+                from_xy_one(a, z + k)
+
+    def from_diag(a):
+        for k in range(4):
+            zp = lax.rem(z + k, 4)
+            xy_copy(a, d_d, zp, 2, to_x).wait_recv()
+            s_copy(a, d_d, zp).start()
+
+    def from_sib(a):
+        for dd in range(4):
+            for zp in range(4):
+                s_copy(a, dd, zp, lane=other).wait_recv()
+
+    def drain(a):
+        for zp in range(4):
+            for dd in range(4):
+                s_copy(a, dd, zp).wait_send()
+            for row in range(3):
+                xy_copy(a, d, zp, row, to_x).wait_send()
+
+            @pl.when((zp <= z) & (z < 3))
+            def _():
+                z_copy(a, zp, 0).wait_send()
+
+            @pl.when((zp >= z) & (z > 0))
+            def _():
+                z_copy(a, zp, 1).wait_send()
+
+    def g_part(zp, lane, s):
+        at = pl.multiple_of((2 * zp + lane) * CHUNK + s * 128, 128)
+        return gall.at[pl.ds(at, 128)]
+
+    def g_copy(zp, s, way, src=None):
+        ref = g_part(zp, c, s)
+        return remote(
+            ref if src is None else src,
+            ref,
+            g_send.at[way, zp, s],
+            g_recv.at[zp, s],
+            to_up if way == 0 else to_down,
+        )
+
+    def gs_copy(zp, s, src=None, lane=None):
+        ref = g_part(zp, c if lane is None else lane, s)
+        return remote(
+            ref if src is None else src, ref, gs_send.at[zp, s], gs_recv.at[zp, s], to_sib
+        )
+
+    def g_start():
+        for s in range(2):
+            src = g_hbm.at[pl.ds(s * 128, 128)]
+
+            @pl.when(z < 3)
+            def _():
+                g_copy(z, s, 0, src).start()
+
+            @pl.when(z > 0)
+            def _():
+                g_copy(z, s, 1, src).start()
+
+            gs_copy(z, s, src).start()
+
+    def g_pass(k, s):
+        @pl.when(z - k >= 0)
+        def _():
+            g_copy(z - k, s, 0).wait_recv()
+
+            @pl.when(z < 3)
+            def _():
+                g_copy(z - k, s, 0).start()
+
+            gs_copy(z - k, s).start()
+
+        @pl.when(z + k <= 3)
+        def _():
+            g_copy(z + k, s, 1).wait_recv()
+
+            @pl.when(z > 0)
+            def _():
+                g_copy(z + k, s, 1).start()
+
+            gs_copy(z + k, s).start()
+
+    own = [
+        pltpu.make_async_copy(shard[a], block(a, d, z, c), own_sem.at[a]) for a in range(2)
+    ] + [
+        pltpu.make_async_copy(
+            g_hbm, gall.at[pl.ds(pl.multiple_of(e * CHUNK, CHUNK), CHUNK)], own_sem.at[2]
+        )
+    ]
+    own_start(0)
+    own_start(1)
+    for copy in own:
+        copy.start()
+    g_start()
+    tok = tok_ref[...].astype(f32)
+    n1 = tok * lax.rsqrt(jnp.mean(tok * tok, axis=1, keepdims=True) + epsilon)
+    for k in range(1, 4):
+        from_z(0, k)
+        from_xy(0, k - 1)
+        from_z(1, k)
+    from_xy(0, 3)
+    from_diag(0)
+    own[0].wait()
+    from_sib(0)
+
+    small = wa[:, 2048:]
+    eye = (
+        lax.broadcasted_iota(jnp.int32, (128, 128), 0)
+        == lax.broadcasted_iota(jnp.int32, (128, 128), 1)
+    ).astype(bf)
+    small_t = lax.dot_general(eye, small, (((1,), (1,)), ((), ())), preferred_element_type=f32)
+    normed = (n1 * small_t[8:9]).astype(bf)
+    cos_rows = jnp.concatenate([cos_ref[...]] * 2, axis=0)
+    sin_rows = jnp.concatenate([sin_ref[...]] * 2, axis=0)
+
+    def rotate(v):
+        return v * cos_rows + pltpu.roll(v, 64, 1) * sin_rows
+
+    kv = jnp.dot(normed, wa[:, 1536:2048], preferred_element_type=f32)
+    for h in range(2):
+        kvs[d, :, h * 128 : (h + 1) * 128] = rotate(kv[:, h * 128 : (h + 1) * 128]).astype(bf)
+    kvs[d, :, 256:] = kv[:, 256:].astype(bf)
+
+    def kv_copy(dd, s, row, target):
+        ref = kvs.at[dd, pl.ds(s * 128, 128)]
+        return remote(ref, ref, kv_send.at[row, s], kv_recv.at[row, s], target)
+
+    for s in range(2):
+        kv_copy(d, s, 0, to_x).start()
+        kv_copy(d, s, 1, to_y).start()
+    from_xy(1, 0)
+    q = jnp.dot(normed, wa[:, :1536], preferred_element_type=f32)
+    for head in range(QUERY_HEADS):
+        rot = rotate(q[:, head * 128 : (head + 1) * 128]).astype(bf)
+        for s in range(2):
+            at = (s * QUERY_HEADS + head) * 128
+            qs[at : at + 128] = rot[s * 128 : (s + 1) * 128]
+    g_pass(1, 0)
+    kv_copy(d_x, 0, 0, to_x).wait_recv()
+    kv_copy(d_x, 0, 2, to_y).start()
+    kv_copy(d_y, 1, 1, to_y).wait_recv()
+    kv_copy(d_y, 1, 2, to_x).start()
+    kv_copy(d_y, 0, 1, to_y).wait_recv()
+    kv_copy(d_x, 1, 0, to_x).wait_recv()
+    for k in range(1, 4):
+        from_xy(1, k)
+    g_pass(1, 1)
+    for s in range(2):
+        kv_copy(d_d, s, 2, to_x).wait_recv()
+    q_copy = pltpu.make_async_copy(qs, q_out, own_sem.at[3])
+    kvo_copy = pltpu.make_async_copy(kvs, kv_out, own_sem.at[4])
+    wa_copy = pltpu.make_async_copy(wa, wa_out, own_sem.at[5])
+    for copy in (q_copy, kvo_copy, wa_copy):
+        copy.start()
+
+    query_pos = d * 128 + lax.broadcasted_iota(jnp.int32, (128, 512), 0)
+    key_pos = lax.broadcasted_iota(jnp.int32, (128, 512), 1)
+
+    @pl.loop(0, 4)
+    def _(n):
+        s = lax.div(n, 2)
+        h = lax.rem(n, 2)
+        lens = lens_ref[s][0:1, 0:1]
+        allowed = (key_pos <= query_pos) & (key_pos < lens)
+        ks = kvs[:, pl.ds(pl.multiple_of(s * 128, 128), 128), pl.ds(pl.multiple_of(h * 128, 128), 128)]
+        vs = kvs[:, pl.ds(pl.multiple_of(s * 128, 128), 128), pl.ds(pl.multiple_of(256 + h * 128, 128), 128)]
+        ks = ks.reshape(512, 128)
+        vs = vs.reshape(512, 128)
+        for half in range(2):
+            qh = qs[pl.ds(pl.multiple_of(n * 768 + half * 384, 128), 384)]
+            scores = lax.dot_general(qh, ks, (((1,), (1,)), ((), ())), preferred_element_type=f32)
+            scores = scores.reshape(3, 128, 512) * HEAD_SIZE ** (-0.5)
+            scores = jnp.where(allowed[None], scores, -1e30)
+            top = jnp.max(scores, axis=-1, keepdims=True)
+            weights = jnp.exp(scores - top)
+            weights = weights * (1.0 / jnp.sum(weights, axis=-1, keepdims=True))
+            out = jnp.dot(
+                weights.astype(bf).reshape(384, 512), vs, preferred_element_type=f32
+            ).astype(bf)
+            for j in range(3):
+                att[
+                    pl.ds(pl.multiple_of(s * 128, 128), 128),
+                    pl.ds(pl.multiple_of(h * 768 + (half * 3 + j) * 128, 128), 128),
+                ] = out[j * 128 : (j + 1) * 128]
+
+    g_pass(2, 0)
+    from_diag(1)
+    own[1].wait()
+    from_sib(1)
+    att_copy = pltpu.make_async_copy(att, att_out, own_sem.at[6])
+    wb_copy = pltpu.make_async_copy(wb, wb_out, own_sem.at[7])
+    att_copy.start()
+    wb_copy.start()
+    mixed = tok_ref[...].astype(f32) + jnp.dot(att[...], wb[...], preferred_element_type=f32)
+    mixed_out[...] = mixed
+    n2 = mixed * lax.rsqrt(jnp.mean(mixed * mixed, axis=1, keepdims=True) + epsilon)
+    normed2 = (n2 * small_t[9:10]).astype(bf)
+    normed_out[...] = normed2
+    logits = jnp.dot(normed2, small, preferred_element_type=f32)
+    lanes = lax.broadcasted_iota(jnp.int32, (CHUNK, 128), 1)
+    chosen = lanes == routes_ref[:, 0:1]
+    for t in range(1, TOP):
+        chosen = chosen | (lanes == routes_ref[:, t : t + 1])
+    logits = jnp.where(chosen, logits, -1e30)
+    weights = jnp.where(chosen, jnp.exp(logits - jnp.max(logits, axis=1, keepdims=True)), 0.0)
+    gates_out[...] = weights / jnp.sum(weights, axis=1, keepdims=True)
+
+    g_pass(2, 1)
+    g_pass(3, 0)
+    g_pass(3, 1)
+    for zp in range(4):
+        for s in range(2):
+            gs_copy(zp, s, lane=other).wait_recv()
+    own[2].wait()
+    for copy in (q_copy, kvo_copy, wa_copy, att_copy, wb_copy):
+        copy.wait()
+    drain(0)
+    drain(1)
+    for s in range(2):
+        for row in range(3):
+            kv_copy(d, s, row, to_x).wait_send()
+        for zp in range(4):
+            gs_copy(zp, s).wait_send()
+
+            @pl.when((zp <= z) & (z < 3))
+            def _():
+                g_copy(zp, s, 0).wait_send()
+
+            @pl.when((zp >= z) & (z > 0))
+            def _():
+                g_copy(zp, s, 1).wait_send()
+
+
+def attention_stage(rows, w_a, w_b, grads, cos_rows, sin_rows, lens, routes):
+    bf, f32 = jnp.bfloat16, jnp.float32
+    shape = jax.ShapeDtypeStruct
+    width = rows.shape[-1]
+    wide = w_a.shape[-1]
+    hbm = pl.BlockSpec(memory_space=pltpu.HBM)
+    vmem = pl.BlockSpec(memory_space=pltpu.VMEM)
+    dma = pltpu.SemaphoreType.DMA
+    return pl.pallas_call(
+        attention_kernel,
+        out_shape=(
+            shape((width, wide), bf),
+            shape((width, width), bf),
+            shape((8 * CHUNK, width), bf),
+            shape((2 * QUERY_HEADS * 128, 128), bf),
+            shape((4, CHUNK, 512), bf),
+            shape((CHUNK, width), bf),
+            shape((CHUNK, width), f32),
+            shape((CHUNK, width), bf),
+            shape((CHUNK, 128), f32),
+        ),
+        in_specs=[vmem, hbm, hbm, hbm, vmem, vmem, vmem, vmem],
+        out_specs=(hbm, hbm, hbm, hbm, hbm, hbm, vmem, vmem, vmem),
+        scratch_shapes=[
+            pltpu.VMEM((width, wide), bf),
+            pltpu.VMEM((width, width), bf),
+            pltpu.VMEM((2 * QUERY_HEADS * 128, 128), bf),
+            pltpu.VMEM((4, CHUNK, 512), bf),
+            pltpu.VMEM((CHUNK, width), bf),
+            dma((8,)),
+            dma((2, 4)),
+            dma((2, 2, 4)),
+            dma((2, 3, 4)),
+            dma((2, 3, 4)),
+            dma((2, 4, 4)),
+            dma((2, 4, 4)),
+            dma((4, 2)),
+            dma((2, 4, 2)),
+            dma((4, 2)),
+            dma((4, 2)),
+            dma((3, 2)),
+            dma((3, 2)),
+        ],
+        compiler_params=pltpu.CompilerParams(
+            collective_id=2, has_side_effects=True, vmem_limit_bytes=60 * 2**20
+        ),
+        name="attention_stage",
+    )(rows, w_a, w_b, grads, cos_rows, sin_rows, lens, routes)
 
 
 def fast_local(
@@ -893,65 +1335,46 @@
     small = jnp.concatenate(
         [w_router, prenorm[:, None], midnorm[:, None], jnp.zeros((w_router.shape[0], 118), bf)], axis=1
     )
-    packed = jnp.concatenate([w_query, key_value_weight, w_output, small], axis=1)
-    packed = lax.all_gather(packed, both, axis=0, tiled=True)
-    query_all = packed[:, :1536]
-    keyval_all = packed[:, 1536:2048]
-    output_all = packed[:, 2048:3584]
-    router_all = packed[:, 3584:3592]
-    gain_one = packed[:, 3592].astype(f32)
-    gain_two = packed[:, 3593].astype(f32)
-
+    shard_a = jnp.concatenate([w_query, key_value_weight, small], axis=1)
     positions = dp_rank * token_rows + jnp.arange(token_rows, dtype=jnp.int32)
     key_pos = jnp.arange(slots, dtype=jnp.int32)
     cosine_table, sine_table = rope_tables(positions)
-    cosine_table = jnp.tile(cosine_table, (seqs, 1))
-    sine_table = jnp.tile(sine_table, (seqs, 1))
+    cos_rows = jnp.concatenate([cosine_table, cosine_table], axis=1)
+    sin_rows = jnp.concatenate([-sine_table, sine_table], axis=1)
     live = (positions[None, :] < lengths[:, None]).reshape(rows, 1)
-    x = tokens.reshape(rows, width).astype(f32)
+    x = tokens.reshape(rows, width)
     g = jnp.where(live, cotangent.reshape(rows, width), 0)
+    lens = jnp.broadcast_to(lengths[:, None, None], (seqs, 8, 128))
+    full_a, output_all, gall, q_rot, kv_all, attended, mixed, normed2, gates = attention_stage(
+        x, shard_a, w_output, g, cos_rows, sin_rows, lens, routes.reshape(rows, TOP)
+    )
+    gates_t = jnp.transpose(gates[:, :8].reshape(seqs, token_rows, 8), (0, 2, 1))
+    dx, dgate_t, outp, gin, gout = expert_stage(
+        normed2, gall, gates_t, expert_in[0], expert_out[0]
+    )
+    gates = gates[:, :8]
+
+    query_all = full_a[:, :1536]
+    keyval_all = full_a[:, 1536:2048]
+    router_all = full_a[:, 2048:2056]
+    gain_one = full_a[:, 2056].astype(f32)
+    gain_two = full_a[:, 2057].astype(f32)
+    x = x.astype(f32)
     n1, inv1 = rms_parts(x)
     normed = (n1 * gain_one).astype(bf)
-    q = jnp.dot(normed, query_all, preferred_element_type=f32).reshape(rows, QUERY_HEADS, HEAD_SIZE)
-    kv = jnp.dot(normed, keyval_all, preferred_element_type=f32).reshape(
-        rows, 2, KEY_VALUE_HEADS, HEAD_SIZE
-    )
-    q_rot = apply_rotation(q, cosine_table, sine_table).astype(bf)
-    q_rot = q_rot.reshape(seqs, token_rows, KEY_VALUE_HEADS, group, HEAD_SIZE)
-    k_rot = apply_rotation(kv[:, 0], cosine_table, sine_table).astype(bf)
-    kv_own = jnp.stack([k_rot, kv[:, 1].astype(bf)], axis=1).reshape(seqs, token_rows, 512)
-    kv_all = lax.all_gather(kv_own, "dp", axis=1, tiled=True).reshape(
-        seqs, slots, 2, KEY_VALUE_HEADS, HEAD_SIZE
-    )
+    n2, inv2 = rms_parts(mixed)
+    q_rot = q_rot.reshape(seqs, KEY_VALUE_HEADS, group, token_rows, HEAD_SIZE)
+    kv_all = kv_all.reshape(4, seqs, token_rows, 512).transpose(1, 0, 2, 3)
+    kv_all = kv_all.reshape(seqs, slots, 2, KEY_VALUE_HEADS, HEAD_SIZE)
     keys, values = kv_all[:, :, 0], kv_all[:, :, 1]
     allowed = (key_pos[None, None, :] <= positions[None, :, None]) & (
         key_pos[None, None, :] < lengths[:, None, None]
     )
-
-    def score():
-        out = jnp.einsum("sqhgd,skhd->shgqk", q_rot, keys, preferred_element_type=f32) * scale
-        return jnp.where(allowed[:, None, None], out, -1e30)
-
-    scores = score()
-    top = jnp.max(scores, axis=-1, keepdims=True)
-    weights = jnp.exp(scores - top)
-    total = jnp.sum(weights, axis=-1, keepdims=True)
-    lse = top + jnp.log(total)
-    probs_low = (weights / total).astype(bf)
-    attended = jnp.einsum("shgqk,skhd->sqhgd", probs_low, values, preferred_element_type=f32)
-    attended = attended.reshape(rows, QUERY_HEADS * HEAD_SIZE).astype(bf)
-    mixed = x + jnp.dot(attended, output_all, preferred_element_type=f32)
-    n2, inv2 = rms_parts(mixed)
-    normed2 = (n2 * gain_two).astype(bf)
-    logits = jnp.dot(normed2, router_all, preferred_element_type=f32)
-    chosen = jnp.any(
-        routes.reshape(rows, TOP)[:, :, None] == jnp.arange(expert_count, dtype=jnp.int32), axis=1
-    )
-    gates = jax.nn.softmax(jnp.where(chosen, logits, -jnp.inf), axis=-1)
-    gates_t = jnp.transpose(gates.reshape(seqs, token_rows, expert_count), (0, 2, 1))
-    dx, dgate_t, outp, gin, gout = expert_stage(
-        normed2, g, gates_t, expert_in[0], expert_out[0]
-    )
+    cosine_table = jnp.tile(cosine_table, (seqs, 1))
+    sine_table = jnp.tile(sine_table, (seqs, 1))
+    scores = jnp.einsum("shgqd,skhd->shgqk", q_rot, keys, preferred_element_type=f32) * scale
+    scores = jnp.where(allowed[:, None, None], scores, -1e30)
+
     expert_sum = lax.psum_scatter(outp, "expert", scatter_dimension=0, tiled=True).astype(f32)
     block_out = jnp.where(live, mixed + expert_sum, 0.0).astype(bf)
     gf = g.astype(f32)
@@ -965,15 +1388,13 @@
     g_out = jnp.dot(attended.T, dproj, preferred_element_type=f32)
     datt = jnp.dot(dproj, output_all.T, preferred_element_type=f32).astype(bf)
     datt = datt.reshape(seqs, token_rows, KEY_VALUE_HEADS, group, HEAD_SIZE)
-    probs = jnp.exp(score() - lse)
+    probs = jax.nn.softmax(scores, axis=-1)
     dprobs = jnp.einsum("sqhgd,skhd->shgqk", datt, values, preferred_element_type=f32)
     delta = jnp.sum(probs * dprobs, axis=-1, keepdims=True)
     dscores = (probs * (dprobs - delta)).astype(bf)
     dq_rot = jnp.einsum("shgqk,skhd->sqhgd", dscores, keys, preferred_element_type=f32) * scale
-    dk = jnp.einsum("shgqk,sqhgd->skhd", dscores, q_rot, preferred_element_type=f32) * scale
-    dv = jnp.einsum(
-        "shgqk,sqhgd->skhd", probs.astype(bf), datt, preferred_element_type=f32
-    )
+    dk = jnp.einsum("shgqk,shgqd->skhd", dscores, q_rot, preferred_element_type=f32) * scale
+    dv = jnp.einsum("shgqk,sqhgd->skhd", probs.astype(bf), datt, preferred_element_type=f32)
     dkv = jnp.stack([dk, dv], axis=2).reshape(seqs, slots, 512).astype(bf)
     own = lax.psum_scatter(dkv, "dp", scatter_dimension=1, tiled=True).astype(f32)
     own = own.reshape(rows, 2, KEY_VALUE_HEADS, HEAD_SIZE)
@@ -1022,9 +1443,9 @@
         P("expert", "dp", None),
         P("expert", "dp", None),
     )
-    small = mesh.shape["dp"] == 4 and mesh.shape["expert"] == 8
+    fits = mesh.shape["dp"] == 4 and mesh.shape["expert"] == 8
     return jax.shard_map(
-        fast_local if small else local,
+        fast_local if fits else local,
         mesh=mesh,
         in_specs=placed,
         out_specs=(

time: 734 us -> 644 us (0.88)
  waiting for transfers between devices: 337 us -> 228 us
  Pallas kernels: 179 us -> 229 us
  local copies, waits for them, and re-layouts: 116 us -> 97.1 us
  matrix products: 52.8 us -> 38.8 us
    all_gather x2 -> x0, waiting for transfers between devices: 98.3 us -> none  [the longest x1 90.2 us: fast_local(): packed = lax.all_gather(packed, both, axis=0, tiled=True)]
    pallas_call x0 -> x1, Pallas kernels: none -> 96.1 us  [attention_stage(): pl.pallas_call(attention_kernel, out_shape=(shape((width, wide), bf), sha...]
    pallas_call x1, Pallas kernels: 179 us -> 133 us  [expert_stage(): pl.pallas_call(expert_kernel, out_shape=(shape((CHUNK, width), f32), shap...]
    dot_general x7 -> x1, matrix products: 15.4 us -> 0.68 us  [fast_local(): jnp.einsum('shgqk,shgqd->skhd', dscores, q_rot, preferred_element_type=f32)]
    dot_general x4 -> x0, local copies, waits for them, and re-layouts: 14.6 us -> none  [the longest x2 11.5 us: fast_local(): jnp.dot(normed, query_all, preferred_element_type=f32)]
    reduce_scatter x1, waiting for transfers between devices: 64.8 us -> 50.3 us  [fast_local(): lax.psum_scatter(outp, 'expert', scatter_dimension=0, tiled=True)]
    unnamed x9 -> x7, waiting for transfers between devices: 152 us -> 155 us
    unnamed x71 -> x80, local copies, waits for them, and re-layouts: 33.4 us -> 31.9 us
  transfers between devices with their start and end apart: 7 -> 5, of which waited for: 6 -> 4; matrix products, arithmetic and copies ran while one was open for 18% -> 18% of each run, Pallas kernels for 0% -> 0%
where the time goes in v2:
time: 644 us; the launch traced here: 637 us
  Pallas kernels  229 us (36%)
  waiting for transfers between devices  228 us (35%)
  local copies, waits for them, and re-layouts  97.1 us (15%)
  matrix products  38.8 us (6%)
  other arithmetic  27.7 us (4%)
  between operations  14.7 us (2%)
    unnamed x7, waiting for transfers between devices  155 us
    pallas_call x1, Pallas kernels, expert_stage(): pl.pallas_call(expert_kernel, out_shape=(shape((CHUNK, width), f32), shap...  133 us
    pallas_call x1, Pallas kernels, attention_stage(): pl.pallas_call(attention_kernel, out_shape=(shape((width, wide), bf), sha...  96.1 us
    reduce_scatter x1, waiting for transfers between devices, fast_local(): lax.psum_scatter(outp, 'expert', scatter_dimension=0, tiled=True)  50.3 us
    concatenate x1, local copies, waits for them, and re-layouts, fast_local(): jnp.concatenate([g_query, g_kv, g_out, g_router, g_pre[:, None], g_mid[:,...  49.3 us
    unnamed x80, local copies, waits for them, and re-layouts  31.9 us
    reduce_scatter x1, waiting for transfers between devices, fast_local(): lax.psum_scatter(gin, 'dp', scatter_dimension=0, tiled=True).astype(f32)  23.2 us
  transfers between devices with their start and end apart: 5, of which 4 were waited for; matrix products, arithmetic and copies ran while one was open for 18% of the time, Pallas kernels for 0%

profile of v2, /device:TPU:0, one launch (start us, length us, event | category | flops | bytes accessed | tf_op | source)
XLA Modules:
  0.0 636.6 jit_solution(2226775923762143855)
XLA Ops:
  10.6 1.5 copy.85
  13.6 2.1 bitcast_select_fusion.g_hbm
  17.1 96.1 %attention_stage.1 = (bf16[1536,2176]{1,0:T(8,128)(2,1)}, bf16[1536,1536]{1,0:T(8,128)(2,1)}, bf16[2048,1536]{1,0:T(8,128)(2,1)}, bf16[3072,128]{1,0:T(8,128)(2,...) custom-call(bf16[256,1536]{1,0:T(8,128)(2,1)} %bitcast.144, ...), custom_call_target="tpu_custom_call" | custom-call | tf_op jit(solution)/shard_map/attention_stage/pallas_call | solution.py:1269
  113.3 1.6 copy.86
  114.9 133.1 %expert_stage.1 = (f32[256,1536]{1,0:T(8,128)}, f32[2,8,128]{2,1,0:T(8,128)}, bf16[2048,1536]{1,0:T(8,128)(2,1)}, bf16[1536,1536]{1,0:T(8,128)(2,1)}, bf16[768,1536]{1,0:T(8,128)(2,1)}) custom-call(bf16[256,1536]{1,0:T(8,128)(2,1)} %get-tuple-element.25.x_hbm, bf16[2048,1536]{1,0:T(8,128)(2,1)} %get-tuple-element.26.g_hbm, f32[2,8,128]{2,1,0:T(8,128)} %bitcast.173, ...), custom_call_target="tpu_custom_call" | custom-call | tf_op jit(solution)/shard_map/expert_stage/pallas_call | solution.py:819
  249.3 1.1 reshape.327
  250.5 1.8 convert_reduce_fusion
  252.6 3.0 multiply_reduce_fusion
  257.0 1.7 fusion.45
  258.7 6.9 %fusion.47 = (f32[2,2,6,128]{3,2,1,0:T(8,128)}, f32[2,2,6,128,512]{4,3,2,1,0:T(8,128)}) fusion(pred[2,128,512]{2,1,0:T(8,128)(4,1)} %broadcast_and_fusion, bf16[2,2,6,128,128]{4,3,2,1,0:T(8,128)(2,1)} %bitcast.167, bf16[2,512,1,2,128]{4,3,2,1,0:T(2,128)(2,1)} %get-tuple-element.90), kind=kOutput, calls=%fused_computation.99 | convolution fusion | flops 408945152 | bytes 7745536 | tf_op jit(solution)/shard_map/sub | solution.py:1391
  265.6 50.3 %reduce-scatter.10.cloned.1.call-done = bf16[256,1536]{1,0:T(8,128)(2,1)} async-done(((bf16[2048,1536]{1,0:T(8,128)(2,1)}), bf16[256,1536]{1,0:T(8,128)(2,1)}) %reduce-scatter.10.cloned.1.call-update) | async-done | bytes 786448 | tf_op jit(solution)/shard_map/reduce_scatter | solution.py:1378
  315.9 3.0 multiply_add_fusion.2
  318.9 1.1 copy-done
  320.0 3.7 convolution_convert_fusion.3
  323.8 0.9 reshape.349
  324.7 1.5 copy.98
  326.2 3.8 fusion.24
  330.8 2.0 fusion.1
  332.9 1.0 fusion.3
  334.9 1.1 copy.99
  335.9 3.7 copy.112
  339.6 2.4 copy.122
  344.5 1.4 fusion.12
  346.5 2.3 convolution_convert_fusion.4
  348.8 1.1 fusion.14
  349.9 1.0 multiply_bitcast_fusion
  352.8 3.6 convolution_convert_fusion
  356.5 3.7 convolution_convert_fusion.1
  360.1 2.6 fusion.5
  362.7 5.6 reduce-scatter.16.cloned.1.call-done
  368.3 1.1 reshape.344
  370.3 1.2 fusion.35
  372.0 1.2 pad_maximum_fusion.1
  373.2 1.1 reshape.332
  374.3 3.7 multiply_reduce_fusion.1
  378.0 1.8 convolution_convert_fusion.2
  379.8 49.3 %concatenate.38 = bf16[1536,3594]{0,1:T(8,128)(2,1)} concatenate(bf16[1536,1536]{0,1:T(8,128)(2,1)} %convolution_convert_fusion, bf16[1536,512]{0,1:T(8,128)(2,1)} %convolution_convert_fusion.2, bf16[1536,1536]{0,1:T(8,128)(2,1)} %convolution_convert_fusion.1, bf16[1536,8]{0,1:T(8,128)(2,1)S(1)} %copy-done.17, bf16[1536,1]{0,1:T(2,128)(2,1)S(1)} %broadcast_in_dim.98, ...), dimensions={1} | concatenate | bytes 22081536 | tf_op jit(solution)/shard_map/concatenate | solution.py:1411
  429.1 14.8 %copy.114 = bf16[1536,3594]{1,0:T(8,128)(2,1)} copy(bf16[1536,3594]{0,1:T(8,128)(2,1)} %concatenate.38) | data formatting | bytes 22081536
  443.9 2.2 bitcast_convert_fusion.1
  446.1 23.2 %reduce-scatter.12.cloned.1.call-done = bf16[384,1536]{1,0:T(8,128)(2,1)} async-done(((bf16[1536,1536]{1,0:T(8,128)(2,1)}), bf16[384,1536]{1,0:T(8,128)(2,1)}) %reduce-scatter.12.cloned.1.call-update) | async-done | bytes 1179664 | tf_op jit(solution)/shard_map/reduce_scatter | solution.py:1415
  469.3 3.1 bitcast_convert_fusion
  472.4 1.6 multiply_add_fusion
  474.0 148.1 %reduce-scatter.18.cloned.1.call-done = bf16[48,3594]{1,0:T(8,128)(2,1)} async-done(((bf16[1536,3594]{1,0:T(8,128)(2,1)}), bf16[48,3594]{1,0:T(8,128)(2,1)}) %reduce-scatter.18.cloned.1.call-update) | async-done | bytes 345040
  622.1 1.4 copy.115
  623.7 1.4 convert_element_type.121
  625.7 1.0 copy.103
  626.7 1.0 copy.105
  627.6 1.3 slice_bitcast_fusion.1
  (123 shorter events, 18.8 us)
Async XLA Ops:
  7.2 9.3 %copy-start.25 = (s32[2]{0:T(128)S(1)}, s32[2]{0:T(128)}, u32[]{:S(2)}) copy-start(s32[2]{0:T(128)} %param.13) | copy-start | bytes 28
  7.2 8.5 %copy-start.16 = (bf16[48,1536]{1,0:T(8,128)(2,1)S(1)}, bf16[48,1536]{1,0:T(8,128)(2,1)}, u32[]{:S(2)}) copy-start(bf16[48,1536]{1,0:T(8,128)(2,1)} %param.16) | copy-start | bytes 442372
  7.2 8.5 %copy-start.18 = (bf16[48,512]{1,0:T(8,128)(2,1)S(1)}, bf16[48,512]{1,0:T(8,128)(2,1)}, u32[]{:S(2)}) copy-start(bf16[48,512]{1,0:T(8,128)(2,1)} %param.17) | copy-start | bytes 147460
  7.2 308.7 %reduce-scatter.10.cloned.1.call-start = ((), (), s32[]{:S(2)}) async-start(), calls=%async_computation.5 | async-start | bytes 7077888 | tf_op jit(solution)/shard_map/reduce_scatter | solution.py:1378
  7.3 106.0 %copy-start.27 = (s32[128]{0:T(128)}, s32[128]{0:T(128)S(1)}, u32[]{:S(2)}) copy-start(s32[128]{0:T(128)S(1)} %get-tuple-element.109) | copy-start | bytes 1540
  13.5 99.7 %copy-start.24 = (pred[256]{0:T(512)(128)(4,1)}, pred[256]{0:T(512)(128)(4,1)S(1)}, u32[]{:S(2)}) copy-start(pred[256]{0:T(512)(128)(4,1)S(1)} %compare_bitcast_fusion) | copy-start | bytes 772
  247.9 0.7 copy-start.22
  248.0 1.2 copy-start.12
  248.0 120.3 %reduce-scatter.16.cloned.1.call-start = ((), (), s32[]{:S(2)}) async-start(), calls=%async_computation.8 | async-start | bytes 1310720
  249.3 1.1 copy-start.7
  249.3 3.0 copy-start.2
  250.4 2.1 copy-start.11
  250.5 5.0 copy-start.20
  252.5 3.0 copy-start.21
  252.5 3.6 copy-start.26
  252.5 3.6 copy-start.28
  252.6 4.5 copy-start.6
  318.9 1.1 copy-start
  324.7 5.3 slice-start
  326.2 4.3 slice-start.1
  326.2 4.4 copy-start.13
  326.2 4.6 copy-start.15
  326.2 4.6 copy-start.19
  330.0 2.8 slice-start.2
  330.8 2.1 slice-start.3
  332.9 1.1 copy-start.14
  342.1 101.8 %reduce-scatter.14.cloned.1.call-start = ((), (), s32[]{:S(2)}) async-start(), calls=%async_computation.7 | async-start | bytes 2949120 | tf_op jit(solution)/shard_map/reduce_scatter | solution.py:1416
  342.8 126.5 %reduce-scatter.12.cloned.1.call-start = ((), (), s32[]{:S(2)}) async-start(), calls=%async_computation.6 | async-start | bytes 5898240 | tf_op jit(solution)/shard_map/reduce_scatter | solution.py:1415
  343.4 278.7 %reduce-scatter.18.cloned.1.call-start = ((), (), s32[]{:S(2)}) async-start(), calls=%async_computation.9 | async-start | bytes 11759616
  343.7 5.1 copy-start.3
  344.5 5.5 copy-start.8
  351.7 1.2 copy-start.5
  352.8 3.6 copy-start.1
  352.8 3.6 copy-start.9
  352.8 7.3 %slice-start.4 = ((s8[6684672]{0:T(1024)(128)(4,1)}), s8[4194304]{0:T(1024)(128)(4,1)S(1)}, s32[]{:S(2)}) async-start(s8[6684672]{0:T(1024)(128)(4,1)} %bitcast.171), calls=%async_computation.14 | async-start | bytes 8388608
  356.5 3.7 slice-start.5
  370.3 4.0 copy-start.4
  370.3 4.0 copy-start.23
  378.0 1.8 copy-start.17
  469.3 3.1 copy-start.10
Sparse Core Ops, SparseCore 0:
  248.1 67.7 reduce-scatter.9
  342.2 26.0 reduce-scatter.15
  371.7 37.3 reduce-scatter.13
  412.2 57.0 reduce-scatter.11
  476.2 145.8 reduce-scatter.17

commit v3 on v2

--- a/solution.py
+++ b/solution.py
@@ -1308,6 +1308,642 @@
     )(rows, w_a, w_b, grads, cos_rows, sin_rows, lens, routes)
 
 
+def backward_kernel(
+    dx_ref,
+    dgt_ref,
+    gates_ref,
+    mixed_ref,
+    g_ref,
+    tok_ref,
+    q_ref,
+    kv_ref,
+    att_ref,
+    cos_ref,
+    sin_ref,
+    lens_ref,
+    live_ref,
+    wa_hbm,
+    wb_hbm,
+    gin_hbm,
+    gout_hbm,
+    outp_hbm,
+    block_out,
+    dtok_out,
+    ga_out,
+    gb_out,
+    ein_out,
+    eout_out,
+    osib,
+    oro,
+    ori,
+    wide,
+    small,
+    ga,
+    gb,
+    sib_a,
+    sib_b,
+    ta,
+    xa,
+    ya,
+    roa,
+    ria,
+    tb,
+    xb,
+    yb,
+    rob,
+    rib,
+    te,
+    xe,
+    ye,
+    le,
+    old,
+    oslot,
+    dat,
+    dkv,
+    tk,
+    xk,
+    yk,
+    load_sem,
+    le_sem,
+    old_sem,
+    os_recv,
+    os_send,
+    ds_recv,
+    ds_send,
+    t_recv,
+    x_recv,
+    y_recv,
+    t_send,
+    d_send,
+    s_send,
+    ro_recv,
+    ri_recv,
+    hop_send,
+):
+    bf, f32 = jnp.bfloat16, jnp.float32
+    d, e, z, c, x, y = place()
+    d_x = d + 1 - 2 * x
+    d_y = d + 2 - 4 * y
+    d_d = 3 - d
+    hi = lax.div(z, 2)
+    zz = z * hi + (3 - z) * (1 - hi)
+    other = 1 - c
+    mid = zz == 2
+    end = zz == 3
+    to_x = (d_x, e)
+    to_y = (d_y, e)
+    to_sib = (d, 2 * z + other)
+    e_in = e + 2 - 4 * hi
+    to_in = (d, e_in)
+    to_out = (d, jnp.where(zz == 2, e - 2 + 4 * hi, e_in))
+
+    dqs = block_out
+    dmix = dtok_out
+
+    barrier = pltpu.get_barrier_semaphore()
+    for target in (to_x, to_y, to_sib, to_in):
+        pl.semaphore_signal(barrier, inc=1, device_id=target, device_id_type=MESH)
+
+    @pl.when(mid)
+    def _():
+        pl.semaphore_signal(barrier, inc=1, device_id=to_out, device_id_type=MESH)
+
+    pl.semaphore_wait(barrier, 7 - zz)
+
+    def order(i):
+        v = i if i < 2 else (5 - zz if i == 2 else zz)
+        return v * hi + (3 - v) * (1 - hi)
+
+    def across(k, src, t, fx, fy):
+        def diag(i):
+            return remote(
+                src(d_d, i), t.at[i], t_send.at[k, i], t_recv.at[k, i], (to_x, to_y)[i % 2]
+            )
+
+        def direct(i):
+            if i % 2 == 0:
+                return remote(src(d_x, i), fx.at[i], d_send.at[k, i], x_recv.at[k, i], to_x)
+            return remote(src(d_y, i), fy.at[i], d_send.at[k, i], y_recv.at[k, i], to_y)
+
+        def summed(i, ref):
+            if i % 2 == 0:
+                return remote(ref, fy.at[i], s_send.at[k, i], y_recv.at[k, i], to_y)
+            return remote(ref, fx.at[i], s_send.at[k, i], x_recv.at[k, i], to_x)
+
+        def wait_t(i):
+            remote(t.at[i], t.at[i], t_send.at[k, i], t_recv.at[k, i], to_x).wait_recv()
+
+        def wait_xy(i):
+            remote(fx.at[i], fx.at[i], d_send.at[k, i], x_recv.at[k, i], to_x).wait_recv()
+            remote(fy.at[i], fy.at[i], d_send.at[k, i], y_recv.at[k, i], to_y).wait_recv()
+
+        def drain(n):
+            for i in range(n):
+                diag(i).wait_send()
+                direct(i).wait_send()
+                summed(i, t.at[i]).wait_send()
+
+        return diag, direct, summed, wait_t, wait_xy, drain
+
+    def along(k, slot, ro, ri):
+        def send(i, target, dst, recv):
+            return remote(slot(i), dst.at[i], hop_send.at[k, i], recv.at[k, i], target)
+
+        def to_ro(i):
+            return send(i, to_in, ro, ro_recv)
+
+        def to_ri(i):
+            return send(i, to_in if i < 2 else to_out, ri, ri_recv)
+
+        def wait_ro(i):
+            remote(ro.at[i], ro.at[i], hop_send.at[k, i], ro_recv.at[k, i], to_in).wait_recv()
+
+        def wait_ri(i):
+            remote(ri.at[i], ri.at[i], hop_send.at[k, i], ri_recv.at[k, i], to_in).wait_recv()
+
+        def drain():
+            for i in range(3):
+                to_ro(i).wait_send()
+
+        return to_ro, to_ri, wait_ro, wait_ri, drain
+
+    def expert_src(dd, p):
+        if p < 4:
+            return gin_hbm.at[pl.ds(pl.multiple_of(dd * 384 + p * PIECE, 16), PIECE)]
+        return gout_hbm.at[pl.ds(pl.multiple_of(dd * 192 + (p - 4) * PIECE, 16), PIECE)]
+
+    e_diag, e_direct, e_summed, e_wait_t, e_wait_xy, e_drain = across(0, expert_src, te, xe, ye)
+
+    def e_load(p, dd, j):
+        return pltpu.make_async_copy(expert_src(dd, p), le.at[j], le_sem.at[j])
+
+    def e_middle(p):
+        load = e_load(p, d_y if p % 2 == 0 else d_x, 0)
+        load.start()
+        e_wait_t(p)
+        load.wait()
+        te[p] = (te[p].astype(f32) + le[0].astype(f32)).astype(bf)
+        e_summed(p, te.at[p]).start()
+
+    def e_final(p):
+        load = e_load(p, d, 1)
+        load.start()
+        e_wait_xy(p)
+        load.wait()
+        total = le[1].astype(f32) + xe[p].astype(f32) + ye[p].astype(f32)
+        if p < 4:
+            ein_out[p * PIECE : (p + 1) * PIECE] = total.astype(bf)
+        else:
+            eout_out[(p - 4) * PIECE : (p - 3) * PIECE] = total.astype(bf)
+
+    dense = ((ga, sib_a, ta, xa, ya, roa, ria, ga_out), (gb, sib_b, tb, xb, yb, rob, rib, gb_out))
+
+    def dense_stream(j):
+        grad, sib, t, fx, fy, ro, ri, out = dense[j]
+
+        def src(dd, i):
+            return grad.at[dd * 4 + order(i), c]
+
+        diag, direct, summed, wait_t, wait_xy, drain = across(1 + j, src, t, fx, fy)
+
+        def own_slot(i):
+            return grad.at[d * 4 + order(i), c]
+
+        to_ro, to_ri, wait_ro, wait_ri, drain_z = along(j, own_slot, ro, ri)
+
+        def sib_copy():
+            return remote(grad.at[:, other], sib, ds_send.at[j], ds_recv.at[j], to_sib)
+
+        def begin():
+            sib_copy().wait_recv()
+
+            @pl.loop(0, 16)
+            def _(k):
+                grad[k, c] = (grad[k, c].astype(f32) + sib[k].astype(f32)).astype(bf)
+
+            for i in range(4):
+                diag(i).start()
+            for i in range(4):
+                direct(i).start()
+
+        def middle(i):
+            dd = d_y if i % 2 == 0 else d_x
+            wait_t(i)
+            at = dd * 4 + order(i)
+            grad[at, c] = (grad[at, c].astype(f32) + t[i].astype(f32)).astype(bf)
+            summed(i, src(dd, i)).start()
+
+        def local(i):
+            return grad[d * 4 + order(i), c].astype(f32) + fx[i].astype(f32) + fy[i].astype(f32)
+
+        def put(i, total):
+            grad[d * 4 + order(i), c] = total.astype(bf)
+
+        def last(i):
+            wait_xy(i)
+            if i == 3:
+                return
+
+            @pl.when(end)
+            def _():
+                put(i, local(i))
+                to_ro(i).start()
+
+        def hop(i):
+            @pl.when(mid)
+            def _():
+                if i < 2:
+                    wait_ro(i)
+                    put(i, local(i) + ro[i].astype(f32))
+                else:
+                    wait_ri(0)
+                    put(2, local(2) + ri[0].astype(f32))
+                to_ri(i).start()
+
+        def finish():
+            @pl.when(mid)
+            def _():
+                wait_ro(2)
+                wait_ri(1)
+                out[...] = local(3) + ro[2].astype(f32) + ri[1].astype(f32)
+
+            @pl.when(end)
+            def _():
+                wait_ri(2)
+                out[...] = local(3) + ri[2].astype(f32)
+
+        def drain_all():
+            sib_copy().wait_send()
+            drain(4)
+            drain_z()
+
+        return sib_copy, begin, middle, last, hop, finish, drain_all
+
+    a_sib, a_begin, a_middle, a_last, a_hop, a_finish, a_drain = dense_stream(0)
+    b_sib, b_begin, b_middle, b_last, b_hop, b_finish, b_drain = dense_stream(1)
+
+    def out_rows(i, lane):
+        return outp_hbm.at[pl.ds(pl.multiple_of((2 * order(i) + lane) * CHUNK, CHUNK), CHUNK)]
+
+    def out_sib(i):
+        return remote(out_rows(i, other), osib.at[i], os_send.at[i], os_recv.at[i], to_sib)
+
+    o_ro, o_ri, o_wait_ro, o_wait_ri, o_drain = along(2, lambda i: oslot.at[i], oro, ori)
+
+    def out_sum(i, incoming, store):
+        out_sib(i).wait_recv()
+        for half in range(2):
+            rows = pl.ds(half * 128, 128)
+            loads = [
+                pltpu.make_async_copy(ref.at[rows], old.at[j], old_sem.at[j])
+                for j, ref in enumerate([out_rows(i, c), osib.at[i]] + incoming)
+            ]
+            for load in loads:
+                load.start()
+            for load in loads:
+                load.wait()
+            total = old[0].astype(f32)
+            for j in range(1, len(loads)):
+                total = total + old[j].astype(f32)
+            store(slice(half * 128, (half + 1) * 128), total)
+
+    def out_slot(i):
+        def store(rows, total):
+            oslot[i, rows] = total.astype(bf)
+
+        return store
+
+    def out_end(i):
+        @pl.when(end)
+        def _():
+            out_sum(i, [], out_slot(i))
+            o_ro(i).start()
+
+    def out_mid(i):
+        @pl.when(mid)
+        def _():
+            if i < 2:
+                o_wait_ro(i)
+                out_sum(i, [oro.at[i]], out_slot(i))
+            else:
+                o_wait_ri(0)
+                out_sum(2, [ori.at[0]], out_slot(2))
+            o_ri(i).start()
+
+    def out_finish():
+        def store(rows, total):
+            total = total + mixed_ref[rows]
+            block_out[rows] = jnp.where(live_ref[rows, 0:1] > 0, total, 0.0).astype(bf)
+
+        @pl.when(mid)
+        def _():
+            o_wait_ro(2)
+            o_wait_ri(1)
+            out_sum(3, [oro.at[2], ori.at[1]], store)
+
+        @pl.when(end)
+        def _():
+            o_wait_ri(2)
+            out_sum(3, [ori.at[2]], store)
+
+    def kv_src(dd, i):
+        return dkv.at[dd, pl.ds(i * 128, 128)]
+
+    k_diag, k_direct, k_summed, k_wait_t, k_wait_xy, k_drain = across(3, kv_src, tk, xk, yk)
+
+    def k_middle(i):
+        dd = d_y if i % 2 == 0 else d_x
+        k_wait_t(i)
+        rows = slice(i * 128, (i + 1) * 128)
+        dkv[dd, rows] = (dkv[dd, rows].astype(f32) + tk[i].astype(f32)).astype(bf)
+        k_summed(i, kv_src(dd, i)).start()
+
+    small_load = pltpu.make_async_copy(wa_hbm.at[:, pl.ds(2048, 128)], small, load_sem.at[0])
+    wb_load = pltpu.make_async_copy(wb_hbm, wide.at[:, pl.ds(0, 1536)], load_sem.at[1])
+    wa_load = pltpu.make_async_copy(wa_hbm.at[:, pl.ds(0, 2048)], wide, load_sem.at[2])
+    small_load.start()
+    wb_load.start()
+    for p in range(6):
+        e_diag(p).start()
+    for p in range(6):
+        e_direct(p).start()
+    for i in range(4):
+        out_sib(i).start()
+
+    ones = lax.broadcasted_iota(jnp.int32, (CHUNK, 128), 1)
+    eye = (
+        lax.broadcasted_iota(jnp.int32, (128, 128), 0)
+        == lax.broadcasted_iota(jnp.int32, (128, 128), 1)
+    ).astype(f32)
+    dgate = jnp.concatenate(
+        [
+            lax.dot_general(
+                eye,
+                jnp.concatenate([dgt_ref[s], jnp.zeros((120, 128), f32)], axis=0),
+                (((1,), (1,)), ((), ())),
+                preferred_element_type=f32,
+                precision=highest,
+            )
+            for s in range(2)
+        ],
+        axis=0,
+    )
+    gates = gates_ref[...]
+    dlogit = gates * (dgate - jnp.sum(gates * dgate, axis=1, keepdims=True))
+
+    def halves(v):
+        high = v.astype(bf)
+        return high, (v - high.astype(f32)).astype(bf)
+
+    dl_hi, dl_lo = halves(dlogit)
+    small_load.wait()
+    small_t = lax.dot_general(
+        eye.astype(bf), small[...], (((1,), (1,)), ((), ())), preferred_element_type=f32
+    )
+    nt = (((1,), (1,)), ((), ()))
+    tn = (((0,), (0,)), ((), ()))
+
+    def dot_nt(a, b):
+        return lax.dot_general(a, b, nt, preferred_element_type=f32)
+
+    def dot_tn(a, b):
+        return lax.dot_general(a, b, tn, preferred_element_type=f32)
+
+    dn2 = dx_ref[...] + dot_nt(dl_hi, small[...]) + dot_nt(dl_lo, small[...])
+    mixed = mixed_ref[...]
+    inv2 = lax.rsqrt(jnp.mean(mixed * mixed, axis=1, keepdims=True) + epsilon)
+    n2 = mixed * inv2
+    normed2 = (n2 * small_t[9:10]).astype(bf)
+    mid_hi, mid_lo = halves(dn2 * n2)
+    col9 = (ones == 9).astype(bf)
+    for r in range(4):
+        cols = slice(r * 384, (r + 1) * 384)
+        part = (
+            dot_tn(normed2[:, cols], dl_hi)
+            + dot_tn(normed2[:, cols], dl_lo)
+            + dot_tn(mid_hi[:, cols], col9)
+            + dot_tn(mid_lo[:, cols], col9)
+        )
+        dsm = part.reshape(4, 2, 48, 128)
+        ga[4 * r : 4 * r + 4, :, :, 2048:] = dsm.astype(bf)
+    u = dn2 * small_t[9:10]
+    dmixed = g_ref[...].astype(f32) + inv2 * (u - n2 * jnp.mean(u * n2, axis=1, keepdims=True))
+    dmix[...] = dmixed
+    dproj = dmixed.astype(bf)
+    for r in range(4):
+        part = dot_tn(att_ref[:, r * 384 : (r + 1) * 384], dproj)
+        gb[4 * r : 4 * r + 4] = part.astype(bf).reshape(4, 2, 48, 1536)
+    b_sib().start()
+    wb_load.wait()
+    datt = dot_nt(dproj, wide[:, :1536]).astype(bf)
+    for head in range(QUERY_HEADS):
+        for s in range(2):
+            at = (s * QUERY_HEADS + head) * 128
+            dat[at : at + 128] = datt[s * 128 : (s + 1) * 128, head * 128 : (head + 1) * 128]
+    wa_load.start()
+    e_middle(0)
+    e_middle(1)
+    b_begin()
+    for i in range(3):
+        out_end(i)
+
+    query_pos = d * 128 + lax.broadcasted_iota(jnp.int32, (128, 512), 0)
+    key_pos = lax.broadcasted_iota(jnp.int32, (128, 512), 1)
+    cos_rows = cos_ref[...]
+    sin_rows = sin_ref[...]
+    scale = HEAD_SIZE ** (-0.5)
+
+    def unrotate_rows(v, cos, sin):
+        return v * cos - pltpu.roll(v, 64, 1) * sin
+
+    @pl.loop(0, 4)
+    def _(n):
+        s = lax.div(n, 2)
+        h = lax.rem(n, 2)
+        srow = pl.ds(pl.multiple_of(s * 128, 128), 128)
+        kcol = pl.ds(pl.multiple_of(h * 128, 128), 128)
+        vcol = pl.ds(pl.multiple_of(256 + h * 128, 128), 128)
+        lens = lens_ref[s][0:1, 0:1]
+        allowed = (key_pos <= query_pos) & (key_pos < lens)
+        ks = kv_ref[:, srow, kcol].reshape(512, 128)
+        vs = kv_ref[:, srow, vcol].reshape(512, 128)
+        dk = None
+        dv = None
+        for half in range(2):
+            rows = pl.ds(pl.multiple_of(n * 768 + half * 384, 128), 384)
+            qh = q_ref[rows]
+            dh = dat[rows]
+            scores = dot_nt(qh, ks).reshape(3, 128, 512) * scale
+            scores = jnp.where(allowed[None], scores, -1e30)
+            probs = jnp.exp(scores - jnp.max(scores, axis=-1, keepdims=True))
+            probs = probs * (1.0 / jnp.sum(probs, axis=-1, keepdims=True))
+            dprobs = dot_nt(dh, vs).reshape(3, 128, 512)
+            delta = jnp.sum(probs * dprobs, axis=-1, keepdims=True)
+            dscores = (probs * (dprobs - delta)).astype(bf).reshape(384, 512)
+            low = probs.astype(bf).reshape(384, 512)
+            dq = jnp.dot(dscores, ks, preferred_element_type=f32) * scale
+            for j in range(3):
+                dqs[srow, pl.ds(pl.multiple_of(h * 768 + (half * 3 + j) * 128, 128), 128)] = (
+                    unrotate_rows(dq[j * 128 : (j + 1) * 128], cos_rows, sin_rows).astype(bf)
+                )
+            dk_part = dot_tn(dscores, qh)
+            dv_part = dot_tn(low, dh)
+            dk = dk_part if dk is None else dk + dk_part
+            dv = dv_part if dv is None else dv + dv_part
+        dkv[:, srow, kcol] = (dk * scale).astype(bf).reshape(4, 128, 128)
+        dkv[:, srow, vcol] = dv.astype(bf).reshape(4, 128, 128)
+
+    for i in range(2):
+        k_diag(i).start()
+    for i in range(2):
+        k_direct(i).start()
+    e_middle(2)
+    e_middle(3)
+
+    tok = tok_ref[...].astype(f32)
+    inv1 = lax.rsqrt(jnp.mean(tok * tok, axis=1, keepdims=True) + epsilon)
+    n1 = tok * inv1
+    normed = (n1 * small_t[8:9]).astype(bf)
+    for r in range(4):
+        part = dot_tn(normed[:, r * 384 : (r + 1) * 384], dqs[...])
+        ga[4 * r : 4 * r + 4, :, :, :1536] = part.astype(bf).reshape(4, 2, 48, 1536)
+    wa_load.wait()
+    k_middle(0)
+    k_middle(1)
+    dn1 = dot_nt(dqs[...], wide[:, :1536])
+    e_middle(4)
+    e_middle(5)
+    out_mid(0)
+    for i in range(4):
+        b_middle(i)
+
+    for i in range(2):
+        k_wait_xy(i)
+    own = jnp.concatenate(
+        [
+            dkv[d, i * 128 : (i + 1) * 128].astype(f32) + xk[i].astype(f32) + yk[i].astype(f32)
+            for i in range(2)
+        ],
+        axis=0,
+    )
+    cos_two = jnp.concatenate([cos_rows] * 2, axis=0)
+    sin_two = jnp.concatenate([sin_rows] * 2, axis=0)
+    dkv_own = jnp.concatenate(
+        [
+            unrotate_rows(own[:, h * 128 : (h + 1) * 128], cos_two, sin_two)
+            for h in range(2)
+        ]
+        + [own[:, 256:]],
+        axis=1,
+    ).astype(bf)
+    dn1 = dn1 + dot_nt(dkv_own, wide[:, 1536:])
+    pre_hi, pre_lo = halves(dn1 * n1)
+    col8 = (ones == 8).astype(bf)
+    for r in range(4):
+        cols = slice(r * 384, (r + 1) * 384)
+        part = dot_tn(normed[:, cols], dkv_own)
+        ga[4 * r : 4 * r + 4, :, :, 1536:2048] = part.astype(bf).reshape(4, 2, 48, 512)
+        part = dot_tn(pre_hi[:, cols], col8) + dot_tn(pre_lo[:, cols], col8)
+        ga[4 * r : 4 * r + 4, :, :, 2048:] = (
+            ga[4 * r : 4 * r + 4, :, :, 2048:].astype(f32) + part.reshape(4, 2, 48, 128)
+        ).astype(bf)
+    a_sib().start()
+    u = dn1 * small_t[8:9]
+    dtok_out[...] = dmix[...] + inv1 * (u - n1 * jnp.mean(u * n1, axis=1, keepdims=True))
+
+    a_begin()
+    for i in range(4):
+        b_last(i)
+    out_mid(1)
+    out_mid(2)
+    for i in range(3):
+        b_hop(i)
+    for p in range(6):
+        e_final(p)
+    for i in range(4):
+        a_middle(i)
+    out_finish()
+    b_finish()
+    for i in range(4):
+        a_last(i)
+        if i < 3:
+            a_hop(i)
+    a_finish()
+
+    e_drain(6)
+    k_drain(2)
+    a_drain()
+    b_drain()
+    o_drain()
+    for i in range(4):
+        out_sib(i).wait_send()
+
+
+def backward_stage(dx, dgt, gates, mixed, g, tok, q, kv, att, cos, sin, lens, live, wa, wb, gin, gout, outp):
+    bf, f32 = jnp.bfloat16, jnp.float32
+    shape = jax.ShapeDtypeStruct
+    width = tok.shape[-1]
+    wide = wa.shape[-1]
+    hbm = pl.BlockSpec(memory_space=pltpu.HBM)
+    vmem = pl.BlockSpec(memory_space=pltpu.VMEM)
+    dma = pltpu.SemaphoreType.DMA
+    dense = []
+    for w in (wide, width):
+        dense += [pltpu.VMEM((4, 48, w), bf)] * 3 + [pltpu.VMEM((3, 48, w), bf)] * 2
+    return pl.pallas_call(
+        backward_kernel,
+        out_shape=(
+            shape((CHUNK, width), bf),
+            shape((CHUNK, width), f32),
+            shape((48, wide), f32),
+            shape((48, width), f32),
+            shape((384, 2 * FF), bf),
+            shape((192, width), bf),
+            shape((4, CHUNK, width), bf),
+            shape((3, CHUNK, width), bf),
+            shape((3, CHUNK, width), bf),
+        ),
+        in_specs=[vmem] * 13 + [hbm] * 5,
+        out_specs=[vmem] * 6 + [hbm] * 3,
+        scratch_shapes=[
+            pltpu.VMEM((width, 2048), bf),
+            pltpu.VMEM((width, 128), bf),
+            pltpu.VMEM((16, 2, 48, wide), bf),
+            pltpu.VMEM((16, 2, 48, width), bf),
+            pltpu.VMEM((16, 48, wide), bf),
+            pltpu.VMEM((16, 48, width), bf),
+            *dense,
+            *([pltpu.VMEM((6, PIECE, width), bf)] * 3),
+            pltpu.VMEM((2, PIECE, width), bf),
+            pltpu.VMEM((4, 128, width), bf),
+            pltpu.VMEM((3, CHUNK, width), bf),
+            pltpu.VMEM((2 * QUERY_HEADS * 128, 128), bf),
+            pltpu.VMEM((4, CHUNK, 512), bf),
+            *([pltpu.VMEM((2, 128, 512), bf)] * 3),
+            dma((3,)),
+            dma((2,)),
+            dma((4,)),
+            dma((4,)),
+            dma((4,)),
+            dma((2,)),
+            dma((2,)),
+            dma((4, 6)),
+            dma((4, 6)),
+            dma((4, 6)),
+            dma((4, 6)),
+            dma((4, 6)),
+            dma((4, 6)),
+            dma((3, 3)),
+            dma((3, 3)),
+            dma((3, 3)),
+        ],
+        compiler_params=pltpu.CompilerParams(
+            collective_id=3, has_side_effects=True, vmem_limit_bytes=64 * 2**20 - 65536
+        ),
+        name="backward_stage",
+    )(dx, dgt, gates, mixed, g, tok, q, kv, att, cos, sin, lens, live, wa, wb, gin, gout, outp)
+
+
 def fast_local(
     tokens,
     lengths,
@@ -1324,20 +1960,13 @@
 ):
     bf, f32 = jnp.bfloat16, jnp.float32
     seqs, token_rows, width = tokens.shape
-    dp_size = lax.axis_size("dp")
     dp_rank = lax.axis_index("dp")
-    expert_count = lax.axis_size("expert")
-    group = QUERY_HEADS // KEY_VALUE_HEADS
-    slots = token_rows * dp_size
     rows = seqs * token_rows
-    scale = HEAD_SIZE ** (-0.5)
-    both = ("dp", "expert")
     small = jnp.concatenate(
         [w_router, prenorm[:, None], midnorm[:, None], jnp.zeros((w_router.shape[0], 118), bf)], axis=1
     )
     shard_a = jnp.concatenate([w_query, key_value_weight, small], axis=1)
     positions = dp_rank * token_rows + jnp.arange(token_rows, dtype=jnp.int32)
-    key_pos = jnp.arange(slots, dtype=jnp.int32)
     cosine_table, sine_table = rope_tables(positions)
     cos_rows = jnp.concatenate([cosine_table, cosine_table], axis=1)
     sin_rows = jnp.concatenate([-sine_table, sine_table], axis=1)
@@ -1345,86 +1974,29 @@
     x = tokens.reshape(rows, width)
     g = jnp.where(live, cotangent.reshape(rows, width), 0)
     lens = jnp.broadcast_to(lengths[:, None, None], (seqs, 8, 128))
-    full_a, output_all, gall, q_rot, kv_all, attended, mixed, normed2, gates = attention_stage(
+    full_a, full_b, gall, q_rot, kv_all, attended, mixed, normed2, gates = attention_stage(
         x, shard_a, w_output, g, cos_rows, sin_rows, lens, routes.reshape(rows, TOP)
     )
     gates_t = jnp.transpose(gates[:, :8].reshape(seqs, token_rows, 8), (0, 2, 1))
     dx, dgate_t, outp, gin, gout = expert_stage(
         normed2, gall, gates_t, expert_in[0], expert_out[0]
     )
-    gates = gates[:, :8]
-
-    query_all = full_a[:, :1536]
-    keyval_all = full_a[:, 1536:2048]
-    router_all = full_a[:, 2048:2056]
-    gain_one = full_a[:, 2056].astype(f32)
-    gain_two = full_a[:, 2057].astype(f32)
-    x = x.astype(f32)
-    n1, inv1 = rms_parts(x)
-    normed = (n1 * gain_one).astype(bf)
-    n2, inv2 = rms_parts(mixed)
-    q_rot = q_rot.reshape(seqs, KEY_VALUE_HEADS, group, token_rows, HEAD_SIZE)
-    kv_all = kv_all.reshape(4, seqs, token_rows, 512).transpose(1, 0, 2, 3)
-    kv_all = kv_all.reshape(seqs, slots, 2, KEY_VALUE_HEADS, HEAD_SIZE)
-    keys, values = kv_all[:, :, 0], kv_all[:, :, 1]
-    allowed = (key_pos[None, None, :] <= positions[None, :, None]) & (
-        key_pos[None, None, :] < lengths[:, None, None]
-    )
-    cosine_table = jnp.tile(cosine_table, (seqs, 1))
-    sine_table = jnp.tile(sine_table, (seqs, 1))
-    scores = jnp.einsum("shgqd,skhd->shgqk", q_rot, keys, preferred_element_type=f32) * scale
-    scores = jnp.where(allowed[:, None, None], scores, -1e30)
-
-    expert_sum = lax.psum_scatter(outp, "expert", scatter_dimension=0, tiled=True).astype(f32)
-    block_out = jnp.where(live, mixed + expert_sum, 0.0).astype(bf)
-    gf = g.astype(f32)
-    dgate = jnp.transpose(dgate_t, (0, 2, 1)).reshape(rows, expert_count)
-    dlogit = gates * (dgate - jnp.sum(gates * dgate, axis=-1, keepdims=True))
-    g_router = jnp.dot(normed2.astype(f32).T, dlogit, precision=highest)
-    dn2 = dx + jnp.dot(dlogit, router_all.astype(f32).T, precision=highest)
-    g_mid = jnp.sum(dn2 * n2, axis=0)
-    dmixed = gf + norm_back(dn2, n2, inv2, gain_two)
-    dproj = dmixed.astype(bf)
-    g_out = jnp.dot(attended.T, dproj, preferred_element_type=f32)
-    datt = jnp.dot(dproj, output_all.T, preferred_element_type=f32).astype(bf)
-    datt = datt.reshape(seqs, token_rows, KEY_VALUE_HEADS, group, HEAD_SIZE)
-    probs = jax.nn.softmax(scores, axis=-1)
-    dprobs = jnp.einsum("sqhgd,skhd->shgqk", datt, values, preferred_element_type=f32)
-    delta = jnp.sum(probs * dprobs, axis=-1, keepdims=True)
-    dscores = (probs * (dprobs - delta)).astype(bf)
-    dq_rot = jnp.einsum("shgqk,skhd->sqhgd", dscores, keys, preferred_element_type=f32) * scale
-    dk = jnp.einsum("shgqk,shgqd->skhd", dscores, q_rot, preferred_element_type=f32) * scale
-    dv = jnp.einsum("shgqk,sqhgd->skhd", probs.astype(bf), datt, preferred_element_type=f32)
-    dkv = jnp.stack([dk, dv], axis=2).reshape(seqs, slots, 512).astype(bf)
-    own = lax.psum_scatter(dkv, "dp", scatter_dimension=1, tiled=True).astype(f32)
-    own = own.reshape(rows, 2, KEY_VALUE_HEADS, HEAD_SIZE)
-    dq = unrotate(dq_rot.reshape(rows, QUERY_HEADS, HEAD_SIZE), cosine_table, sine_table)
-    dq = dq.astype(bf).reshape(rows, QUERY_HEADS * HEAD_SIZE)
-    dk_own = unrotate(own[:, 0], cosine_table, sine_table).astype(bf)
-    dkv_own = jnp.stack([dk_own, own[:, 1].astype(bf)], axis=1).reshape(rows, 512)
-    g_query = jnp.dot(normed.T, dq, preferred_element_type=f32)
-    g_kv = jnp.dot(normed.T, dkv_own, preferred_element_type=f32)
-    dn1 = jnp.dot(dq, query_all.T, preferred_element_type=f32)
-    dn1 = dn1 + jnp.dot(dkv_own, keyval_all.T, preferred_element_type=f32)
-    g_pre = jnp.sum(dn1 * n1, axis=0)
-    grad_tokens = dmixed + norm_back(dn1, n1, inv1, gain_one)
-    dense = jnp.concatenate(
-        [g_query, g_kv, g_out, g_router, g_pre[:, None], g_mid[:, None]], axis=1
-    ).astype(bf)
-    dense = lax.psum_scatter(dense, both, scatter_dimension=0, tiled=True).astype(f32)
-    upper = lax.psum_scatter(gin, "dp", scatter_dimension=0, tiled=True).astype(f32)
-    down = lax.psum_scatter(gout, "dp", scatter_dimension=0, tiled=True).astype(f32)
+    live_f = jnp.broadcast_to(live.astype(f32), (rows, 128))
+    block_out, grad_tokens, g_a, g_b, g_in, g_out = backward_stage(
+        dx, dgate_t, gates, mixed, g, x, q_rot, kv_all, attended, cos_rows, sin_rows, lens, live_f,
+        full_a, full_b, gin, gout, outp,
+    )[:6]
     return (
         block_out.reshape(seqs, token_rows, width),
         grad_tokens.reshape(seqs, token_rows, width),
-        dense[:, 3592],
-        dense[:, :1536],
-        dense[:, 1536:2048],
-        dense[:, 2048:3584],
-        dense[:, 3593],
-        dense[:, 3584:3592],
-        upper[None],
-        down[None],
+        g_a[:, 2056],
+        g_a[:, :1536],
+        g_a[:, 1536:2048],
+        g_b,
+        g_a[:, 2057],
+        g_a[:, 2048:2056],
+        g_in.astype(f32)[None],
+        g_out.astype(f32)[None],
     )
 
 

time: 644 us -> 403 us (0.63)
  waiting for transfers between devices: 228 us -> 0 us
  Pallas kernels: 229 us -> 369 us
  local copies, waits for them, and re-layouts: 97.1 us -> 18 us
  matrix products: 38.8 us -> 0 us
  other arithmetic: 27.7 us -> 8.6 us
  between operations: 14.7 us -> 0.9 us
    unnamed x7 -> x0, waiting for transfers between devices: 155 us -> none
    pallas_call x0 -> x1, Pallas kernels: none -> 140 us  [backward_stage(): pl.pallas_call(backward_kernel, out_shape=(shape((CHUNK, width), bf), sha...]
    reduce_scatter x3 -> x0, waiting for transfers between devices: 73.5 us -> none  [the longest x1 50.3 us: fast_local(): lax.psum_scatter(outp, 'expert', scatter_dimension=0, tiled=True)]
    concatenate x1 -> x0, local copies, waits for them, and re-layouts: 49.3 us -> none  [fast_local(): jnp.concatenate([g_query, g_kv, g_out, g_router, g_pre[:, None], g_mid[:,...]
    dot_general x12 -> x0, matrix products: 31.8 us -> none  [the longest x1 3.78 us: fast_local(): jnp.einsum('shgqk,sqhgd->skhd', probs.astype(bf), datt, preferred_element...]
    unnamed x80 -> x14, local copies, waits for them, and re-layouts: 31.9 us -> 5.66 us
    sub x1 -> x0, matrix products: 6.93 us -> none  [fast_local(): probs = jax.nn.softmax(scores, axis=-1)]
  transfers between devices with their start and end apart: 5 -> 0, of which waited for: 4 -> 0; matrix products, arithmetic and copies ran while one was open for 18% -> 0% of each run, Pallas kernels for 0% -> 0%
where the time goes in v3:
time: 403 us; the launch traced here: 397 us
  Pallas kernels  369 us (92%)
  local copies, waits for them, and re-layouts  18 us (4%)
  other arithmetic  8.6 us (2%)
    pallas_call x1, Pallas kernels, backward_stage(): pl.pallas_call(backward_kernel, out_shape=(shape((CHUNK, width), bf), sha...  140 us
    pallas_call x1, Pallas kernels, expert_stage(): pl.pallas_call(expert_kernel, out_shape=(shape((CHUNK, width), f32), shap...  133 us
    pallas_call x1, Pallas kernels, attention_stage(): pl.pallas_call(attention_kernel, out_shape=(shape((width, wide), bf), sha...  96.1 us

profile of v3, /device:TPU:0, one launch (start us, length us, event | category | flops | bytes accessed | tf_op | source)
XLA Modules:
  0.0 397.0 jit_solution(12017872394018168647)
XLA Ops:
  0.7 0.7 fusion.2
  1.4 1.3 broadcast_in_dim.53.lens_ref
  2.7 0.8 copy.28
  3.5 0.8 copy.29
  4.2 0.8 copy.27
  5.0 0.8 broadcast_in_dim.54.live_ref
  5.8 1.5 copy.30
  7.3 1.7 concatenate.9.wa_hbm
  8.9 0.3 fusion
  9.2 0.7 pad_maximum_fusion.1.sin_ref
  10.0 0.7 pad_maximum_fusion.cos_ref
  10.7 2.1 bitcast_select_fusion.g_hbm.g_ref
  12.8 96.1 %attention_stage.1 = (bf16[1536,2176]{1,0:T(8,128)(2,1)}, bf16[1536,1536]{1,0:T(8,128)(2,1)}, bf16[2048,1536]{1,0:T(8,128)(2,1)}, bf16[3072,128]{1,0:T(8,128)(2,...) custom-call(bf16[256,1536]{1,0:T(8,128)(2,1)} %bitcast.23, ...), custom_call_target="tpu_custom_call" | custom-call | tf_op jit(solution)/shard_map/attention_stage/pallas_call | solution.py:1269
  108.9 1.6 copy.31
  110.5 133.0 %expert_stage.1 = (f32[256,1536]{1,0:T(8,128)}, f32[2,8,128]{2,1,0:T(8,128)}, bf16[2048,1536]{1,0:T(8,128)(2,1)}, bf16[1536,1536]{1,0:T(8,128)(2,1)}, bf16[768,1536]{1,0:T(8,128)(2,1)}) custom-call(bf16[256,1536]{1,0:T(8,128)(2,1)} %get-tuple-element.30.x_hbm, bf16[2048,1536]{1,0:T(8,128)(2,1)} %get-tuple-element.31.g_hbm, f32[2,8,128]{2,1,0:T(8,128)} %bitcast.31, ...), custom_call_target="tpu_custom_call" | custom-call | tf_op jit(solution)/shard_map/expert_stage/pallas_call | solution.py:819
  243.5 140.3 %backward_stage.1 = (bf16[256,1536]{1,0:T(8,128)(2,1)}, f32[256,1536]{1,0:T(8,128)}, f32[48,2176]{1,0:T(8,128)}, f32[48,1536]{1,0:T(8,128)}, bf16[384,1536]{1,0:...) custom-call(f32[256,1536]{1,0:T(8,128)} %get-tuple-element.33.dx_ref, ...), custom_call_target="tpu_custom_call" | custom-call | tf_op jit(solution)/shard_map/backward_stage/pallas_call | solution.py:1893
  383.9 0.0 copy-start.1
  383.9 1.6 slice_reduce_fusion
  385.4 0.7 slice.23
  386.2 0.7 copy.32
  386.8 1.5 slice.21
  388.4 1.7 slice.20
  390.1 0.0 copy-start.2
  390.1 2.3 bitcast_convert_fusion.1
  392.3 0.0 copy-done.1
  392.3 0.0 copy-start
  392.4 1.7 bitcast_convert_fusion
  394.0 0.0 copy-done.2
  394.0 0.0 copy-start.3
  394.1 0.9 copy.36
  394.9 0.0 copy-done
  394.9 1.1 copy.37
  396.1 0.0 copy-done.3
  396.1 0.7 copy.38
  (3 shorter events, 0.0 us)
Async XLA Ops:
  383.9 8.5 %copy-start.1 = (bf16[384,1536]{1,0:T(8,128)(2,1)S(1)}, bf16[384,1536]{1,0:T(8,128)(2,1)}, u32[]{:S(2)}) copy-start(bf16[384,1536]{1,0:T(8,128)(2,1)} %get-tuple-element.48) | copy-start | bytes 3538948
  390.1 4.0 %copy-start.2 = (bf16[256,1536]{1,0:T(8,128)(2,1)S(1)}, bf16[256,1536]{1,0:T(8,128)(2,1)}, u32[]{:S(2)}) copy-start(bf16[256,1536]{1,0:T(8,128)(2,1)} %get-tuple-element.44) | copy-start | bytes 2359300
  392.3 2.6 copy-start
  394.0 2.0 copy-start.3

commit v4 on v3

--- a/solution.py
+++ b/solution.py
@@ -1,5 +1,6 @@
 import jax
 import jax.numpy as jnp
+import numpy as np
 from jax import lax
 from jax.experimental import pallas as pl
 from jax.experimental.pallas import tpu as pltpu
@@ -424,455 +425,22 @@
     return d, e, z, c, x, y
 
 
-def expert_kernel(
-    x_hbm,
-    g_hbm,
-    gt_hbm,
-    win_hbm,
-    wout_hbm,
-    dx_out,
-    dgt_out,
-    outp_hbm,
-    gin_hbm,
-    gout_hbm,
-    win,
-    wout,
-    xall,
-    gall,
-    gtall,
-    dgu,
-    hg,
-    dxb,
-    dgb,
-    sibr,
-    sibg,
-    ro,
-    rog,
-    ri,
-    rig,
-    stage,
-    own_sem,
-    stage_sem,
-    w_recv,
-    w_send,
-    ag_recv,
-    ag_send,
-    sib_recv,
-    sib_send,
-    red_recv,
-    red_send,
-):
-    d, e, z, c, x, y = place()
-    d_x = d + 1 - 2 * x
-    d_y = d + 2 - 4 * y
-    d_d = 3 - d
-    hi = lax.div(z, 2)
-    zz = z * hi + (3 - z) * (1 - hi)
-    other = 1 - c
-    to_x = (d_x, e)
-    to_y = (d_y, e)
-    to_sib = (d, 2 * z + other)
-    to_up = (d, e + jnp.where(z < 3, 2, -2))
-    to_down = (d, e + jnp.where(z > 0, -2, 2))
-    e_in = e + 2 - 4 * hi
-    e_out = e - 2 + 4 * hi
-    to_in = (d, e_in)
-    to_out = (d, jnp.where(zz == 2, e_out, e_in))
-    mid = zz == 2
-    end = zz == 3
-
-    barrier = pltpu.get_barrier_semaphore()
-    for target in (to_x, to_y, to_sib, to_in):
-        pl.semaphore_signal(barrier, inc=1, device_id=target, device_id_type=MESH)
-
-    @pl.when(mid)
-    def _():
-        pl.semaphore_signal(barrier, inc=1, device_id=to_out, device_id_type=MESH)
-
-    pl.semaphore_wait(barrier, 7 - zz)
-
-    gathered = ((x_hbm, xall), (gt_hbm, gtall))
-
-    def part(a, ref, zp, lane, s):
-        if a == 1:
-            return ref.at[2 * zp + lane, s]
-        return ref.at[pl.ds(pl.multiple_of((2 * zp + lane) * CHUNK + s * 128, 128), 128)]
-
-    def own_part(a, ref, s):
-        if a == 1:
-            return ref.at[s]
-        return ref.at[pl.ds(s * 128, 128)]
-
-    def ag_copy(a, zp, s, way, src=None):
-        ref = part(a, gathered[a][1], zp, c, s)
-        return remote(
-            ref if src is None else src,
-            ref,
-            ag_send.at[way, a, zp, s],
-            ag_recv.at[a, zp, s],
-            to_up if way == 0 else to_down,
-        )
-
-    def sib_copy(a, zp, s, src=None):
-        ref = part(a, gathered[a][1], zp, c, s)
-        return remote(
-            ref if src is None else src,
-            ref,
-            sib_send.at[a, zp, s],
-            sib_recv.at[a, zp, s],
-            to_sib,
-        )
-
-    def piece(p, dd):
-        if p < 4:
-            return win.at[pl.ds(pl.multiple_of(dd * 384 + p * PIECE, 16), PIECE)]
-        return wout.at[pl.ds(pl.multiple_of(dd * 192 + (p - 4) * PIECE, 16), PIECE)]
-
-    def own_piece(p):
-        if p < 4:
-            return win_hbm.at[pl.ds(p * PIECE, PIECE)]
-        return wout_hbm.at[pl.ds((p - 4) * PIECE, PIECE)]
-
-    def w_copy(p, way, src_d, target, row, src=None):
-        ref = piece(p, src_d)
-        return remote(
-            ref if src is None else src, ref, w_send.at[row, p], w_recv.at[row, p], target
-        )
-
-    for a in range(2):
-        for s in range(2):
-            src = own_part(a, gathered[a][0], s)
-
-            @pl.when(z < 3)
-            def _():
-                ag_copy(a, z, s, 0, src).start()
-
-            @pl.when(z > 0)
-            def _():
-                ag_copy(a, z, s, 1, src).start()
-
-            sib_copy(a, z, s, src).start()
-    for p in range(6):
-        w_copy(p, 0, d, to_x, 0, own_piece(p)).start()
-        w_copy(p, 0, d, to_y, 1, own_piece(p)).start()
-    own_copies = [
-        pltpu.make_async_copy(
-            x_hbm, xall.at[pl.ds(pl.multiple_of(e * CHUNK, 128), CHUNK)], own_sem.at[0]
-        ),
-        pltpu.make_async_copy(g_hbm, gall, own_sem.at[1]),
-        pltpu.make_async_copy(gt_hbm, gtall.at[e], own_sem.at[2]),
-        pltpu.make_async_copy(
-            win_hbm, win.at[pl.ds(pl.multiple_of(d * 384, 16), 384)], own_sem.at[3]
-        ),
-        pltpu.make_async_copy(
-            wout_hbm, wout.at[pl.ds(pl.multiple_of(d * 192, 16), 192)], own_sem.at[4]
-        ),
-    ]
-    for copy in own_copies:
-        copy.start()
-
-    def pass_on(a, k, s):
-        @pl.when(z - k >= 0)
-        def _():
-            ag_copy(a, z - k, s, 0).wait_recv()
-
-            @pl.when(z < 3)
-            def _():
-                ag_copy(a, z - k, s, 0).start()
-
-            sib_copy(a, z - k, s).start()
-
-        @pl.when(z + k <= 3)
-        def _():
-            ag_copy(a, z + k, s, 1).wait_recv()
-
-            @pl.when(z > 0)
-            def _():
-                ag_copy(a, z + k, s, 1).start()
-
-            sib_copy(a, z + k, s).start()
-
-    for p in range(6):
-        w_copy(p, 0, d_x, to_x, 0).wait_recv()
-        if p % 2 == 0:
-            w_copy(p, 0, d_x, to_y, 3).start()
-        w_copy(p, 0, d_y, to_y, 1).wait_recv()
-        if p % 2 == 1:
-            w_copy(p, 0, d_y, to_x, 2).start()
-        for a in range(2):
-            pass_on(a, 1 + p // 2, p % 2)
-    for p in range(6):
-        if p % 2 == 0:
-            w_copy(p, 0, d_d, to_y, 3).wait_recv()
-        else:
-            w_copy(p, 0, d_d, to_x, 2).wait_recv()
-    for a in range(2):
-        for zp in range(4):
-            for s in range(2):
-                ref = part(a, gathered[a][1], zp, other, s)
-                remote(
-                    ref, ref, sib_send.at[a, zp, s], sib_recv.at[a, zp, s], to_sib
-                ).wait_recv()
-    for copy in own_copies:
-        copy.wait()
-
-    eye = lax.broadcasted_iota(jnp.int32, (128, 128), 0) == lax.broadcasted_iota(
-        jnp.int32, (128, 128), 1
-    )
-    mine = lax.broadcasted_iota(jnp.int32, (8, 128), 0) == e
-
-    def order(i):
-        v = jnp.where(i < 2, i, jnp.where(i == 2, 5 - zz, zz))
-        return v * hi + (3 - v) * (1 - hi)
-
-    def out_copy(i, zp):
-        return pltpu.make_async_copy(
-            stage.at[lax.rem(i, 2)],
-            outp_hbm.at[pl.ds(pl.multiple_of(zp * 512, 512), 512)],
-            stage_sem.at[lax.rem(i, 2)],
-        )
-
-    def lane_rows(i, lane):
-        return pl.ds(pl.multiple_of(i * 512 + lane * CHUNK, CHUNK), CHUNK)
-
-    def sib_sum_copies(i):
-        return (
-            remote(
-                dxb.at[lane_rows(i, other)], sibr.at[i], red_send.at[0, i], red_recv.at[0, i], to_sib
-            ),
-            remote(dgb.at[i, other], sibg.at[i], red_send.at[1, i], red_recv.at[1, i], to_sib),
-        )
-
-    def hop_copies(i, target, dst, dstg, row):
-        return (
-            remote(
-                dxb.at[lane_rows(i, c)], dst.at[i], red_send.at[2, i], red_recv.at[row, i], target
-            ),
-            remote(dgb.at[i, c], dstg.at[i], red_send.at[3, i], red_recv.at[row + 1, i], target),
-        )
-
-    def wait_from(ref, refg, slot, row):
-        remote(ref.at[slot], ref.at[slot], red_send.at[2, slot], red_recv.at[row, slot], to_in).wait_recv()
-        remote(refg.at[slot], refg.at[slot], red_send.at[3, slot], red_recv.at[row + 1, slot], to_in).wait_recv()
-
-    def combine(i, incoming):
-        total = dxb[lane_rows(i, c)].astype(jnp.float32) + sibr[i].astype(jnp.float32)
-        totalg = dgb[i, c] + sibg[i]
-        for ref, refg, slot in incoming:
-            total = total + ref[slot].astype(jnp.float32)
-            totalg = totalg + refg[slot]
-        return total, totalg
-
-    def combine_store(i, incoming):
-        total, totalg = combine(i, incoming)
-        dxb[lane_rows(i, c)] = total.astype(jnp.bfloat16)
-        dgb[i, c] = totalg
-
-    @pl.loop(0, 4)
-    def _(i):
-        zp = order(i)
-        rows = pl.ds(pl.multiple_of(zp * 512, 512), 512)
-        xc = xall[rows]
-        gate = jnp.dot(xc, win[:, :FF], preferred_element_type=jnp.float32)
-        up = jnp.dot(xc, win[:, FF:], preferred_element_type=jnp.float32)
-        back = lax.dot_general(
-            gall[rows], wout[...], (((1,), (1,)), ((), ())), preferred_element_type=jnp.float32
-        )
-        columns = []
-        for lane in range(2):
-            for s in range(2):
-                row = jnp.sum(jnp.where(mine, gtall[2 * zp + lane, s], 0.0), axis=0, keepdims=True)
-                columns.append(jnp.sum(jnp.where(eye, row, 0.0), axis=1, keepdims=True))
-        weight = jnp.concatenate(columns, axis=0)
-        sig = jax.nn.sigmoid(gate)
-        silu = gate * sig
-        hidden = (silu * up).astype(jnp.bfloat16).astype(jnp.float32)
-        dgate = jnp.sum(hidden * back, axis=1, keepdims=True)
-        for lane in range(2):
-            for s in range(2):
-                at = (2 * lane + s) * 128
-                row = jnp.sum(jnp.where(eye, dgate[at : at + 128], 0.0), axis=0, keepdims=True)
-                dgb[i, lane, s] = jnp.where(mine, row, 0.0)
-        hg[rows] = (hidden * weight).astype(jnp.bfloat16)
-        back = back * weight
-        dgu[rows, :FF] = (back * up * (sig * (1.0 + gate * (1.0 - sig)))).astype(jnp.bfloat16)
-        dgu[rows, FF:] = (back * silu).astype(jnp.bfloat16)
-        dxb[pl.ds(pl.multiple_of(i * 512, 512), 512)] = lax.dot_general(
-            dgu[rows], win[...], (((1,), (1,)), ((), ())), preferred_element_type=jnp.float32
-        ).astype(jnp.bfloat16)
-        for copy in sib_sum_copies(i):
-            copy.start()
-
-        @pl.when(i >= 2)
-        def _():
-            out_copy(i, zp).wait()
-
-        stage[lax.rem(i, 2)] = jnp.dot(
-            hg[rows], wout[...], preferred_element_type=jnp.float32
-        ).astype(jnp.bfloat16)
-        out_copy(i, zp).start()
-        for copy in sib_sum_copies(i):
-            copy.wait_recv()
-
-        @pl.when(end & (i < 3))
-        def _():
-            combine_store(i, ())
-            for copy in hop_copies(i, to_in, ro, rog, 2):
-                copy.start()
-
-        @pl.when(mid & (i == 2))
-        def _():
-            wait_from(ro, rog, 0, 2)
-            combine_store(0, ((ro, rog, 0),))
-            for copy in hop_copies(0, to_in, ri, rig, 4):
-                copy.start()
-
-    @pl.when(mid)
-    def _():
-        wait_from(ro, rog, 1, 2)
-        combine_store(1, ((ro, rog, 1),))
-        for copy in hop_copies(1, to_in, ri, rig, 4):
-            copy.start()
-
-    def grad_copy(k, target, at):
-        return pltpu.make_async_copy(
-            stage.at[k % 2, pl.ds(0, 384)], target.at[pl.ds(at, 384)], stage_sem.at[k % 2]
-        )
-
-    blocks = [(gout_hbm, 0), (gout_hbm, 384)] + [(gin_hbm, 384 * k) for k in range(4)]
-    for k in range(2):
-        out_copy(k, 0).wait()
-    for k, (target, at) in enumerate(blocks):
-        if k >= 2:
-            grad_copy(k - 2, *blocks[k - 2]).wait()
-        left = hg if k < 2 else xall
-        right = gall if k < 2 else dgu
-        stage[k % 2, :384] = lax.dot_general(
-            left[:, at : at + 384],
-            right[...],
-            (((0,), (0,)), ((), ())),
-            preferred_element_type=jnp.float32,
-        ).astype(jnp.bfloat16)
-        grad_copy(k, target, at).start()
-        if k == 1:
-
-            @pl.when(mid)
-            def _():
-                wait_from(ri, rig, 0, 4)
-                combine_store(2, ((ri, rig, 0),))
-                for copy in hop_copies(2, to_out, ri, rig, 4):
-                    copy.start()
-
-    for k in (4, 5):
-        grad_copy(k, *blocks[k]).wait()
-
-    @pl.when(mid)
-    def _():
-        wait_from(ro, rog, 2, 2)
-        wait_from(ri, rig, 1, 4)
-        total, totalg = combine(3, ((ro, rog, 2), (ri, rig, 1)))
-        dx_out[...] = total
-        dgt_out[...] = totalg
-
-    @pl.when(end)
-    def _():
-        wait_from(ri, rig, 2, 4)
-        total, totalg = combine(3, ((ri, rig, 2),))
-        dx_out[...] = total
-        dgt_out[...] = totalg
-
-    for p in range(6):
-        w_copy(p, 0, d, to_x, 0, own_piece(p)).wait_send()
-        w_copy(p, 0, d, to_y, 1, own_piece(p)).wait_send()
-        if p % 2 == 0:
-            w_copy(p, 0, d_x, to_y, 3).wait_send()
-        else:
-            w_copy(p, 0, d_y, to_x, 2).wait_send()
-    for a in range(2):
-        for s in range(2):
-            for zp in range(4):
-                sib_copy(a, zp, s).wait_send()
-
-                @pl.when((zp <= z) & (z < 3))
-                def _():
-                    ag_copy(a, zp, s, 0).wait_send()
-
-                @pl.when((zp >= z) & (z > 0))
-                def _():
-                    ag_copy(a, zp, s, 1).wait_send()
-
-    for i in range(4):
-        for copy in sib_sum_copies(i):
-            copy.wait_send()
-        if i < 3:
-            for copy in hop_copies(i, to_in, ro, rog, 2):
-                copy.wait_send()
-
-
-def expert_stage(rows, grads, gates_t, w_in, w_out):
-    bf, f32 = jnp.bfloat16, jnp.float32
-    shape = jax.ShapeDtypeStruct
-    width = rows.shape[-1]
-    hbm = pl.BlockSpec(memory_space=pltpu.HBM)
-    vmem = pl.BlockSpec(memory_space=pltpu.VMEM)
-    dma = pltpu.SemaphoreType.DMA
-    return pl.pallas_call(
-        expert_kernel,
-        out_shape=(
-            shape((CHUNK, width), f32),
-            shape((2, 8, 128), f32),
-            shape((8 * CHUNK, width), bf),
-            shape((width, 2 * FF), bf),
-            shape((FF, width), bf),
-        ),
-        in_specs=[hbm] * 5,
-        out_specs=(vmem, vmem, hbm, hbm, hbm),
-        scratch_shapes=[
-            pltpu.VMEM((width, 2 * FF), bf),
-            pltpu.VMEM((FF, width), bf),
-            pltpu.VMEM((8 * CHUNK, width), bf),
-            pltpu.VMEM((8 * CHUNK, width), bf),
-            pltpu.VMEM((8, 2, 8, 128), f32),
-            pltpu.VMEM((8 * CHUNK, 2 * FF), bf),
-            pltpu.VMEM((8 * CHUNK, FF), bf),
-            pltpu.VMEM((8 * CHUNK, width), bf),
-            pltpu.VMEM((4, 2, 2, 8, 128), f32),
-            pltpu.VMEM((4, CHUNK, width), bf),
-            pltpu.VMEM((4, 2, 8, 128), f32),
-            pltpu.VMEM((3, CHUNK, width), bf),
-            pltpu.VMEM((3, 2, 8, 128), f32),
-            pltpu.VMEM((3, CHUNK, width), bf),
-            pltpu.VMEM((3, 2, 8, 128), f32),
-            pltpu.VMEM((2, 512, width), bf),
-            dma((5,)),
-            dma((2,)),
-            dma((4, 6)),
-            dma((4, 6)),
-            dma((2, 4, 2)),
-            dma((2, 2, 4, 2)),
-            dma((2, 4, 2)),
-            dma((2, 4, 2)),
-            dma((6, 4)),
-            dma((4, 4)),
-        ],
-        compiler_params=pltpu.CompilerParams(
-            collective_id=1, has_side_effects=True, vmem_limit_bytes=63 * 2**20
-        ),
-        name="expert_stage",
-    )(rows, grads, gates_t, w_in, w_out)
-
-
 def attention_kernel(
     tok_ref,
-    wa_hbm,
+    wq_hbm,
+    wkv_hbm,
+    wr_ref,
+    pre_ref,
+    mid_ref,
     wb_hbm,
-    g_hbm,
-    cos_ref,
-    sin_ref,
+    cot_ref,
+    wo_hbm,
+    rope_hbm,
     lens_ref,
     routes_ref,
     wa_out,
     wb_out,
+    wo_out,
     gall,
     q_out,
     kv_out,
@@ -885,7 +453,11 @@
     qs,
     kvs,
     att,
+    g_own,
+    rope,
     own_sem,
+    wo_recv,
+    wo_send,
     z_recv,
     z_send,
     xy_recv,
@@ -923,10 +495,37 @@
     def _():
         pl.semaphore_signal(barrier, inc=1, device_id=to_down, device_id_type=MESH)
 
-    pl.semaphore_wait(barrier, 5 - jnp.where((z == 0) | (z == 3), 1, 0))
+    own_at = pl.multiple_of((d * 8 + e) * 48, 16)
+    own_rows = pl.ds(own_at, 48)
+    own_a = [
+        pltpu.make_async_copy(wq_hbm, wa.at[own_rows, pl.ds(0, 1536)], own_sem.at[0]),
+        pltpu.make_async_copy(wkv_hbm, wa.at[own_rows, pl.ds(1536, 512)], own_sem.at[1]),
+        pltpu.make_async_copy(rope_hbm.at[:, pl.ds(pl.multiple_of(d * 128, 128), 128)], rope, own_sem.at[2]),
+    ]
+    for copy in own_a:
+        copy.start()
+    eye = lax.broadcasted_iota(jnp.int32, (128, 128), 0) == lax.broadcasted_iota(
+        jnp.int32, (128, 128), 1
+    )
+    eye_low = eye.astype(bf)
+    turned = (((0,), (0,)), ((), ()))
+    sub = lax.broadcasted_iota(jnp.int32, (8, 48), 0)
+    gains = jnp.where(
+        sub == 0,
+        pre_ref[...].astype(f32),
+        jnp.where(sub == 1, mid_ref[...].astype(f32), 0.0),
+    )
+    tile = jnp.concatenate([wr_ref[...].astype(f32), gains], axis=0).astype(bf)
+    wa[own_rows, 2048:] = lax.dot_general(
+        tile, eye_low[:16], turned, preferred_element_type=f32
+    ).astype(bf)
+    for s in range(2):
+        rows = slice(s * 128, (s + 1) * 128)
+        slot = d * 128 + lax.broadcasted_iota(jnp.int32, (128, 1), 0)
+        g_own[rows] = jnp.where(slot < lens_ref[s], cot_ref[rows].astype(f32), 0.0).astype(bf)
 
     full = (wa, wb)
-    shard = (wa_hbm, wb_hbm)
+    shard = (None, wb_hbm)
 
     def block(a, dd, zp, lane):
         at = pl.multiple_of((dd * 8 + 2 * zp + lane) * 48, 16)
@@ -962,10 +561,9 @@
             to_sib,
         )
 
-    def have(a, zp, src=None):
-        xy_copy(a, d, zp, 0, to_x, src).start()
-        xy_copy(a, d, zp, 1, to_y, src).start()
-        s_copy(a, d, zp, src).start()
+    def send_xy(a, zp):
+        xy_copy(a, d, zp, 0, to_x).start()
+        xy_copy(a, d, zp, 1, to_y).start()
 
     def own_start(a):
         @pl.when(z < 3)
@@ -976,28 +574,27 @@
         def _():
             z_copy(a, z, 1, shard[a]).start()
 
-        have(a, z, shard[a])
+        s_copy(a, d, z, shard[a]).start()
 
     def from_z(a, k):
+        def arrived(zp, way):
+            z_copy(a, zp, way).wait_recv()
+
+            @pl.when((z < 3) if way == 0 else (z > 0))
+            def _():
+                z_copy(a, zp, way).start()
+
+            if a == 0:
+                send_xy(a, zp)
+            s_copy(a, d, zp).start()
+
         @pl.when(z - k >= 0)
         def _():
-            z_copy(a, z - k, 0).wait_recv()
-
-            @pl.when(z < 3)
-            def _():
-                z_copy(a, z - k, 0).start()
-
-            have(a, z - k)
+            arrived(z - k, 0)
 
         @pl.when(z + k <= 3)
         def _():
-            z_copy(a, z + k, 1).wait_recv()
-
-            @pl.when(z > 0)
-            def _():
-                z_copy(a, z + k, 1).start()
-
-            have(a, z + k)
+            arrived(z + k, 1)
 
     def from_xy_one(a, zp):
         xy_copy(a, d_x, zp, 0, to_x).wait_recv()
@@ -1074,7 +671,7 @@
 
     def g_start():
         for s in range(2):
-            src = g_hbm.at[pl.ds(s * 128, 128)]
+            src = g_own.at[pl.ds(s * 128, 128)]
 
             @pl.when(z < 3)
             def _():
@@ -1107,38 +704,76 @@
 
             gs_copy(z + k, s).start()
 
-    own = [
-        pltpu.make_async_copy(shard[a], block(a, d, z, c), own_sem.at[a]) for a in range(2)
-    ] + [
-        pltpu.make_async_copy(
-            g_hbm, gall.at[pl.ds(pl.multiple_of(e * CHUNK, CHUNK), CHUNK)], own_sem.at[2]
-        )
-    ]
+    def wo_copy(dd, p, row, target, src=None):
+        ref = wo_out.at[pl.ds(pl.multiple_of(dd * 192 + p * PIECE, 16), PIECE)]
+        return remote(
+            ref if src is None else src, ref, wo_send.at[row, p], wo_recv.at[row, p], target
+        )
+
+    def wo_start():
+        for p in range(2):
+            src = wo_hbm.at[pl.ds(p * PIECE, PIECE)]
+            wo_copy(d, p, 0, to_x, src).start()
+            wo_copy(d, p, 1, to_y, src).start()
+
+    def wo_pass():
+        wo_copy(d_x, 0, 0, to_x).wait_recv()
+        wo_copy(d_x, 0, 2, to_y).start()
+        wo_copy(d_y, 1, 1, to_y).wait_recv()
+        wo_copy(d_y, 1, 2, to_x).start()
+
+    def wo_rest():
+        wo_copy(d_x, 1, 0, to_x).wait_recv()
+        wo_copy(d_y, 0, 1, to_y).wait_recv()
+        for p in range(2):
+            wo_copy(d_d, p, 2, to_x).wait_recv()
+
+    pl.semaphore_wait(barrier, 5 - jnp.where((z == 0) | (z == 3), 1, 0))
+    for copy in own_a:
+        copy.wait()
     own_start(0)
     own_start(1)
+    own = [
+        pltpu.make_async_copy(wb_hbm, block(1, d, z, c), own_sem.at[0]),
+        pltpu.make_async_copy(
+            g_own, gall.at[pl.ds(pl.multiple_of(e * CHUNK, CHUNK), CHUNK)], own_sem.at[1]
+        ),
+        pltpu.make_async_copy(
+            wo_hbm, wo_out.at[pl.ds(pl.multiple_of(d * 192, 16), 192)], own_sem.at[2]
+        ),
+    ]
     for copy in own:
         copy.start()
-    g_start()
+    send_xy(0, z)
     tok = tok_ref[...].astype(f32)
     n1 = tok * lax.rsqrt(jnp.mean(tok * tok, axis=1, keepdims=True) + epsilon)
-    for k in range(1, 4):
-        from_z(0, k)
-        from_xy(0, k - 1)
-        from_z(1, k)
+    from_z(0, 1)
+    from_z(1, 1)
+    from_xy(0, 0)
+    from_z(0, 2)
+    from_z(1, 2)
+    g_start()
+    from_xy(0, 1)
+    from_z(0, 3)
+    from_z(1, 3)
+    from_xy(0, 2)
     from_xy(0, 3)
+
+    def turn(j):
+        return lax.rem(z + j, 4)
+
+    own[0].wait()
+    for j in range(2):
+        send_xy(1, turn(j))
     from_diag(0)
-    own[0].wait()
     from_sib(0)
 
-    small = wa[:, 2048:]
-    eye = (
-        lax.broadcasted_iota(jnp.int32, (128, 128), 0)
-        == lax.broadcasted_iota(jnp.int32, (128, 128), 1)
-    ).astype(bf)
-    small_t = lax.dot_general(eye, small, (((1,), (1,)), ((), ())), preferred_element_type=f32)
+    small_t = lax.dot_general(
+        eye_low[:16], wa[:, 2048:], (((1,), (1,)), ((), ())), preferred_element_type=f32
+    )
     normed = (n1 * small_t[8:9]).astype(bf)
-    cos_rows = jnp.concatenate([cos_ref[...]] * 2, axis=0)
-    sin_rows = jnp.concatenate([sin_ref[...]] * 2, axis=0)
+    cos_rows = jnp.concatenate([rope[0]] * 2, axis=0)
+    sin_rows = jnp.concatenate([rope[1]] * 2, axis=0)
 
     def rotate(v):
         return v * cos_rows + pltpu.roll(v, 64, 1) * sin_rows
@@ -1155,23 +790,24 @@
     for s in range(2):
         kv_copy(d, s, 0, to_x).start()
         kv_copy(d, s, 1, to_y).start()
-    from_xy(1, 0)
+    g_pass(1, 0)
     q = jnp.dot(normed, wa[:, :1536], preferred_element_type=f32)
     for head in range(QUERY_HEADS):
         rot = rotate(q[:, head * 128 : (head + 1) * 128]).astype(bf)
         for s in range(2):
             at = (s * QUERY_HEADS + head) * 128
             qs[at : at + 128] = rot[s * 128 : (s + 1) * 128]
-    g_pass(1, 0)
     kv_copy(d_x, 0, 0, to_x).wait_recv()
     kv_copy(d_x, 0, 2, to_y).start()
     kv_copy(d_y, 1, 1, to_y).wait_recv()
     kv_copy(d_y, 1, 2, to_x).start()
+    for j in range(2, 4):
+        send_xy(1, turn(j))
+    for j in range(2):
+        from_xy_one(1, turn(j))
+    g_pass(1, 1)
     kv_copy(d_y, 0, 1, to_y).wait_recv()
     kv_copy(d_x, 1, 0, to_x).wait_recv()
-    for k in range(1, 4):
-        from_xy(1, k)
-    g_pass(1, 1)
     for s in range(2):
         kv_copy(d_d, s, 2, to_x).wait_recv()
     q_copy = pltpu.make_async_copy(qs, q_out, own_sem.at[3])
@@ -1183,11 +819,10 @@
     query_pos = d * 128 + lax.broadcasted_iota(jnp.int32, (128, 512), 0)
     key_pos = lax.broadcasted_iota(jnp.int32, (128, 512), 1)
 
-    @pl.loop(0, 4)
-    def _(n):
+    def attend(n):
         s = lax.div(n, 2)
         h = lax.rem(n, 2)
-        lens = lens_ref[s][0:1, 0:1]
+        lens = lens_ref[s]
         allowed = (key_pos <= query_pos) & (key_pos < lens)
         ks = kvs[:, pl.ds(pl.multiple_of(s * 128, 128), 128), pl.ds(pl.multiple_of(h * 128, 128), 128)]
         vs = kvs[:, pl.ds(pl.multiple_of(s * 128, 128), 128), pl.ds(pl.multiple_of(256 + h * 128, 128), 128)]
@@ -1210,9 +845,14 @@
                     pl.ds(pl.multiple_of(h * 768 + (half * 3 + j) * 128, 128), 128),
                 ] = out[j * 128 : (j + 1) * 128]
 
+    pl.loop(0, 2)(attend)
     g_pass(2, 0)
+    from_xy_one(1, turn(2))
+    pl.loop(2, 4)(attend)
+    from_xy_one(1, turn(3))
+    wo_start()
+    g_pass(2, 1)
     from_diag(1)
-    own[1].wait()
     from_sib(1)
     att_copy = pltpu.make_async_copy(att, att_out, own_sem.at[6])
     wb_copy = pltpu.make_async_copy(wb, wb_out, own_sem.at[7])
@@ -1223,21 +863,27 @@
     n2 = mixed * lax.rsqrt(jnp.mean(mixed * mixed, axis=1, keepdims=True) + epsilon)
     normed2 = (n2 * small_t[9:10]).astype(bf)
     normed_out[...] = normed2
-    logits = jnp.dot(normed2, small, preferred_element_type=f32)
-    lanes = lax.broadcasted_iota(jnp.int32, (CHUNK, 128), 1)
-    chosen = lanes == routes_ref[:, 0:1]
-    for t in range(1, TOP):
-        chosen = chosen | (lanes == routes_ref[:, t : t + 1])
-    logits = jnp.where(chosen, logits, -1e30)
-    weights = jnp.where(chosen, jnp.exp(logits - jnp.max(logits, axis=1, keepdims=True)), 0.0)
-    gates_out[...] = weights / jnp.sum(weights, axis=1, keepdims=True)
-
-    g_pass(2, 1)
+    logits = lax.dot_general(
+        small_t[:8].astype(bf), normed2, (((1,), (1,)), ((), ())), preferred_element_type=f32
+    )
+    number = lax.broadcasted_iota(jnp.int32, (8, 128), 0)
+    for s in range(2):
+        chosen = number == routes_ref[s, 0:1]
+        for t in range(1, TOP):
+            chosen = chosen | (number == routes_ref[s, t : t + 1])
+        picked = jnp.where(chosen, logits[:, s * 128 : (s + 1) * 128], -1e30)
+        top = jnp.max(picked, axis=0, keepdims=True)
+        weights = jnp.where(chosen, jnp.exp(picked - top), 0.0)
+        gates_out[s] = weights / jnp.sum(weights, axis=0, keepdims=True)
+
     g_pass(3, 0)
+    wo_pass()
     g_pass(3, 1)
+    wo_rest()
     for zp in range(4):
         for s in range(2):
             gs_copy(zp, s, lane=other).wait_recv()
+    own[1].wait()
     own[2].wait()
     for copy in (q_copy, kvo_copy, wa_copy, att_copy, wb_copy):
         copy.wait()
@@ -1246,6 +892,7 @@
     for s in range(2):
         for row in range(3):
             kv_copy(d, s, row, to_x).wait_send()
+            wo_copy(d, s, row, to_x).wait_send()
         for zp in range(4):
             gs_copy(zp, s).wait_send()
 
@@ -1258,36 +905,42 @@
                 g_copy(zp, s, 1).wait_send()
 
 
-def attention_stage(rows, w_a, w_b, grads, cos_rows, sin_rows, lens, routes):
+def attention_stage(tok, wq, wkv, wr, pre, mid, wb, cot, wo, rope, lens, routes):
     bf, f32 = jnp.bfloat16, jnp.float32
     shape = jax.ShapeDtypeStruct
-    width = rows.shape[-1]
-    wide = w_a.shape[-1]
+    width = tok.shape[-1]
+    wide = wq.shape[-1] + wkv.shape[-1] + 128
     hbm = pl.BlockSpec(memory_space=pltpu.HBM)
     vmem = pl.BlockSpec(memory_space=pltpu.VMEM)
+    smem = pl.BlockSpec(memory_space=pltpu.SMEM)
     dma = pltpu.SemaphoreType.DMA
     return pl.pallas_call(
         attention_kernel,
         out_shape=(
             shape((width, wide), bf),
             shape((width, width), bf),
+            shape((FF, width), bf),
             shape((8 * CHUNK, width), bf),
             shape((2 * QUERY_HEADS * 128, 128), bf),
             shape((4, CHUNK, 512), bf),
             shape((CHUNK, width), bf),
             shape((CHUNK, width), f32),
             shape((CHUNK, width), bf),
-            shape((CHUNK, 128), f32),
+            shape((2, 8, 128), f32),
         ),
-        in_specs=[vmem, hbm, hbm, hbm, vmem, vmem, vmem, vmem],
-        out_specs=(hbm, hbm, hbm, hbm, hbm, hbm, vmem, vmem, vmem),
+        in_specs=[vmem, hbm, hbm, vmem, vmem, vmem, hbm, vmem, hbm, hbm, smem, vmem],
+        out_specs=[hbm] * 7 + [vmem] * 3,
         scratch_shapes=[
             pltpu.VMEM((width, wide), bf),
             pltpu.VMEM((width, width), bf),
             pltpu.VMEM((2 * QUERY_HEADS * 128, 128), bf),
             pltpu.VMEM((4, CHUNK, 512), bf),
             pltpu.VMEM((CHUNK, width), bf),
+            pltpu.VMEM((CHUNK, width), bf),
+            pltpu.VMEM((2, 128, 128), f32),
             dma((8,)),
+            dma((3, 2)),
+            dma((3, 2)),
             dma((2, 4)),
             dma((2, 2, 4)),
             dma((2, 3, 4)),
@@ -1305,7 +958,547 @@
             collective_id=2, has_side_effects=True, vmem_limit_bytes=60 * 2**20
         ),
         name="attention_stage",
-    )(rows, w_a, w_b, grads, cos_rows, sin_rows, lens, routes)
+    )(tok, wq, wkv, wr, pre, mid, wb, cot, wo, rope, lens, routes)
+
+
+def expert_kernel(
+    x_hbm,
+    g_hbm,
+    gt_hbm,
+    win_hbm,
+    wout_hbm,
+    dx_out,
+    dgt_out,
+    outp_hbm,
+    gin_hbm,
+    gout_out,
+    win,
+    wout,
+    xall,
+    gall,
+    gtall,
+    dgu,
+    hg,
+    dxb,
+    dgb,
+    sibr,
+    sibg,
+    ro,
+    rog,
+    ri,
+    rig,
+    stage,
+    gout,
+    tg,
+    xg,
+    yg,
+    own_sem,
+    stage_sem,
+    g_recv,
+    g_send,
+    w_recv,
+    w_send,
+    ag_recv,
+    ag_send,
+    sib_recv,
+    sib_send,
+    red_recv,
+    red_send,
+):
+    bf, f32 = jnp.bfloat16, jnp.float32
+    d, e, z, c, x, y = place()
+    d_x = d + 1 - 2 * x
+    d_y = d + 2 - 4 * y
+    d_d = 3 - d
+    hi = lax.div(z, 2)
+    zz = z * hi + (3 - z) * (1 - hi)
+    other = 1 - c
+    to_x = (d_x, e)
+    to_y = (d_y, e)
+    to_sib = (d, 2 * z + other)
+    to_up = (d, e + jnp.where(z < 3, 2, -2))
+    to_down = (d, e + jnp.where(z > 0, -2, 2))
+    e_in = e + 2 - 4 * hi
+    to_in = (d, e_in)
+    to_out = (d, jnp.where(zz == 2, e - 2 + 4 * hi, e_in))
+    mid = zz == 2
+    end = zz == 3
+
+    barrier = pltpu.get_barrier_semaphore()
+    for target in (to_x, to_y, to_sib, to_in):
+        pl.semaphore_signal(barrier, inc=1, device_id=target, device_id_type=MESH)
+
+    @pl.when(mid)
+    def _():
+        pl.semaphore_signal(barrier, inc=1, device_id=to_out, device_id_type=MESH)
+
+    own_copies = [
+        pltpu.make_async_copy(x_hbm.at[s], xall.at[e, s], own_sem.at[s]) for s in range(2)
+    ] + [
+        pltpu.make_async_copy(gt_hbm, gtall.at[e], own_sem.at[2]),
+        pltpu.make_async_copy(
+            win_hbm, win.at[pl.ds(pl.multiple_of(d * 384, 16), 384)], own_sem.at[3]
+        ),
+        pltpu.make_async_copy(wout_hbm, wout, own_sem.at[4]),
+        pltpu.make_async_copy(g_hbm, gall, own_sem.at[5]),
+    ]
+    pl.semaphore_wait(barrier, 7 - zz)
+
+    gathered = ((x_hbm, xall), (gt_hbm, gtall))
+
+    def ag_copy(a, zp, s, way, src=None):
+        ref = gathered[a][1].at[2 * zp + c, s]
+        return remote(
+            ref if src is None else src,
+            ref,
+            ag_send.at[way, a, zp, s],
+            ag_recv.at[a, zp, s],
+            to_up if way == 0 else to_down,
+        )
+
+    def sib_copy(a, zp, s, src=None, lane=None):
+        ref = gathered[a][1].at[2 * zp + (c if lane is None else lane), s]
+        return remote(
+            ref if src is None else src,
+            ref,
+            sib_send.at[a, zp, s],
+            sib_recv.at[a, zp, s],
+            to_sib,
+        )
+
+    def own_rows(s):
+        for a in range(2):
+            src = gathered[a][0].at[s]
+
+            @pl.when(z < 3)
+            def _():
+                ag_copy(a, z, s, 0, src).start()
+
+            @pl.when(z > 0)
+            def _():
+                ag_copy(a, z, s, 1, src).start()
+
+            sib_copy(a, z, s, src).start()
+
+    def pass_on(k, s):
+        for a in range(2):
+
+            @pl.when(z - k >= 0)
+            def _():
+                ag_copy(a, z - k, s, 0).wait_recv()
+
+                @pl.when(z < 3)
+                def _():
+                    ag_copy(a, z - k, s, 0).start()
+
+                sib_copy(a, z - k, s).start()
+
+            @pl.when(z + k <= 3)
+            def _():
+                ag_copy(a, z + k, s, 1).wait_recv()
+
+                @pl.when(z > 0)
+                def _():
+                    ag_copy(a, z + k, s, 1).start()
+
+                sib_copy(a, z + k, s).start()
+
+    def from_sib(s):
+        for a in range(2):
+            for zp in range(4):
+                sib_copy(a, zp, s, lane=other).wait_recv()
+
+    def w_copy(p, src_d, target, row, src=None):
+        ref = win.at[pl.ds(pl.multiple_of(src_d * 384 + p * PIECE, 16), PIECE)]
+        return remote(
+            ref if src is None else src, ref, w_send.at[row, p], w_recv.at[row, p], target
+        )
+
+    def w_pass(p):
+        w_copy(p, d_x, to_x, 0).wait_recv()
+        if p % 2 == 0:
+            w_copy(p, d_x, to_y, 3).start()
+        w_copy(p, d_y, to_y, 1).wait_recv()
+        if p % 2 == 1:
+            w_copy(p, d_y, to_x, 2).start()
+
+    own_rows(0)
+    for p in range(4):
+        src = win_hbm.at[pl.ds(p * PIECE, PIECE)]
+        w_copy(p, d, to_x, 0, src).start()
+        w_copy(p, d, to_y, 1, src).start()
+    for copy in own_copies:
+        copy.start()
+    w_pass(0)
+    pass_on(1, 0)
+    w_pass(1)
+    pass_on(2, 0)
+    own_rows(1)
+    w_pass(2)
+    w_pass(3)
+    pass_on(3, 0)
+    pass_on(1, 1)
+    from_sib(0)
+    for p in range(4):
+        if p % 2 == 0:
+            w_copy(p, d_d, to_y, 3).wait_recv()
+        else:
+            w_copy(p, d_d, to_x, 2).wait_recv()
+    for copy in own_copies:
+        copy.wait()
+
+    def order(i):
+        v = i if i < 2 else (5 - zz if i == 2 else zz)
+        return v * hi + (3 - v) * (1 - hi)
+
+    def sib_sum(zp, s, a):
+        src, dst = ((dxb, sibr), (dgb, sibg))[a]
+        return remote(
+            src.at[2 * zp + other, s], dst.at[zp, s], red_send.at[a, zp, s], red_recv.at[a, zp, s], to_sib
+        )
+
+    def hop(i, s, target, inward):
+        dst, dstg, row = (ro, rog, 2) if inward else (ri, rig, 4)
+        zp = order(i)
+        return (
+            remote(
+                dxb.at[2 * zp + c, s], dst.at[i, s], red_send.at[2, i, s], red_recv.at[row, i, s], target
+            ),
+            remote(
+                dgb.at[2 * zp + c, s], dstg.at[i, s], red_send.at[3, i, s], red_recv.at[row + 1, i, s], target
+            ),
+        )
+
+    def wait_from(ref, refg, slot, s, row):
+        remote(
+            ref.at[slot, s], ref.at[slot, s], red_send.at[2, slot, s], red_recv.at[row, slot, s], to_in
+        ).wait_recv()
+        remote(
+            refg.at[slot, s], refg.at[slot, s], red_send.at[3, slot, s], red_recv.at[row + 1, slot, s], to_in
+        ).wait_recv()
+
+    def combine(i, s, incoming):
+        zp = order(i)
+        for a in range(2):
+            remote(
+                sibr.at[zp, s] if a == 0 else sibg.at[zp, s],
+                sibr.at[zp, s] if a == 0 else sibg.at[zp, s],
+                red_send.at[a, zp, s],
+                red_recv.at[a, zp, s],
+                to_sib,
+            ).wait_recv()
+        for ref, refg, slot, row in incoming:
+            wait_from(ref, refg, slot, s, row)
+        total = dxb[2 * zp + c, s].astype(f32) + sibr[zp, s].astype(f32)
+        totalg = dgb[2 * zp + c, s] + sibg[zp, s]
+        for ref, refg, slot, row in incoming:
+            total = total + ref[slot, s].astype(f32)
+            totalg = totalg + refg[slot, s]
+        return total, totalg
+
+    def pass_sum(i, s, incoming, target, inward):
+        total, totalg = combine(i, s, incoming)
+        zp = order(i)
+        dxb[2 * zp + c, s] = total.astype(bf)
+        dgb[2 * zp + c, s] = totalg
+        for copy in hop(i, s, target, inward):
+            copy.start()
+
+    def end_sums(s, which):
+        @pl.when(end)
+        def _():
+            for i in which:
+                pass_sum(i, s, (), to_in, True)
+
+    def mid_sum(i, s):
+        @pl.when(mid)
+        def _():
+            if i < 2:
+                pass_sum(i, s, ((ro, rog, i, 2),), to_in, False)
+            else:
+                pass_sum(2, s, ((ri, rig, 0, 4),), to_out, False)
+
+    def last_sum(s):
+        @pl.when(mid)
+        def _():
+            total, totalg = combine(3, s, ((ro, rog, 2, 2), (ri, rig, 1, 4)))
+            dx_out[s * 128 : (s + 1) * 128] = total
+            dgt_out[s] = totalg
+
+        @pl.when(end)
+        def _():
+            total, totalg = combine(3, s, ((ri, rig, 2, 4),))
+            dx_out[s * 128 : (s + 1) * 128] = total
+            dgt_out[s] = totalg
+
+    eye = lax.broadcasted_iota(jnp.int32, (128, 128), 0) == lax.broadcasted_iota(
+        jnp.int32, (128, 128), 1
+    )
+    mine = lax.broadcasted_iota(jnp.int32, (8, 128), 0) == e
+    nt = (((1,), (1,)), ((), ()))
+    tn = (((0,), (0,)), ((), ()))
+
+    def expert_step(s, pair):
+        first = 4 * pair if pair is not None else 0
+        block = pl.ds(first, 4)
+        xc = xall[block, s].reshape(512, 1536)
+        gate = jnp.dot(xc, win[:, :FF], preferred_element_type=f32)
+        up = jnp.dot(xc, win[:, FF:], preferred_element_type=f32)
+        back = lax.dot_general(
+            gall[block, s].reshape(512, 1536), wout[...], nt, preferred_element_type=f32
+        )
+        columns = []
+        for j in range(4):
+            row = jnp.sum(jnp.where(mine, gtall[first + j, s], 0.0), axis=0, keepdims=True)
+            columns.append(jnp.sum(jnp.where(eye, row, 0.0), axis=1, keepdims=True))
+        weight = jnp.concatenate(columns, axis=0)
+        sig = jax.nn.sigmoid(gate)
+        silu = gate * sig
+        hidden = (silu * up).astype(bf).astype(f32)
+        dgate = jnp.sum(hidden * back, axis=1, keepdims=True)
+        for j in range(4):
+            row = jnp.sum(
+                jnp.where(eye, dgate[j * 128 : (j + 1) * 128], 0.0), axis=0, keepdims=True
+            )
+            dgb[first + j, s] = jnp.where(mine, row, 0.0)
+        hgv = (hidden * weight).astype(bf)
+        hg[block, s] = hgv.reshape(4, 128, FF)
+        back = back * weight
+        dgu[block, s, :, :FF] = (
+            (back * up * (sig * (1.0 + gate * (1.0 - sig)))).astype(bf).reshape(4, 128, FF)
+        )
+        dgu[block, s, :, FF:] = (back * silu).astype(bf).reshape(4, 128, FF)
+        dxb[block, s] = (
+            lax.dot_general(
+                dgu[block, s].reshape(512, 1536), win[...], nt, preferred_element_type=f32
+            )
+            .astype(bf)
+            .reshape(4, 128, 1536)
+        )
+        for j in range(2):
+            for a in range(2):
+                sib_sum(lax.div(first, 2) + j, s, a).start()
+
+    def out_copy(slot, s, first):
+        return pltpu.make_async_copy(
+            stage.at[slot], outp_hbm.at[pl.ds(first, 4), s], stage_sem.at[slot]
+        )
+
+    def out_step(slot, s, pair):
+        first = 4 * pair
+        stage[slot] = (
+            jnp.dot(
+                hg[pl.ds(first, 4), s].reshape(512, FF), wout[...], preferred_element_type=f32
+            )
+            .astype(bf)
+            .reshape(4, 128, 1536)
+        )
+        out_copy(slot, s, first).start()
+
+    far = 1 - hi
+    near = hi
+
+    @pl.loop(0, 4)
+    def _(t):
+        s = lax.div(t, 2)
+        pair = far + lax.rem(t, 2) * (1 - 2 * far)
+        expert_step(s, pair)
+
+        @pl.when(t == 0)
+        def _():
+            pass_on(2, 1)
+            out_step(0, 0, far)
+            end_sums(0, (0, 1))
+
+        @pl.when(t == 1)
+        def _():
+            pass_on(3, 1)
+            from_sib(1)
+            out_step(1, 0, near)
+            end_sums(0, (2,))
+            mid_sum(0, 0)
+
+        @pl.when(t == 2)
+        def _():
+            out_copy(0, 0, 0).wait()
+            out_step(0, 1, far)
+            end_sums(1, (0, 1))
+            mid_sum(1, 0)
+            mid_sum(2, 0)
+
+        @pl.when(t == 3)
+        def _():
+            out_copy(1, 0, 0).wait()
+            out_step(1, 1, near)
+            end_sums(1, (2,))
+            mid_sum(0, 1)
+
+    def g_piece(dd, p):
+        return gout.at[pl.ds(pl.multiple_of(dd * 192 + p * PIECE, 16), PIECE)]
+
+    def g_diag(p):
+        return remote(g_piece(d_d, p), tg.at[p], g_send.at[0, p], g_recv.at[0, p], (to_x, to_y)[p])
+
+    def g_direct(p):
+        if p == 0:
+            return remote(g_piece(d_x, p), xg.at[p], g_send.at[1, p], g_recv.at[1, p], to_x)
+        return remote(g_piece(d_y, p), yg.at[p], g_send.at[1, p], g_recv.at[2, p], to_y)
+
+    def g_summed(p):
+        if p == 0:
+            return remote(g_piece(d_y, p), yg.at[p], g_send.at[2, p], g_recv.at[2, p], to_y)
+        return remote(g_piece(d_x, p), xg.at[p], g_send.at[2, p], g_recv.at[1, p], to_x)
+
+    def g_middle(p):
+        g_diag(p).wait_recv()
+        rows = pl.ds(pl.multiple_of((d_y if p == 0 else d_x) * 192 + p * PIECE, 16), PIECE)
+        gout[rows] = (gout[rows].astype(f32) + tg[p].astype(f32)).astype(bf)
+        g_summed(p).start()
+
+    for k in range(2):
+        at = k * 384
+        gout[at : at + 384] = lax.dot_general(
+            hg[:, :, :, at : at + 384].reshape(2048, 384),
+            gall[...].reshape(2048, 1536),
+            tn,
+            preferred_element_type=f32,
+        ).astype(bf)
+    for p in range(2):
+        g_diag(p).start()
+    for p in range(2):
+        g_direct(p).start()
+
+    def grad_copy(k):
+        return pltpu.make_async_copy(
+            stage.at[k % 2, pl.ds(0, 3)], gin_hbm.at[k], stage_sem.at[k % 2]
+        )
+
+    for k in range(4):
+        if k < 2:
+            out_copy(k, 0, 0).wait()
+        else:
+            grad_copy(k - 2).wait()
+        stage[k % 2, :3] = (
+            lax.dot_general(
+                xall[:, :, :, k * 384 : (k + 1) * 384].reshape(2048, 384),
+                dgu[...].reshape(2048, 1536),
+                tn,
+                preferred_element_type=f32,
+            )
+            .astype(bf)
+            .reshape(3, 128, 1536)
+        )
+        grad_copy(k).start()
+        if k == 0:
+            mid_sum(1, 1)
+        if k == 1:
+            for p in range(2):
+                g_middle(p)
+        if k == 2:
+            mid_sum(2, 1)
+            last_sum(0)
+
+    for p in range(2):
+        remote(xg.at[p], xg.at[p], g_send.at[1, p], g_recv.at[1, p], to_x).wait_recv()
+        remote(yg.at[p], yg.at[p], g_send.at[1, p], g_recv.at[2, p], to_y).wait_recv()
+        rows = pl.ds(pl.multiple_of(d * 192 + p * PIECE, 16), PIECE)
+        gout_out[p * PIECE : (p + 1) * PIECE] = (
+            gout[rows].astype(f32) + xg[p].astype(f32) + yg[p].astype(f32)
+        ).astype(bf)
+    for k in (2, 3):
+        grad_copy(k).wait()
+    last_sum(1)
+
+    for p in range(2):
+        for copy in (g_diag(p), g_direct(p), g_summed(p)):
+            copy.wait_send()
+    for p in range(4):
+        w_copy(p, d, to_x, 0).wait_send()
+        w_copy(p, d, to_y, 1).wait_send()
+        if p % 2 == 0:
+            w_copy(p, d_x, to_y, 3).wait_send()
+        else:
+            w_copy(p, d_y, to_x, 2).wait_send()
+    for s in range(2):
+        for zp in range(4):
+            for a in range(2):
+                sib_copy(a, zp, s).wait_send()
+                sib_sum(zp, s, a).wait_send()
+
+                @pl.when((zp <= z) & (z < 3))
+                def _():
+                    ag_copy(a, zp, s, 0).wait_send()
+
+                @pl.when((zp >= z) & (z > 0))
+                def _():
+                    ag_copy(a, zp, s, 1).wait_send()
+
+        for i in range(3):
+            for copy in hop(i, s, to_in, True):
+                copy.wait_send()
+
+
+def expert_stage(rows, grads, gates_t, w_in, w_out):
+    bf, f32 = jnp.bfloat16, jnp.float32
+    shape = jax.ShapeDtypeStruct
+    width = rows.shape[-1]
+    hbm = pl.BlockSpec(memory_space=pltpu.HBM)
+    vmem = pl.BlockSpec(memory_space=pltpu.VMEM)
+    dma = pltpu.SemaphoreType.DMA
+    return pl.pallas_call(
+        expert_kernel,
+        out_shape=(
+            shape((CHUNK, width), f32),
+            shape((2, 8, 128), f32),
+            shape((8, 2, 128, width), bf),
+            shape((4, 3, 128, 2 * FF), bf),
+            shape((FF // 4, width), bf),
+        ),
+        in_specs=[hbm] * 5,
+        out_specs=(vmem, vmem, hbm, hbm, vmem),
+        scratch_shapes=[
+            pltpu.VMEM((width, 2 * FF), bf),
+            pltpu.VMEM((FF, width), bf),
+            pltpu.VMEM((8, 2, 128, width), bf),
+            pltpu.VMEM((8, 2, 128, width), bf),
+            pltpu.VMEM((8, 2, 8, 128), f32),
+            pltpu.VMEM((8, 2, 128, 2 * FF), bf),
+            pltpu.VMEM((8, 2, 128, FF), bf),
+            pltpu.VMEM((8, 2, 128, width), bf),
+            pltpu.VMEM((8, 2, 8, 128), f32),
+            pltpu.VMEM((4, 2, 128, width), bf),
+            pltpu.VMEM((4, 2, 8, 128), f32),
+            pltpu.VMEM((3, 2, 128, width), bf),
+            pltpu.VMEM((3, 2, 8, 128), f32),
+            pltpu.VMEM((3, 2, 128, width), bf),
+            pltpu.VMEM((3, 2, 8, 128), f32),
+            pltpu.VMEM((2, 4, 128, width), bf),
+            pltpu.VMEM((FF, width), bf),
+            *([pltpu.VMEM((2, PIECE, width), bf)] * 3),
+            dma((6,)),
+            dma((2,)),
+            dma((3, 2)),
+            dma((3, 2)),
+            dma((4, 4)),
+            dma((4, 4)),
+            dma((2, 4, 2)),
+            dma((2, 2, 4, 2)),
+            dma((2, 4, 2)),
+            dma((2, 4, 2)),
+            dma((6, 4, 2)),
+            dma((4, 4, 2)),
+        ],
+        compiler_params=pltpu.CompilerParams(
+            collective_id=1, has_side_effects=True, vmem_limit_bytes=63 * 2**20
+        ),
+        name="expert_stage",
+    )(
+        rows.reshape(2, 128, width),
+        grads.reshape(8, 2, 128, width),
+        gates_t,
+        w_in,
+        w_out,
+    )
 
 
 def backward_kernel(
@@ -1313,45 +1506,50 @@
     dgt_ref,
     gates_ref,
     mixed_ref,
-    g_ref,
+    cot_ref,
     tok_ref,
     q_ref,
     kv_ref,
     att_ref,
-    cos_ref,
-    sin_ref,
     lens_ref,
-    live_ref,
+    rope_hbm,
     wa_hbm,
     wb_hbm,
     gin_hbm,
-    gout_hbm,
     outp_hbm,
     block_out,
     dtok_out,
-    ga_out,
+    gq_out,
     gb_out,
+    gkv_out,
+    small_out,
     ein_out,
-    eout_out,
     osib,
     oro,
     ori,
     wide,
     small,
-    ga,
+    gq,
     gb,
-    sib_a,
+    gk,
+    sib_q,
     sib_b,
-    ta,
-    xa,
-    ya,
-    roa,
-    ria,
+    sib_k,
+    tq,
+    xq,
+    yq,
+    roq,
+    riq,
     tb,
     xb,
     yb,
     rob,
     rib,
+    tw,
+    xw,
+    yw,
+    row_,
+    riw,
     te,
     xe,
     ye,
@@ -1363,6 +1561,7 @@
     tk,
     xk,
     yk,
+    rope,
     load_sem,
     le_sem,
     old_sem,
@@ -1468,9 +1667,7 @@
         return to_ro, to_ri, wait_ro, wait_ri, drain
 
     def expert_src(dd, p):
-        if p < 4:
-            return gin_hbm.at[pl.ds(pl.multiple_of(dd * 384 + p * PIECE, 16), PIECE)]
-        return gout_hbm.at[pl.ds(pl.multiple_of(dd * 192 + (p - 4) * PIECE, 16), PIECE)]
+        return gin_hbm.at[pl.ds(pl.multiple_of(dd * 384 + p * PIECE, 16), PIECE)]
 
     e_diag, e_direct, e_summed, e_wait_t, e_wait_xy, e_drain = across(0, expert_src, te, xe, ye)
 
@@ -1491,12 +1688,29 @@
         e_wait_xy(p)
         load.wait()
         total = le[1].astype(f32) + xe[p].astype(f32) + ye[p].astype(f32)
-        if p < 4:
-            ein_out[p * PIECE : (p + 1) * PIECE] = total.astype(bf)
-        else:
-            eout_out[(p - 4) * PIECE : (p - 3) * PIECE] = total.astype(bf)
-
-    dense = ((ga, sib_a, ta, xa, ya, roa, ria, ga_out), (gb, sib_b, tb, xb, yb, rob, rib, gb_out))
+        ein_out[p * PIECE : (p + 1) * PIECE] = total.astype(bf)
+
+    def store_q(total):
+        gq_out[...] = total
+
+    def store_b(total):
+        gb_out[...] = total
+
+    def store_k(total):
+        gkv_out[...] = total[:, :512]
+        small_out[...] = lax.dot_general(
+            eye[:16],
+            total[:, 512:],
+            (((1,), (1,)), ((), ())),
+            preferred_element_type=f32,
+            precision=highest,
+        )
+
+    dense = (
+        (gq, sib_q, tq, xq, yq, roq, riq, store_q),
+        (gb, sib_b, tb, xb, yb, rob, rib, store_b),
+        (gk, sib_k, tw, xw, yw, row_, riw, store_k),
+    )
 
     def dense_stream(j):
         grad, sib, t, fx, fy, ro, ri, out = dense[j]
@@ -1565,12 +1779,12 @@
             def _():
                 wait_ro(2)
                 wait_ri(1)
-                out[...] = local(3) + ro[2].astype(f32) + ri[1].astype(f32)
+                out(local(3) + ro[2].astype(f32) + ri[1].astype(f32))
 
             @pl.when(end)
             def _():
                 wait_ri(2)
-                out[...] = local(3) + ri[2].astype(f32)
+                out(local(3) + ri[2].astype(f32))
 
         def drain_all():
             sib_copy().wait_send()
@@ -1579,8 +1793,9 @@
 
         return sib_copy, begin, middle, last, hop, finish, drain_all
 
-    a_sib, a_begin, a_middle, a_last, a_hop, a_finish, a_drain = dense_stream(0)
+    q_sib, q_begin, q_middle, q_last, q_hop, q_finish, q_drain = dense_stream(0)
     b_sib, b_begin, b_middle, b_last, b_hop, b_finish, b_drain = dense_stream(1)
+    w_sib, w_begin, w_middle, w_last, w_hop, w_finish, w_drain = dense_stream(2)
 
     def out_rows(i, lane):
         return outp_hbm.at[pl.ds(pl.multiple_of((2 * order(i) + lane) * CHUNK, CHUNK), CHUNK)]
@@ -1588,7 +1803,7 @@
     def out_sib(i):
         return remote(out_rows(i, other), osib.at[i], os_send.at[i], os_recv.at[i], to_sib)
 
-    o_ro, o_ri, o_wait_ro, o_wait_ri, o_drain = along(2, lambda i: oslot.at[i], oro, ori)
+    o_ro, o_ri, o_wait_ro, o_wait_ri, o_drain = along(3, lambda i: oslot.at[i], oro, ori)
 
     def out_sum(i, incoming, store):
         out_sib(i).wait_recv()
@@ -1633,7 +1848,9 @@
     def out_finish():
         def store(rows, total):
             total = total + mixed_ref[rows]
-            block_out[rows] = jnp.where(live_ref[rows, 0:1] > 0, total, 0.0).astype(bf)
+            slot = d * 128 + lax.broadcasted_iota(jnp.int32, (128, 1), 0)
+            live = slot < lens_ref[rows.start // 128]
+            block_out[rows] = jnp.where(live, total, 0.0).astype(bf)
 
         @pl.when(mid)
         def _():
@@ -1649,7 +1866,7 @@
     def kv_src(dd, i):
         return dkv.at[dd, pl.ds(i * 128, 128)]
 
-    k_diag, k_direct, k_summed, k_wait_t, k_wait_xy, k_drain = across(3, kv_src, tk, xk, yk)
+    k_diag, k_direct, k_summed, k_wait_t, k_wait_xy, k_drain = across(4, kv_src, tk, xk, yk)
 
     def k_middle(i):
         dd = d_y if i % 2 == 0 else d_x
@@ -1661,73 +1878,59 @@
     small_load = pltpu.make_async_copy(wa_hbm.at[:, pl.ds(2048, 128)], small, load_sem.at[0])
     wb_load = pltpu.make_async_copy(wb_hbm, wide.at[:, pl.ds(0, 1536)], load_sem.at[1])
     wa_load = pltpu.make_async_copy(wa_hbm.at[:, pl.ds(0, 2048)], wide, load_sem.at[2])
+    rope_load = pltpu.make_async_copy(
+        rope_hbm.at[:, pl.ds(pl.multiple_of(d * 128, 128), 128)], rope, load_sem.at[3]
+    )
     small_load.start()
+    rope_load.start()
     wb_load.start()
-    for p in range(6):
+    for p in range(4):
         e_diag(p).start()
-    for p in range(6):
+    for p in range(4):
         e_direct(p).start()
     for i in range(4):
         out_sib(i).start()
 
-    ones = lax.broadcasted_iota(jnp.int32, (CHUNK, 128), 1)
+    nt = (((1,), (1,)), ((), ()))
+    tn = (((0,), (0,)), ((), ()))
+
+    def dot_nt(a, b):
+        return lax.dot_general(a, b, nt, preferred_element_type=f32)
+
+    def dot_tn(a, b):
+        return lax.dot_general(a, b, tn, preferred_element_type=f32)
+
     eye = (
         lax.broadcasted_iota(jnp.int32, (128, 128), 0)
         == lax.broadcasted_iota(jnp.int32, (128, 128), 1)
     ).astype(f32)
-    dgate = jnp.concatenate(
-        [
-            lax.dot_general(
-                eye,
-                jnp.concatenate([dgt_ref[s], jnp.zeros((120, 128), f32)], axis=0),
-                (((1,), (1,)), ((), ())),
-                preferred_element_type=f32,
-                precision=highest,
-            )
-            for s in range(2)
-        ],
-        axis=0,
-    )
-    gates = gates_ref[...]
-    dlogit = gates * (dgate - jnp.sum(gates * dgate, axis=1, keepdims=True))
-
-    def halves(v):
-        high = v.astype(bf)
-        return high, (v - high.astype(f32)).astype(bf)
-
-    dl_hi, dl_lo = halves(dlogit)
+    eye_low = eye.astype(bf)
+    gates = jnp.concatenate([gates_ref[s] for s in range(2)], axis=1)
+    dgate = jnp.concatenate([dgt_ref[s] for s in range(2)], axis=1)
+    dlogit = gates * (dgate - jnp.sum(gates * dgate, axis=0, keepdims=True))
+    dl_hi = dlogit.astype(bf).astype(f32)
+    dl = jnp.concatenate([dl_hi, dlogit - dl_hi], axis=0).astype(bf)
     small_load.wait()
-    small_t = lax.dot_general(
-        eye.astype(bf), small[...], (((1,), (1,)), ((), ())), preferred_element_type=f32
-    )
-    nt = (((1,), (1,)), ((), ()))
-    tn = (((0,), (0,)), ((), ()))
-
-    def dot_nt(a, b):
-        return lax.dot_general(a, b, nt, preferred_element_type=f32)
-
-    def dot_tn(a, b):
-        return lax.dot_general(a, b, tn, preferred_element_type=f32)
-
-    dn2 = dx_ref[...] + dot_nt(dl_hi, small[...]) + dot_nt(dl_lo, small[...])
+    small_t = dot_nt(eye_low[:16], small[...])
+    router = jnp.concatenate([small_t[:8]] * 2, axis=0).astype(bf)
+    dn2 = dx_ref[...] + dot_tn(dl, router)
     mixed = mixed_ref[...]
     inv2 = lax.rsqrt(jnp.mean(mixed * mixed, axis=1, keepdims=True) + epsilon)
     n2 = mixed * inv2
     normed2 = (n2 * small_t[9:10]).astype(bf)
-    mid_hi, mid_lo = halves(dn2 * n2)
-    col9 = (ones == 9).astype(bf)
-    for r in range(4):
-        cols = slice(r * 384, (r + 1) * 384)
-        part = (
-            dot_tn(normed2[:, cols], dl_hi)
-            + dot_tn(normed2[:, cols], dl_lo)
-            + dot_tn(mid_hi[:, cols], col9)
-            + dot_tn(mid_lo[:, cols], col9)
-        )
-        dsm = part.reshape(4, 2, 48, 128)
-        ga[4 * r : 4 * r + 4, :, :, 2048:] = dsm.astype(bf)
+    router_sum = jnp.dot(dl, normed2, preferred_element_type=f32)
+    router_sum = router_sum[:8] + router_sum[8:]
+    mid_sum = jnp.sum(dn2 * n2, axis=0, keepdims=True)
+    grads = [
+        jnp.where(
+            d * 128 + lax.broadcasted_iota(jnp.int32, (128, 1), 0) < lens_ref[s],
+            cot_ref[s * 128 : (s + 1) * 128].astype(f32),
+            0.0,
+        )
+        for s in range(2)
+    ]
     u = dn2 * small_t[9:10]
-    dmixed = g_ref[...].astype(f32) + inv2 * (u - n2 * jnp.mean(u * n2, axis=1, keepdims=True))
+    dmixed = jnp.concatenate(grads, axis=0) + inv2 * (u - n2 * jnp.mean(u * n2, axis=1, keepdims=True))
     dmix[...] = dmixed
     dproj = dmixed.astype(bf)
     for r in range(4):
@@ -1743,14 +1946,13 @@
     wa_load.start()
     e_middle(0)
     e_middle(1)
-    b_begin()
-    for i in range(3):
-        out_end(i)
+    out_end(0)
 
     query_pos = d * 128 + lax.broadcasted_iota(jnp.int32, (128, 512), 0)
     key_pos = lax.broadcasted_iota(jnp.int32, (128, 512), 1)
-    cos_rows = cos_ref[...]
-    sin_rows = sin_ref[...]
+    rope_load.wait()
+    cos_rows = rope[0]
+    sin_rows = rope[1]
     scale = HEAD_SIZE ** (-0.5)
 
     def unrotate_rows(v, cos, sin):
@@ -1763,7 +1965,7 @@
         srow = pl.ds(pl.multiple_of(s * 128, 128), 128)
         kcol = pl.ds(pl.multiple_of(h * 128, 128), 128)
         vcol = pl.ds(pl.multiple_of(256 + h * 128, 128), 128)
-        lens = lens_ref[s][0:1, 0:1]
+        lens = lens_ref[s]
         allowed = (key_pos <= query_pos) & (key_pos < lens)
         ks = kv_ref[:, srow, kcol].reshape(512, 128)
         vs = kv_ref[:, srow, vcol].reshape(512, 128)
@@ -1797,8 +1999,6 @@
         k_diag(i).start()
     for i in range(2):
         k_direct(i).start()
-    e_middle(2)
-    e_middle(3)
 
     tok = tok_ref[...].astype(f32)
     inv1 = lax.rsqrt(jnp.mean(tok * tok, axis=1, keepdims=True) + epsilon)
@@ -1806,16 +2006,18 @@
     normed = (n1 * small_t[8:9]).astype(bf)
     for r in range(4):
         part = dot_tn(normed[:, r * 384 : (r + 1) * 384], dqs[...])
-        ga[4 * r : 4 * r + 4, :, :, :1536] = part.astype(bf).reshape(4, 2, 48, 1536)
-    wa_load.wait()
+        gq[4 * r : 4 * r + 4] = part.astype(bf).reshape(4, 2, 48, 1536)
+    q_sib().start()
     k_middle(0)
     k_middle(1)
+    b_begin()
+    e_middle(2)
+    e_middle(3)
+    wa_load.wait()
     dn1 = dot_nt(dqs[...], wide[:, :1536])
-    e_middle(4)
-    e_middle(5)
-    out_mid(0)
-    for i in range(4):
-        b_middle(i)
+    out_end(1)
+    out_end(2)
+    q_begin()
 
     for i in range(2):
         k_wait_xy(i)
@@ -1837,111 +2039,133 @@
         axis=1,
     ).astype(bf)
     dn1 = dn1 + dot_nt(dkv_own, wide[:, 1536:])
-    pre_hi, pre_lo = halves(dn1 * n1)
-    col8 = (ones == 8).astype(bf)
+    pre_sum = jnp.sum(dn1 * n1, axis=0, keepdims=True)
+    row8 = lax.broadcasted_iota(jnp.int32, (8, 1536), 0)
+    gains = jnp.where(row8 == 0, pre_sum, jnp.where(row8 == 1, mid_sum, 0.0))
+    smalls = jnp.concatenate([router_sum, gains], axis=0).astype(bf)
     for r in range(4):
         cols = slice(r * 384, (r + 1) * 384)
         part = dot_tn(normed[:, cols], dkv_own)
-        ga[4 * r : 4 * r + 4, :, :, 1536:2048] = part.astype(bf).reshape(4, 2, 48, 512)
-        part = dot_tn(pre_hi[:, cols], col8) + dot_tn(pre_lo[:, cols], col8)
-        ga[4 * r : 4 * r + 4, :, :, 2048:] = (
-            ga[4 * r : 4 * r + 4, :, :, 2048:].astype(f32) + part.reshape(4, 2, 48, 128)
-        ).astype(bf)
-    a_sib().start()
+        gk[4 * r : 4 * r + 4, :, :, :512] = part.astype(bf).reshape(4, 2, 48, 512)
+        part = dot_tn(smalls[:, cols], eye_low[:16])
+        gk[4 * r : 4 * r + 4, :, :, 512:] = part.astype(bf).reshape(4, 2, 48, 128)
+    w_sib().start()
     u = dn1 * small_t[8:9]
     dtok_out[...] = dmix[...] + inv1 * (u - n1 * jnp.mean(u * n1, axis=1, keepdims=True))
 
-    a_begin()
+    for i in range(4):
+        b_middle(i)
+    w_begin()
+    out_mid(0)
+    for i in range(4):
+        q_middle(i)
+    for p in range(4):
+        e_final(p)
+    out_mid(1)
+    out_mid(2)
+    for i in range(4):
+        w_middle(i)
     for i in range(4):
         b_last(i)
-    out_mid(1)
-    out_mid(2)
-    for i in range(3):
-        b_hop(i)
-    for p in range(6):
-        e_final(p)
+        if i < 3:
+            b_hop(i)
     for i in range(4):
-        a_middle(i)
+        q_last(i)
+        if i < 3:
+            q_hop(i)
     out_finish()
+    for i in range(4):
+        w_last(i)
+        if i < 3:
+            w_hop(i)
     b_finish()
-    for i in range(4):
-        a_last(i)
-        if i < 3:
-            a_hop(i)
-    a_finish()
-
-    e_drain(6)
+    q_finish()
+    w_finish()
+
+    e_drain(4)
     k_drain(2)
-    a_drain()
+    q_drain()
     b_drain()
+    w_drain()
     o_drain()
     for i in range(4):
         out_sib(i).wait_send()
 
 
-def backward_stage(dx, dgt, gates, mixed, g, tok, q, kv, att, cos, sin, lens, live, wa, wb, gin, gout, outp):
+def backward_stage(dx, dgt, gates, mixed, cot, tok, q, kv, att, lens, rope, wa, wb, gin, outp):
     bf, f32 = jnp.bfloat16, jnp.float32
     shape = jax.ShapeDtypeStruct
     width = tok.shape[-1]
-    wide = wa.shape[-1]
     hbm = pl.BlockSpec(memory_space=pltpu.HBM)
     vmem = pl.BlockSpec(memory_space=pltpu.VMEM)
+    smem = pl.BlockSpec(memory_space=pltpu.SMEM)
     dma = pltpu.SemaphoreType.DMA
+    widths = (width, width, 640)
     dense = []
-    for w in (wide, width):
+    for w in widths:
         dense += [pltpu.VMEM((4, 48, w), bf)] * 3 + [pltpu.VMEM((3, 48, w), bf)] * 2
     return pl.pallas_call(
         backward_kernel,
         out_shape=(
             shape((CHUNK, width), bf),
             shape((CHUNK, width), f32),
-            shape((48, wide), f32),
             shape((48, width), f32),
+            shape((48, width), f32),
+            shape((48, 512), f32),
+            shape((16, 48), f32),
             shape((384, 2 * FF), bf),
-            shape((192, width), bf),
             shape((4, CHUNK, width), bf),
             shape((3, CHUNK, width), bf),
             shape((3, CHUNK, width), bf),
         ),
-        in_specs=[vmem] * 13 + [hbm] * 5,
-        out_specs=[vmem] * 6 + [hbm] * 3,
+        in_specs=[vmem] * 9 + [smem] + [hbm] * 5,
+        out_specs=[vmem] * 7 + [hbm] * 3,
         scratch_shapes=[
             pltpu.VMEM((width, 2048), bf),
             pltpu.VMEM((width, 128), bf),
-            pltpu.VMEM((16, 2, 48, wide), bf),
-            pltpu.VMEM((16, 2, 48, width), bf),
-            pltpu.VMEM((16, 48, wide), bf),
-            pltpu.VMEM((16, 48, width), bf),
+            *[pltpu.VMEM((16, 2, 48, w), bf) for w in widths],
+            *[pltpu.VMEM((16, 48, w), bf) for w in widths],
             *dense,
-            *([pltpu.VMEM((6, PIECE, width), bf)] * 3),
+            *([pltpu.VMEM((4, PIECE, width), bf)] * 3),
             pltpu.VMEM((2, PIECE, width), bf),
             pltpu.VMEM((4, 128, width), bf),
             pltpu.VMEM((3, CHUNK, width), bf),
             pltpu.VMEM((2 * QUERY_HEADS * 128, 128), bf),
             pltpu.VMEM((4, CHUNK, 512), bf),
             *([pltpu.VMEM((2, 128, 512), bf)] * 3),
-            dma((3,)),
+            pltpu.VMEM((2, 128, 128), f32),
+            dma((4,)),
             dma((2,)),
             dma((4,)),
             dma((4,)),
             dma((4,)),
-            dma((2,)),
-            dma((2,)),
-            dma((4, 6)),
-            dma((4, 6)),
-            dma((4, 6)),
-            dma((4, 6)),
-            dma((4, 6)),
-            dma((4, 6)),
-            dma((3, 3)),
-            dma((3, 3)),
-            dma((3, 3)),
+            dma((3,)),
+            dma((3,)),
+            dma((5, 4)),
+            dma((5, 4)),
+            dma((5, 4)),
+            dma((5, 4)),
+            dma((5, 4)),
+            dma((5, 4)),
+            dma((4, 3)),
+            dma((4, 3)),
+            dma((4, 3)),
         ],
         compiler_params=pltpu.CompilerParams(
             collective_id=3, has_side_effects=True, vmem_limit_bytes=64 * 2**20 - 65536
         ),
         name="backward_stage",
-    )(dx, dgt, gates, mixed, g, tok, q, kv, att, cos, sin, lens, live, wa, wb, gin, gout, outp)
+    )(dx, dgt, gates, mixed, cot, tok, q, kv, att, lens, rope, wa, wb, gin, outp)
+
+
+def rope_constant(slots):
+    half = HEAD_SIZE // 2
+    inv_freq = np.float32(rope_base) ** (-(np.arange(half, dtype=np.float32) * 2.0 / HEAD_SIZE))
+    angles = np.arange(slots, dtype=np.float32)[:, None] * inv_freq[None, :].astype(np.float32)
+    cos, sin = np.cos(angles), np.sin(angles)
+    return np.stack(
+        [np.concatenate([cos, cos], axis=1), np.concatenate([-sin, sin], axis=1)]
+    ).astype(np.float32)
 
 
 def fast_local(
@@ -1958,43 +2182,40 @@
     expert_out,
     cotangent,
 ):
-    bf, f32 = jnp.bfloat16, jnp.float32
+    f32 = jnp.float32
     seqs, token_rows, width = tokens.shape
-    dp_rank = lax.axis_index("dp")
     rows = seqs * token_rows
-    small = jnp.concatenate(
-        [w_router, prenorm[:, None], midnorm[:, None], jnp.zeros((w_router.shape[0], 118), bf)], axis=1
+    tok = tokens.reshape(rows, width)
+    cot = cotangent.reshape(rows, width)
+    rope = jnp.asarray(rope_constant(token_rows * lax.axis_size("dp")))
+    full_a, full_b, full_out, gall, q_rot, kv_all, attended, mixed, normed2, gates = attention_stage(
+        tok,
+        w_query,
+        key_value_weight,
+        w_router.T,
+        prenorm[None],
+        midnorm[None],
+        w_output,
+        cot,
+        expert_out[0],
+        rope,
+        lengths,
+        jnp.transpose(routes, (0, 2, 1)),
     )
-    shard_a = jnp.concatenate([w_query, key_value_weight, small], axis=1)
-    positions = dp_rank * token_rows + jnp.arange(token_rows, dtype=jnp.int32)
-    cosine_table, sine_table = rope_tables(positions)
-    cos_rows = jnp.concatenate([cosine_table, cosine_table], axis=1)
-    sin_rows = jnp.concatenate([-sine_table, sine_table], axis=1)
-    live = (positions[None, :] < lengths[:, None]).reshape(rows, 1)
-    x = tokens.reshape(rows, width)
-    g = jnp.where(live, cotangent.reshape(rows, width), 0)
-    lens = jnp.broadcast_to(lengths[:, None, None], (seqs, 8, 128))
-    full_a, full_b, gall, q_rot, kv_all, attended, mixed, normed2, gates = attention_stage(
-        x, shard_a, w_output, g, cos_rows, sin_rows, lens, routes.reshape(rows, TOP)
-    )
-    gates_t = jnp.transpose(gates[:, :8].reshape(seqs, token_rows, 8), (0, 2, 1))
-    dx, dgate_t, outp, gin, gout = expert_stage(
-        normed2, gall, gates_t, expert_in[0], expert_out[0]
-    )
-    live_f = jnp.broadcast_to(live.astype(f32), (rows, 128))
-    block_out, grad_tokens, g_a, g_b, g_in, g_out = backward_stage(
-        dx, dgate_t, gates, mixed, g, x, q_rot, kv_all, attended, cos_rows, sin_rows, lens, live_f,
-        full_a, full_b, gin, gout, outp,
-    )[:6]
+    dx, dgate, outp, gin, g_out = expert_stage(normed2, gall, gates, expert_in[0], full_out)
+    block_out, grad_tokens, g_query, g_b, g_kv, small, g_in = backward_stage(
+        dx, dgate, gates, mixed, cot, tok, q_rot, kv_all, attended, lengths, rope,
+        full_a, full_b, gin.reshape(width, 2 * FF), outp.reshape(8 * rows, width),
+    )[:7]
     return (
         block_out.reshape(seqs, token_rows, width),
         grad_tokens.reshape(seqs, token_rows, width),
-        g_a[:, 2056],
-        g_a[:, :1536],
-        g_a[:, 1536:2048],
+        small[8],
+        g_query,
+        g_kv,
         g_b,
-        g_a[:, 2057],
-        g_a[:, 2048:2056],
+        small[9],
+        small[:8].T,
         g_in.astype(f32)[None],
         g_out.astype(f32)[None],
     )

time: 403 us -> 346 us (0.86)
  Pallas kernels: 369 us -> 328 us
  local copies, waits for them, and re-layouts: 18 us -> 6.68 us
  other arithmetic: 8.6 us -> 3.97 us
    pallas_call x1, Pallas kernels: 140 us -> 121 us  [backward_stage(): pl.pallas_call(backward_kernel, out_shape=(shape((CHUNK, width), bf), sha...]
    pallas_call x1, Pallas kernels: 133 us -> 116 us  [expert_stage(): pl.pallas_call(expert_kernel, out_shape=(shape((CHUNK, width), f32), shap...]
    slice x5 -> x0, local copies, waits for them, and re-layouts: 7.1 us -> none  [the longest x1 1.69 us: fast_local(): g_a[:, :1536]]
    pallas_call x1, Pallas kernels: 96.1 us -> 91 us  [attention_stage(): pl.pallas_call(attention_kernel, out_shape=(shape((width, wide), bf), sha...]
where the time goes in v4:
time: 346 us; the launch traced here: 339 us
  Pallas kernels  328 us (95%)
  local copies, waits for them, and re-layouts  6.68 us (2%)
  other arithmetic  3.97 us (1%)
    pallas_call x1, Pallas kernels, backward_stage(): pl.pallas_call(backward_kernel, out_shape=(shape((CHUNK, width), bf), sha...  121 us
    pallas_call x1, Pallas kernels, expert_stage(): pl.pallas_call(expert_kernel, out_shape=(shape((CHUNK, width), f32), shap...  116 us
    pallas_call x1, Pallas kernels, attention_stage(): pl.pallas_call(attention_kernel, out_shape=(shape((width, wide), bf), sha...  91 us

profile of v4, /device:TPU:0, one launch (start us, length us, event | category | flops | bytes accessed | tf_op | source)
XLA Modules:
  0.0 339.2 jit_solution(1423334267516920054)
XLA Ops:
  0.6 91.0 %attention_stage.1 = (bf16[1536,2176]{1,0:T(8,128)(2,1)}, bf16[1536,1536]{1,0:T(8,128)(2,1)}, bf16[768,1536]{1,0:T(8,128)(2,1)}, bf16[2048,1536]{1,0:T(8,128)(2,...) custom-call(bf16[256,1536]{1,0:T(8,128)(2,1)} %bitcast.29, ...), custom_call_target="tpu_custom_call" | custom-call | tf_op jit(solution)/shard_map/attention_stage/pallas_call | solution.py:917
  91.6 115.6 %expert_stage.1 = (f32[256,1536]{1,0:T(8,128)}, f32[2,8,128]{2,1,0:T(8,128)}, bf16[8,2,128,1536]{3,2,1,0:T(8,128)(2,1)}, bf16[4,3,128,1536]{3,2,1,0:T(8,128)(2,1)}, bf16[192,1536]{1,0:T(8,128)(2,1)}) custom-call(bf16[2,128,1536]{2,1,0:T(8,128)(2,1)} %bitcast.35, bf16[8,2,128,1536]{3,2,1,0:T(8,128)(2,1)} %bitcast.26, ...), custom_call_target="tpu_custom_call" | custom-call | tf_op jit(solution)/shard_map/expert_stage/pallas_call | solution.py:1448
  207.2 121.1 %backward_stage.1 = (bf16[256,1536]{1,0:T(8,128)(2,1)}, f32[256,1536]{1,0:T(8,128)}, f32[48,1536]{1,0:T(8,128)}, f32[48,1536]{1,0:T(8,128)}, f32[48,512]{1,0:T(8...) custom-call(f32[256,1536]{1,0:T(8,128)} %get-tuple-element.36.dx_ref, ...), custom_call_target="tpu_custom_call" | custom-call | tf_op jit(solution)/shard_map/backward_stage/pallas_call | solution.py:2107
  328.3 0.0 copy-start.1
  328.3 1.3 slice_bitcast_fusion.1
  329.6 1.3 slice_bitcast_fusion
  330.9 0.0 copy-start.2
  330.9 2.3 bitcast_convert_fusion.1
  333.2 0.0 copy-done.1
  333.2 0.0 copy-start
  333.2 1.7 bitcast_convert_fusion
  334.9 0.0 copy-done.2
  334.9 0.0 copy-start.4
  334.9 0.0 copy-start.5
  334.9 0.9 copy.28
  335.8 0.0 copy-done
  335.8 0.0 copy-start.3
  335.8 1.1 copy.29
  336.9 0.0 copy-done.4
  336.9 0.7 copy.30
  337.6 0.0 copy-done.5
  337.6 0.6 copy.31
  338.3 0.0 copy-done.3
  338.3 0.7 copy.32
Async XLA Ops:
  328.3 4.9 %copy-start.1 = (bf16[384,1536]{1,0:T(8,128)(2,1)S(1)}, bf16[384,1536]{1,0:T(8,128)(2,1)}, u32[]{:S(2)}) copy-start(bf16[384,1536]{1,0:T(8,128)(2,1)} %get-tuple-element.52) | copy-start | bytes 3538948
  330.9 4.0 %copy-start.2 = (bf16[256,1536]{1,0:T(8,128)(2,1)S(1)}, bf16[256,1536]{1,0:T(8,128)(2,1)}, u32[]{:S(2)}) copy-start(bf16[256,1536]{1,0:T(8,128)(2,1)} %get-tuple-element.46) | copy-start | bytes 2359300
  333.2 2.6 copy-start
  334.9 2.0 copy-start.4
  334.9 2.7 copy-start.5
  335.8 2.5 copy-start.3
